TPU v7x, 32 devices: a whole 2x2x4 slice. The times are simulated.
32 devices in a mesh: gx: 2 (over y), gy: 4 (over x, core), gz: 4 (over z).
Axes of the slice: x: 2, y: 2, z: 4, core: 2. Of those that a mesh axis runs over, the one named last changes fastest.
Arguments:
- right_side: float32 [2, 4, 4, 64, 512], P('gx', 'gy', 'gz'), may hold values from -6 to 6
- diag_blocks: float32 [4, 64, 64], replicated, may hold values from -0.27 to 17.9, as said below
- face_blocks: float32 [6, 4, 64, 64], replicated, may hold values from -2.42 to 0.22
- prolong: float32 [8, 64, 64], replicated, may hold values from -0.75 to 0.75
- mats_fine: int32 [2, 4, 4, 512], P('gx', 'gy', 'gz'), may hold values from 0 to 3
- mats_mid: int32 [2, 4, 4, 64], P('gx', 'gy', 'gz'), may hold values from 0 to 3
- mats_coarse: int32 [2, 4, 4, 8], P('gx', 'gy', 'gz'), may hold values from 0 to 3
Outputs:
- solution: float32 [2, 4, 4, 64, 512], P('gx', 'gy', 'gz')
Inputs may be any that keep to these rules, and one draw needn't show every extreme that they name: `diag_blocks`: each block is symmetric positive definite.
All inputs are finite; a program needn't handle non-finite values.
Results may differ from a plain program's by a relative error of at most 0.0003.
Values sent between devices are 32-bit elements; how exact they have to be, the bound alone decides.
No kernel may reach another device: no remote copies, remote signals or barrier semaphores. Data moves between devices by JAX's collectives and lax.ppermute only.
A program may use at most 64 MiB of HBM per device.

v0:
```python
from functools import partial

import jax
import jax.numpy as jnp
from jax import lax
from jax.experimental import pallas as pl
from jax.experimental.pallas import tpu as pltpu
from jax.sharding import PartitionSpec as P

MODES = 64
MATERIALS = 4
SWEEPS = 2
COARSE_SWEEPS = 4
CYCLES = 2
CX = 8
CY = 8
CZ = 8


relax_weight = 0.7
restrict_scale = 0.6
highest = lax.Precision.HIGHEST


def padded_2(shard, sides, width):
    for axis, dim in sides:
        size, length = (lax.axis_size(axis), shard.shape[dim])
        up = [(i, (i + 1) % size) for i in range(size - 1)]
        down = [(j, i) for i, j in up]
        last = lax.slice_in_dim(shard, length - width, length, axis=dim)
        first = lax.slice_in_dim(shard, 0, width, axis=dim)
        before = lax.ppermute(last, axis, up)
        after = lax.ppermute(first, axis, down)
        shard = jnp.concatenate([before, shard, after], axis=dim)
    return shard


def inverse_blocks(diag_blocks):
    identity = jnp.eye(MODES, dtype=diag_blocks.dtype)
    result = []
    for material in range(MATERIALS):
        factor = jnp.linalg.cholesky(diag_blocks[material])
        result.append(jax.scipy.linalg.cho_solve((factor, True), identity))
    return jnp.stack(result).reshape(MATERIALS * MODES, MODES)


def coupling_matrix(diag_blocks, face_blocks):
    blocks = jnp.concatenate([diag_blocks[None], face_blocks], axis=0)
    return jnp.transpose(blocks, (1, 2, 0, 3)).reshape(MATERIALS * MODES, 7 * MODES)


def choose_blocks(weights, columns, onehot):
    product = jnp.dot(weights, columns, precision=highest, preferred_element_type=jnp.float32)
    product = product.reshape(MATERIALS, MODES, columns.shape[1])
    return jnp.sum(product * onehot.reshape(MATERIALS, 1, columns.shape[1]), axis=0)


def operate(padded, onehot, coupling):
    centre = padded[:, 1:-1, 1:-1, 1:-1]
    stacked = jnp.concatenate(
        [
            centre,
            padded[:, 2:, 1:-1, 1:-1],
            padded[:, :-2, 1:-1, 1:-1],
            padded[:, 1:-1, 2:, 1:-1],
            padded[:, 1:-1, :-2, 1:-1],
            padded[:, 1:-1, 1:-1, 2:],
            padded[:, 1:-1, 1:-1, :-2],
        ],
        axis=0,
    )
    columns = stacked.reshape(7 * MODES, -1)
    return choose_blocks(coupling, columns, onehot.reshape(MATERIALS, -1)).reshape(centre.shape)


def apply_inverse(inverse, field, onehot):
    return choose_blocks(inverse, field.reshape(MODES, -1), onehot.reshape(MATERIALS, -1)).reshape(
        field.shape
    )


def restrict(field, prolong):
    blocked = field.reshape(
        MODES, field.shape[1] // 2, 2, field.shape[2] // 2, 2, field.shape[3] // 2, 2
    )
    return restrict_scale * jnp.einsum(
        "abcji,jxaybzc->ixyz", prolong.reshape(2, 2, 2, MODES, MODES), blocked, precision=highest
    )


def expand(coarse_field, prolong):
    finer = jnp.einsum(
        "abcji,ixyz->jxaybzc",
        prolong.reshape(2, 2, 2, MODES, MODES),
        coarse_field,
        precision=highest,
    )
    return finer.reshape(
        MODES, 2 * coarse_field.shape[1], 2 * coarse_field.shape[2], 2 * coarse_field.shape[3]
    )


def make_onehot(materials):
    return (materials[None] == jnp.arange(MATERIALS, dtype=jnp.int32)[:, None, None, None]).astype(
        jnp.float32
    )


def fine_border(field):
    return padded_2(field, (("gx", 1), ("gy", 2), ("gz", 3)), 1)


def section_border(field):
    padded = padded_2(field, (("gx", 1), ("gy", 2)), 1)
    return jnp.pad(padded, ((0, 0), (0, 0), (0, 0), (1, 1)))


def smooth(iterate, source, onehot, border, inverse, coupling):
    residual = source - operate(border(iterate), onehot, coupling)
    return iterate + relax_weight * apply_inverse(inverse, residual, onehot)


def coarse_solve(source, onehot, border, inverse, coupling):
    iterate = relax_weight * apply_inverse(inverse, source, onehot)
    for repeat in range(COARSE_SWEEPS - 1):
        iterate = smooth(iterate, source, onehot, border, inverse, coupling)
    return iterate


def middle_cycle(source, onehot, border, inverse, coupling, prolong, coarse_solver):
    iterate = relax_weight * apply_inverse(inverse, source, onehot)
    iterate = smooth(iterate, source, onehot, border, inverse, coupling)
    residual = source - operate(border(iterate), onehot, coupling)
    iterate = iterate + expand(coarse_solver(restrict(residual, prolong)), prolong)
    for repeat in range(SWEEPS):
        iterate = smooth(iterate, source, onehot, border, inverse, coupling)
    return iterate


def single_steps(iterate, actions, source, onehot, inverse, coupling):
    residual = None
    for action in actions:
        if action == "sweep":
            iterate = smooth(iterate, source, onehot, fine_border, inverse, coupling)
        else:
            residual = source - operate(fine_border(iterate), onehot, coupling)
    return (iterate, residual)


def per_device(right_side, diag_blocks, face_blocks, prolong, mats_fine, mats_mid, mats_coarse):
    inverse = inverse_blocks(diag_blocks)
    coupling = coupling_matrix(diag_blocks, face_blocks)
    source = right_side[0, 0, 0].reshape(MODES, CX, CY, CZ)
    onehot_fine = make_onehot(mats_fine[0, 0, 0].reshape(CX, CY, CZ))
    onehot_mid = make_onehot(mats_mid[0, 0, 0].reshape(CX // 2, CY // 2, CZ // 2))
    onehot_coarse = make_onehot(mats_coarse[0, 0, 0].reshape(CX // 4, CY // 4, CZ // 4))
    stepper = partial(
        single_steps, source=source, onehot=onehot_fine, inverse=inverse, coupling=coupling
    )
    iterate = relax_weight * apply_inverse(inverse, source, onehot_fine)
    for cycle_index in range(CYCLES):
        if cycle_index == 0:
            actions = ["sweep"] * (SWEEPS - 1) + ["residual"]
        else:
            actions = ["sweep"] * SWEEPS + ["residual"]
        iterate, residual = stepper(iterate, actions)
        gathered_source = lax.all_gather(restrict(residual, prolong), "gz", axis=3, tiled=True)
        gathered_mid = lax.all_gather(onehot_mid, "gz", axis=3, tiled=True)
        gathered_coarse = lax.all_gather(onehot_coarse, "gz", axis=3, tiled=True)
        local_solver = partial(
            coarse_solve,
            onehot=gathered_coarse,
            border=section_border,
            inverse=inverse,
            coupling=coupling,
        )
        section_field = middle_cycle(
            gathered_source, gathered_mid, section_border, inverse, coupling, prolong, local_solver
        )
        iterate = iterate + expand(
            lax.dynamic_slice_in_dim(section_field, lax.axis_index("gz") * (CZ // 2), CZ // 2, 3),
            prolong,
        )
        iterate, unused_residual = stepper(iterate, ["sweep"] * SWEEPS)
    return iterate.reshape(MODES, CX * CY * CZ)[None, None, None]


HALO = 3 * SWEEPS + SWEEPS - 1
PITCH = CY + 2 * HALO
BLOCK = CX * CY * CZ
TILE = 128
LANES = -(-(PITCH * PITCH) // TILE) * TILE
ROWS = MODES + 8
MX, MY, MZ = CX // 2, CY // 2, CZ // 2
f32 = jnp.float32
bf16 = jnp.bfloat16


def split(value):
    high = value.astype(bf16)
    return high, (value - high.astype(f32)).astype(bf16)


def dot(a, b):
    return jnp.dot(a, b, preferred_element_type=f32)


def iota(shape, dim):
    return lax.broadcasted_iota(jnp.int32, shape, dim)


def where_equal(rows, columns):
    return jnp.where(rows == columns, 1.0, 0.0).astype(bf16)


def place(value, selector):
    high, low = split(value)
    return dot(high, selector) + dot(low, selector)


def pick(product, code, first):
    out = jnp.zeros((MODES, product.shape[1]), f32)
    for m in range(MATERIALS):
        out = jnp.where(code == m + first, product[m * MODES:(m + 1) * MODES], out)
    return out


def stack3(value):
    high, low = split(value)
    return jnp.concatenate([high, low, high], axis=0)


def thirds(value):
    high, low = split(value)
    return jnp.concatenate([high, high, low], axis=1)


def inverse_kernel(diag, scaled):
    a = diag[...]
    row_id = iota((1, MODES, 1), 1)
    lane_id = iota((1, 1, MODES), 2)
    for k in range(MODES):
        pivot = 1.0 / a[:, k:k + 1, k:k + 1]
        on_row, on_lane = row_id == k, lane_id == k
        row = jnp.where(on_lane, pivot, a[:, k:k + 1, :] * pivot)
        column = a[:, :, k:k + 1]
        a = jnp.where(on_row, row, jnp.where(on_lane, 0.0, a) - column * row)
    scaled[...] = relax_weight * a


def weights_kernel(scaled, diag, face, prolong, wg, wa, wd, wi, wr, wp):
    beside, gains = [], []
    for m in range(MATERIALS):
        faces = jnp.concatenate([face[d, m] for d in (1, 0, 2, 3, 4, 5)], axis=1)
        beside.append(faces)
        gains.append(jnp.dot(scaled[m], faces, precision=highest, preferred_element_type=f32))
    for target, blocks in ((wa, beside), (wg, gains)):
        high, low = split(jnp.concatenate(blocks, axis=0))
        target[...] = jnp.concatenate([high, low, high], axis=1)
    wd[...] = thirds(jnp.concatenate([diag[m] for m in range(MATERIALS)], axis=0))
    wi[...] = thirds(jnp.concatenate([scaled[m] for m in range(MATERIALS)], axis=0))
    for p in range(2):
        wr[p] = thirds(jnp.concatenate([restrict_scale * prolong[p * 4 + c].T for c in range(4)], axis=0))
    wp[...] = thirds(jnp.concatenate([prolong[c] for c in range(8)], axis=0))


def invert(diag_blocks):
    return call(inverse_kernel, 6, shape_of(*diag_blocks.shape), [], diag_blocks)


def make_weights(scaled, diag_blocks, face_blocks, prolong):
    rows = MATERIALS * MODES
    shapes = [(rows, 18 * MODES)] * 2 + [(rows, 3 * MODES)] * 2
    shapes += [(2, 4 * MODES, 3 * MODES), (8 * MODES, 3 * MODES)]
    shapes = [jax.ShapeDtypeStruct(shape, bf16) for shape in shapes]
    return call(weights_kernel, 1, shapes, [], scaled, diag_blocks, face_blocks, prolong)


SHALLOW = SWEEPS
PAIRS = CX
SLOT = CY * CZ


def layer_rows(depth, halo):
    return CY + 2 * (halo - depth)


SHALLOW_LANES = sum(layer_rows(d, SHALLOW) for d in range(1, SHALLOW + 1))
DEEP_LANES = sum(layer_rows(d, HALO) for d in range(1, HALO + 1))
PER_TILE = TILE // (2 * SHALLOW_LANES)
SHALLOW_TILES = -(-PAIRS // PER_TILE)


def layer_of(index, first, last, halo):
    depth, start, at = jnp.full_like(index, first), jnp.zeros_like(index), 0
    for d in range(first + 1, last + 1):
        at += layer_rows(d - 1, halo)
        inside = index >= at
        depth, start = jnp.where(inside, d, depth), jnp.where(inside, at, start)
    return depth, index - start - (halo - depth)


def lane_of(depth, y, first, last, halo):
    start, at = jnp.zeros_like(depth), 0
    for d in range(first + 1, last + 1):
        at += layer_rows(d - 1, halo)
        start = jnp.where(depth == d, at, start)
    inside = (depth >= first) & (depth <= last) & (y >= depth - halo) & (y < CY + halo - depth)
    return jnp.where(inside, start + y + halo - depth, -(1 << 20))


def prepare_kernel(place_ref, values, other, materials, other_materials, out):
    mine = place_ref[0]
    for half, (block, kinds) in enumerate(((values, materials), (other, other_materials))):
        first = (mine ^ half) * (BLOCK // TILE)
        codes = jnp.broadcast_to((kinds[...] + 1).astype(f32), (ROWS - MODES, BLOCK))
        for tile in range(BLOCK // TILE):
            lanes = slice(tile * TILE, (tile + 1) * TILE)
            out[first + tile, :MODES] = block[:, lanes]
            out[first + tile, MODES:] = codes[:, lanes]


def swap_tile(y, odd):
    place = (y + CY) // CY
    return jnp.where(place == 1, 1, jnp.where(place // 2 == odd, 2, 0))


def pack_kernel(place_ref, own, first, second, thin_first, thin_second, thick_first, thick_second):
    column = iota((1, 4 * TILE), 1)
    lane, kind = column % TILE, column // TILE
    row = iota((3 * TILE, 4 * TILE), 0)
    odd_y, odd_z = place_ref[1] & 1, place_ref[2] & 1
    parts = [jnp.concatenate([r[pair] for r in (first, own, second)], axis=1) for pair in range(PAIRS)]
    parts = split(jnp.concatenate(parts, axis=0))
    shallow = 0.0
    for odd in range(2):
        thin = lane - odd * SHALLOW_LANES
        thin_depth, thin_y = layer_of(thin, 1, SHALLOW, SHALLOW)
        thick_depth, thick_y = layer_of(lane, 1, HALO, HALO)
        depth = jnp.where(kind < 2, thin_depth, thick_depth)
        y = jnp.where(kind < 2, thin_y, thick_y)
        valid = jnp.where(
            kind < 2,
            jnp.where((thin >= 0) & (thin < SHALLOW_LANES), 1, 0),
            jnp.where(lane < DEEP_LANES, 1, 0),
        )
        z = jnp.where(kind % 2 == odd_z, CZ - depth, depth - 1)
        source = swap_tile(y, odd_y) * TILE + ((y + CY) % CY) * CZ + z + odd * SLOT
        selector = where_equal(row, jnp.where(valid == 1, source, -1))
        packed = dot(parts[0], selector) + dot(parts[1], selector)
        shallow = shallow + packed[:, :2 * TILE]
        for pair in range(PAIRS):
            rows = packed[pair * ROWS:(pair + 1) * ROWS]
            thick_first[2 * pair + odd], thick_second[2 * pair + odd] = rows[:, 2 * TILE:3 * TILE], rows[:, 3 * TILE:]
    for tile in range(SHALLOW_TILES):
        for kind, out in enumerate((thin_first, thin_second)):
            strip = 0.0
            for slot in range(PER_TILE):
                pair = tile * PER_TILE + slot
                if pair < PAIRS:
                    piece = shallow[pair * ROWS:(pair + 1) * ROWS, kind * TILE:(kind + 1) * TILE]
                    strip = strip + (pltpu.roll(piece, slot * 2 * SHALLOW_LANES, 1) if slot else piece)
            out[tile] = strip


def shallow_strip(first, second, pair):
    tile, slot = pair // PER_TILE, pair % PER_TILE
    shift = (TILE - slot * 2 * SHALLOW_LANES) % TILE
    lane = iota((1, TILE), 1)
    return jnp.where(
        lane < TILE // 2,
        pltpu.roll(first[tile], shift, 1),
        pltpu.roll(second[tile], (shift + TILE // 2) % TILE, 1),
    )


def in_grid(place_ref, sizes, y, z):
    whole_y, whole_z = y + place_ref[1] * CY, z + place_ref[2] * CZ
    return (whole_y >= 0) & (whole_y < sizes[1] * CY) & (whole_z >= 0) & (whole_z < sizes[2] * CZ)


def unpack(layout, sizes, place_ref, own, along_y, along_z, start, pairs, put, shallow):
    lane = iota((1, layout.lanes), 1)
    y, z = layout.place(lane)
    odd_y, odd_z = place_ref[1] & 1, place_ref[2] & 1
    inner = swap_tile(y, odd_y) * TILE + ((y + CY) % CY) * CZ + z
    depth = jnp.where(z < 0, -z, z - (CZ - 1))
    middle = (z >= 0) & (z < CZ)
    strip = jnp.where(jnp.where(z < 0, 0, 1) == odd_z, 1, 0)
    if shallow:
        outer = lane_of(depth, y, 1, SHALLOW, SHALLOW) + 3 * TILE + strip * (TILE // 2)
        step = SHALLOW_LANES
    else:
        outer = lane_of(depth, y, 1, HALO, HALO) + (3 + strip) * TILE
        step = 0
    row = iota(((4 if shallow else 5) * TILE, layout.lanes), 0)
    valid = (lane < layout.used) & in_grid(place_ref, sizes, y, z)
    parts = []
    for odd in range(2):
        if odd == 0 or not shallow:
            parts = []
            for i in range(pairs):
                pair = start + i
                line = [r[pair] for r in (along_y[0], own, along_y[1])]
                line += [shallow_strip(*along_z, pair)] if shallow else [r[2 * pair + odd] for r in along_z]
                parts.append(jnp.concatenate(line, axis=1))
            parts = split(jnp.concatenate(parts, axis=0))
        source = jnp.where(middle, inner + odd * SLOT, outer + odd * step)
        selector = where_equal(row, jnp.where(valid, source, -1))
        placed = dot(parts[0], selector) + dot(parts[1], selector)
        for i in range(pairs):
            rows = placed[i * ROWS:(i + 1) * ROWS]
            put(2 * (start + i) + odd, rows[:MODES], rows[MODES:MODES + 1])


class Field:
    def __init__(self, full, high, low, shifts, masks=(None,) * 4):
        self.full, self.high, self.low = full, high, low
        self.shifts, self.masks = shifts, masks

    def put(self, x, value):
        self.full[x + 1] = value
        self.high[x + 1], self.low[x + 1] = split(value)

    def put_parts(self, x, high, low):
        self.full[x + 1] = high + low
        self.high[x + 1], self.low[x + 1] = high.astype(bf16), low.astype(bf16)

    def clear_ends(self):
        planes = self.full.shape[0]
        for x in (0, planes - 1):
            self.full[x] = jnp.zeros(self.full.shape[1:], f32)
            self.high[x] = jnp.zeros(self.full.shape[1:], bf16)
            self.low[x] = jnp.zeros(self.full.shape[1:], bf16)

    def get(self, x):
        return self.full[x + 1]


def field_scratch(planes, lanes):
    shape = (planes + 2, MODES, lanes)
    return [pltpu.VMEM(shape, f32), pltpu.VMEM(shape, bf16), pltpu.VMEM(shape, bf16)]


class Layout:
    def __init__(self, halo, lanes):
        self.halo, self.lanes, self.pitch = halo, lanes, CY + 2 * halo
        self.used = self.pitch * self.pitch
        self.factor = -(-(1 << 16) // self.pitch)

    def place(self, lane):
        y = (lane * self.factor) >> 16
        return y - self.halo, lane - y * self.pitch - self.halo

    def parity(self):
        y, z = self.place(iota((1, self.lanes), 1))
        return (y & 1) * 2 + (z & 1)

    def shifts(self):
        return (self.lanes - self.pitch, self.pitch, self.lanes - 1, 1)

    def field(self, refs):
        return Field(*refs, self.shifts())

    def own_lanes(self, lane):
        y, z = self.place(lane)
        return y, z, (lane < self.used) & (y >= 0) & (y < CY) & (z >= 0) & (z < CZ)


def lanes_for(halo):
    return -(-((CY + 2 * halo) ** 2) // TILE) * TILE


NEAR = 2 * SWEEPS
wide_layout = Layout(HALO, lanes_for(HALO))
near_layout = Layout(NEAR, lanes_for(NEAR))


def near_selector():
    y, z = near_layout.place(iota((1, near_layout.lanes), 1))
    source = (y + HALO) * PITCH + z + HALO
    source = jnp.where(iota((1, near_layout.lanes), 1) < near_layout.used, source, -1)
    return where_equal(iota((LANES, near_layout.lanes), 0), source)


def coupled_rows(centre, field, x):
    moved = []
    for shift, mask in zip(field.shifts, field.masks):
        part = pltpu.roll(centre, shift, 1)
        moved.append(part if mask is None else jnp.where(mask, part, 0.0))
    high, low = split(jnp.concatenate(moved, axis=0))
    high = [field.high[x], field.high[x + 2], high]
    low = [field.low[x], field.low[x + 2], low]
    return jnp.concatenate(high + high + low, axis=0)


def grouped(start, count, size, body):
    groups = -(-count // size)
    length = -(-count // groups)
    if groups == 1:
        body(start, count)
        return

    def step(i, carry):
        body(start + jnp.minimum(i * length, count - length), length)
        return carry

    lax.fori_loop(0, groups, step, 0)


def group_size(lanes):
    return 7 if lanes > 2 * TILE else 6


def sweep(source, target, start, count, wg, gain, code, store=None, size=None):
    def body(first, length):
        values = []
        for x in [first + j for j in range(length)]:
            centre = source.get(x)
            product = dot(wg[...], coupled_rows(centre, source, x))
            values.append((1.0 - relax_weight) * centre + gain[x] - pick(product, code[x], 1))
        for j, value in enumerate(values):
            (store or target.put)(first + j, value)

    grouped(start, count, size or group_size(source.full.shape[2]), body)


def residual(field, x, source, wa, wd, code):
    centre = field.get(x)
    applied = dot(wa[...], coupled_rows(centre, field, x)) + dot(wd[...], stack3(centre))
    return source - pick(applied, code, 1)


def restrict_plane(wr, residuals, parity):
    out = 0.0
    for p in range(2):
        out = out + pick(dot(wr[p], stack3(residuals[p])), parity, 0)
    return out


def expand_planes(wp, raised_high, raised_low, parity):
    product = dot(wp[...], jnp.concatenate([raised_high, raised_low, raised_high], axis=0))
    return [pick(product[p * 4 * MODES:(p + 1) * 4 * MODES], parity, 0) for p in range(2)]


def gather_mid(place_ref, here, sibling, sizes, put):
    n_gx, n_gy, n_gz = sizes
    per = MX * MY * MZ
    lines = MY * n_gz * MZ
    column = iota((1, n_gz * 2 * per), 1)
    k, rest = column % MZ, column // MZ
    gz, rest = rest % n_gz, rest // n_gz
    j, rest = rest % MY, rest // MY
    i, h = rest % MX, rest // MX
    source = gz * 2 * per + h * per + (i * MY + j) * MZ + k
    selector = where_equal(iota((n_gz * 2 * per, n_gz * 2 * per), 0), source)
    rows = here.shape[2]
    my_x, my_y, my_z = place_ref[0], place_ref[1], place_ref[2]
    parts = []
    for gx in range(n_gx):
        for gy in range(n_gy):
            slot = ((gx ^ my_x) & 1) + 2 * (((gy ^ my_y) >> 1) & 1)
            line = []
            for gz in range(n_gz):
                turn = my_z ^ gz
                line.append(jnp.where(((gy ^ my_y) & 1) == 0, here[slot, turn], sibling[slot, turn]))
            parts.append(jnp.concatenate(line, axis=1))
    placed = place(jnp.concatenate(parts, axis=0), selector)
    lower = iota((1, TILE), 1) < lines
    for gx in range(n_gx):
        for i in range(MX):
            quarters = []
            for h in range(2):
                tiles = []
                for pair in range(n_gy // 2):
                    block = [placed[(gx * n_gy + 2 * pair + s) * rows:][:rows] for s in range(2)]
                    at = ((h * MX + i) * lines) // TILE * TILE
                    block = [b[:, at:at + TILE] for b in block]
                    if i % 2 == 0:
                        block[1] = pltpu.roll(block[1], lines, 1)
                    else:
                        block[0] = pltpu.roll(block[0], lines, 1)
                    tiles.append(jnp.where(lower, block[0], block[1]))
                quarters.append(jnp.concatenate(tiles, axis=1))
            put(gx * MX + i, quarters)


class Coarse:
    def __init__(self, grid):
        self.x, self.y, self.z = (size // 2 for size in grid)
        self.plane = self.y * self.z
        self.lanes = self.x * self.plane

    def place(self, lane):
        return lane // self.plane, lane // self.z % self.y, lane % self.z

    def solve(self, value, wg, wi, code):
        x, y, z = self.place(iota((1, self.lanes), 1))
        gain = pick(dot(wi[...], stack3(value)), code, 1)
        moves = (
            (self.plane, x > 0), (self.lanes - self.plane, x < self.x - 1),
            (self.lanes - self.z, y < self.y - 1), (self.z, y > 0),
            (self.lanes - 1, z < self.z - 1), (1, z > 0),
        )

        def step(repeat, iterate):
            moved = [jnp.where(mask, pltpu.roll(iterate, shift, 1), 0.0) for shift, mask in moves]
            high, low = split(jnp.concatenate(moved, axis=0))
            product = dot(wg[...], jnp.concatenate([high, high, low], axis=0))
            return (1.0 - relax_weight) * iterate + gain - pick(product, code, 1)

        return lax.fori_loop(0, COARSE_SWEEPS - 1, step, gain)


def solve_mid(source, gain, code, coarse_source, coarse_code, fields, weights, grid):
    wg, wa, wd, wi, wr, wp = weights
    planes, size_y, size_z = grid
    lanes = size_y * size_z
    coarse = Coarse(grid)
    for i in range(2):
        fields(i).clear_ends()

    def begin(first, length):
        values = [pick(dot(wi[...], stack3(source[first + j])), code[first + j], 1) for j in range(length)]
        for j, value in enumerate(values):
            gain[first + j] = value
            fields(0).put(first + j, value)

    grouped(0, planes, 4, begin)
    lane = iota((1, lanes), 1)
    y, z = lane // size_z, lane % size_z
    parity = (y % 2) * 2 + z % 2
    tall, wide = iota((lanes, TILE), 0), iota((lanes, TILE), 1)
    squeeze = (tall // size_z // 2) * coarse.z + tall % size_z // 2
    per_tile = TILE // coarse.plane
    target = (y // 2) * coarse.z + z // 2
    row = iota((coarse.lanes, lanes), 0)

    def correct(field):
        def down(tile, carry):
            total = 0.0
            for part in range(per_tile):
                x = 2 * (tile * per_tile + part)
                rests = [residual(field, x + p, source[x + p], wa, wd, code[x + p]) for p in range(2)]
                selector = where_equal(squeeze + part * coarse.plane, wide)
                total = total + place(restrict_plane(wr, rests, parity), selector)
            coarse_source[:, pl.ds(pl.multiple_of(tile * TILE, TILE), TILE)] = total
            return carry

        lax.fori_loop(0, coarse.lanes // TILE, down, 0)
        result = coarse.solve(coarse_source[...], wg, wi, coarse_code[...])
        parts = jnp.concatenate(split(result), axis=0)

        def up(step, carry):
            for pair in (2 * step, 2 * step + 1):
                raised = dot(parts, where_equal(row, target + pair * coarse.plane)).astype(bf16)
                for p, value in enumerate(expand_planes(wp, raised[:MODES], raised[MODES:], parity)):
                    field.put(2 * pair + p, field.get(2 * pair + p) + value)
            return carry

        lax.fori_loop(0, coarse.x // 2, up, 0)

    def step(i, carry):
        sweep(fields(i % 2), fields(1 - i % 2), 0, planes, wg, gain, code, size=planes)

        @pl.when(i == SWEEPS - 2)
        def _():
            correct(fields(1 - i % 2))

        return carry

    lax.fori_loop(0, 2 * SWEEPS - 1, step, 0)
    return fields((2 * SWEEPS - 1) % 2)


def add_mid(place_ref, layout, result, field, depth, wp, grid, old):
    planes, size_y, size_z = grid
    gx, gy, gz = place_ref[0], place_ref[1], place_ref[2]
    lane = iota((1, layout.lanes), 1)
    y, z = layout.place(lane)
    whole_y, whole_z = y + gy * CY, z + gz * CZ
    inside = (lane < layout.used) & (whole_y >= 0) & (whole_y < 2 * size_y) & (whole_z >= 0) & (whole_z < 2 * size_z)
    target = jnp.where(inside, (whole_y >> 1) * size_z + (whole_z >> 1), -1)
    raise_lanes = where_equal(iota((size_y * size_z, layout.lanes), 0), target)
    parity = layout.parity()

    def body(first, length):
        values = []
        for x in [first + j for j in range(length)]:
            parts = jnp.concatenate([result.high[x + 1], result.low[x + 1]], axis=0)
            raised = dot(parts, raise_lanes).astype(bf16)
            for p, value in enumerate(expand_planes(wp, raised[:MODES], raised[MODES:], parity)):
                values.append(old[2 * x + p] + value)
        for j, value in enumerate(values):
            field.put(2 * first + j, value)

    grouped(gx * ((CX - depth) // 2), (CX + depth) // 2, max(group_size(layout.lanes) // 3, 1), body)


def fine_residual(field, own, source, wr, wa, wd, code):
    layout = near_layout
    tall, wide = iota((layout.lanes, TILE), 0), iota((layout.lanes, TILE), 1)
    y, z, inside = layout.own_lanes(tall)
    target = jnp.where(inside, (y >> 1) * MZ + (z >> 1), -BLOCK)
    per = MX * MY * MZ
    index = wide % per
    parity = layout.parity()
    def add(step, total):
        for i in (2 * step, 2 * step + 1):
            x = own + 2 * i
            rests = [residual(field, x + p, source[2 * i + p], wa, wd, code[x + p]) for p in range(2)]
            total = total + place(restrict_plane(wr, rests, parity), where_equal(target + i * MY * MZ, index))
        return total

    total = lax.fori_loop(0, MX // 2, add, jnp.zeros((MODES, TILE), f32))
    half = MODES // 2
    return jnp.where(iota((1, TILE), 1) < per, total[:half], total[half:])


def near_kernel(sizes, place_ref, own, y0, y1, z0, z1, wg, wa, wd, wi, wr, wp, source, payload, *scratch):
    layout = near_layout
    first, second = layout.field(scratch[0:3]), layout.field(scratch[3:6])
    whole, gain, code = scratch[6:9]
    first.clear_ends()
    second.clear_ends()
    gx = place_ref[0]

    def put(x, value, material):
        whole[x], code[x] = value, material

    start, pairs = gx * ((CX - SHALLOW) // 2), (CX + SHALLOW) // 2
    unpack(layout, sizes, place_ref, own, (y0, y1), (z0, z1), start, pairs, put, True)

    def begin(start, length):
        values = [pick(dot(wi[...], stack3(whole[start + j])), code[start + j], 1) for j in range(length)]
        for j, value in enumerate(values):
            gain[start + j] = value
            first.put(start + j, value)

    grouped(gx * (CX - SHALLOW), CX + SHALLOW, group_size(layout.lanes), begin)
    depth = SHALLOW - 1
    sweep(first, second, gx * (CX - depth), CX + depth, wg, gain, code)
    mine = gx * CX
    source[...] = whole[pl.ds(mine, CX)]
    payload[...] = fine_residual(second, mine, source, wr, wa, wd, code)


def gain_kernel(sizes, place_ref, own, y0, y1, z0, z1, wi, payload, gain, code, near_gain, near_code, whole):
    def put(x, value, material):
        whole[x], code[x] = value, material

    unpack(wide_layout, sizes, place_ref, own, (y0, y1), (z0, z1), 0, PAIRS, put, False)
    to_near = near_selector()

    def begin(start, length):
        values = [pick(dot(wi[...], stack3(whole[start + j])), code[start + j], 1) for j in range(length)]
        for j, value in enumerate(values):
            gain[start + j] = value
            near_gain[start + j] = place(value, to_near)
        for j in range(length):
            near_code[start + j] = dot(jnp.broadcast_to(code[start + j], (8, LANES)).astype(bf16), to_near)[:1]

    grouped(0, 2 * CX, 4, begin)


def deep_kernel(place_ref, gain, code, wg, after, solved, *scratch):
    first = wide_layout.field(scratch)
    first.clear_ends()
    for x in range(2 * CX):
        first.put(x, gain[x])
    depth = HALO - 1
    gx = place_ref[0]

    def store(x, value):
        solved[x] = value

    sweep(first, None, gx * (CX - depth), CX + depth, wg, gain, code, store)


def mid_scratch(grid):
    planes, size_y, size_z = grid
    lanes = size_y * size_z
    both = [pltpu.VMEM((2,) + ref.shape, ref.dtype) for ref in field_scratch(planes, lanes)]
    return both + [pltpu.VMEM((planes, MODES, lanes), f32)] * 2 + [pltpu.VMEM((MODES, planes * lanes // 8), f32)]


def run_mid(place_ref, here, sibling, sizes, grid, weights, scratch, mid_code, coarse_code, read_codes):
    planes, size_y, size_z = grid
    lanes = size_y * size_z
    lane = iota((1, lanes), 1)
    y, z = lane // size_z, lane % size_z
    shifts = (lanes - size_z, size_z, lanes - 1, 1)
    masks = (y < size_y - 1, y > 0, z < size_z - 1, z > 0)
    source, gain, coarse_source = scratch[3:6]

    def fields(i):
        return Field(*(ref.at[i] for ref in scratch[0:3]), shifts, masks)

    half = MODES // 2
    coarse = Coarse(grid)
    corners = []

    def put(x, quarters):
        source[x, :half] = quarters[0][:half]
        source[x, half:] = quarters[1][:half]
        if read_codes:
            mid_code[x] = quarters[0][half:half + 1]
            if x % 2 == 0:
                corners.append(jnp.broadcast_to(quarters[1][half:half + 1], (8, lanes)).astype(bf16))

    gather_mid(place_ref, here, sibling, sizes, put)
    if read_codes:
        tall, wide = iota((lanes, coarse.lanes), 0), iota((lanes, coarse.lanes), 1)
        x, cy, cz = coarse.place(wide)
        total = 0.0
        for pair in range(coarse.x):
            selector = where_equal(jnp.where(x == pair, 2 * cy * size_z + 2 * cz, -1), tall)
            total = total + dot(corners[pair], selector)
        coarse_code[...] = total[:1]
    return solve_mid(source, gain, mid_code, coarse_source, coarse_code, fields, weights, grid)


def second_kernel(sizes, grid, place_ref, here, sibling, gain, code, solved, near_gain, near_code, source,
                  wg, wa, wd, wi, wr, wp, payload, result, mid_code, coarse_code, *scratch):
    weights = (wg, wa, wd, wi, wr, wp)
    answer = run_mid(place_ref, here, sibling, sizes, grid, weights, scratch[12:], mid_code, coarse_code, True)
    first, second = wide_layout.field(scratch[0:3]), wide_layout.field(scratch[3:6])
    now, other = near_layout.field(scratch[6:9]), near_layout.field(scratch[9:12])
    for field in (first, second, now, other):
        field.clear_ends()
    depth = 3 * SWEEPS
    gx = place_ref[0]
    add_mid(place_ref, wide_layout, answer, first, depth, wp, grid, solved)
    to_near = near_selector()

    def narrow(x, value):
        parts = dot(jnp.concatenate(split(value), axis=0), to_near)
        now.put_parts(x, parts[:MODES], parts[MODES:])

    for repeat in range(2 * SWEEPS):
        depth -= 1
        start, count = gx * (CX - depth), CX + depth
        if depth > NEAR:
            sweep(first, second, start, count, wg, gain, code)
            first, second = second, first
        elif depth == NEAR:
            sweep(first, None, start, count, wg, gain, code, narrow)
        else:
            sweep(now, other, start, count, wg, near_gain, near_code)
            now, other = other, now
    payload[...] = fine_residual(now, gx * CX, source, wr, wa, wd, near_code)
    result[...] = now.full[1:1 + 2 * CX]


def third_kernel(sizes, grid, place_ref, here, sibling, mid_code, coarse_code, near_gain, near_code, solved,
                 wg, wa, wd, wi, wr, wp, result, *scratch):
    weights = (wg, wa, wd, wi, wr, wp)
    answer = run_mid(place_ref, here, sibling, sizes, grid, weights, scratch[6:], mid_code, coarse_code, False)
    layout = near_layout
    now, other = layout.field(scratch[0:3]), layout.field(scratch[3:6])
    now.clear_ends()
    other.clear_ends()
    depth = SWEEPS
    gx = place_ref[0]
    add_mid(place_ref, layout, answer, now, depth, wp, grid, solved)
    for repeat in range(SWEEPS):
        depth -= 1
        sweep(now, other, gx * (CX - depth), CX + depth, wg, near_gain, near_code)
        now, other = other, now
    tall, wide = iota((layout.lanes, TILE), 0), iota((layout.lanes, TILE), 1)
    y, z, inside = layout.own_lanes(tall)
    target = jnp.where(inside, y * CZ + z, -BLOCK)
    selectors = [where_equal(target + odd * CY * CZ, wide) for odd in range(2)]
    for pair in range(CX // 2):
        total = 0.0
        for odd in range(2):
            value = now.get(gx * CX + 2 * pair + odd)
            high, low = split(value)
            lowest = (value - high.astype(f32) - low.astype(f32)).astype(bf16)
            for part in (high, low, lowest):
                total = total + dot(part, selectors[odd])
        result[:, pair * TILE:(pair + 1) * TILE] = total


def call(kernel, cost_us, out_shape, scratch, *args, limit=16):
    vmem, smem = pl.BlockSpec(memory_space=pltpu.VMEM), pl.BlockSpec(memory_space=pltpu.SMEM)
    unused = pl.BlockSpec(memory_space=pl.ANY)
    specs = [unused if isinstance(a, After) else smem if a.dtype == jnp.int32 and a.ndim == 1 else vmem for a in args]
    args = [a.value if isinstance(a, After) else a for a in args]
    cost = pl.CostEstimate(flops=int(cost_us * 1e9), bytes_accessed=int(cost_us * 3e6), transcendentals=0)
    return pl.pallas_call(
        kernel,
        out_shape=out_shape,
        in_specs=specs,
        out_specs=jax.tree.map(lambda s: vmem, out_shape),
        scratch_shapes=scratch,
        cost_estimate=cost,
        compiler_params=pltpu.CompilerParams(vmem_limit_bytes=limit * 1024 * 1024),
    )(*args)


class After:
    def __init__(self, value):
        self.value = value


def shape_of(*dims):
    return jax.ShapeDtypeStruct(dims, f32)


def wide_device(sizes, right_side, diag_blocks, face_blocks, prolong, mats_fine, mats_mid, mats_coarse):
    n_gx, n_gy, n_gz = sizes
    axes = ("gx", "gy", "gz")
    grid = (n_gx * MX, n_gy * MY, n_gz * MZ)
    place_ref = jnp.stack([lax.axis_index(a) for a in axes]).astype(jnp.int32)
    tiles = BLOCK // TILE
    values, kinds = right_side.reshape(MODES, BLOCK), mats_fine.reshape(1, BLOCK)
    swap = [(0, 1), (1, 0)]
    others = lax.ppermute(values, "gx", swap), lax.ppermute(kinds, "gx", swap)
    scaled = invert(diag_blocks)
    own = call(
        prepare_kernel, 0.5, shape_of(2 * tiles, ROWS, TILE), [], place_ref, values, others[0], kinds, others[1]
    )
    swaps = {}
    for axis, n in zip(axes, sizes):
        inner = [pair for i in range(1, n - 1, 2) for pair in ((i, i + 1), (i + 1, i))]
        swaps[axis] = [(i, i ^ 1) for i in range(n)], [(0, 0)] + inner + [(n - 1, n - 1)]
    along_y = [lax.ppermute(own, "gy", swap) for swap in swaps["gy"]]
    weights = make_weights(scaled, diag_blocks, face_blocks, prolong)
    thin, thick = shape_of(SHALLOW_TILES, ROWS, TILE), shape_of(2 * PAIRS, ROWS, TILE)
    send = call(pack_kernel, 1.5, [thin, thin, thick, thick], [], place_ref, own, *along_y)
    shallow = [lax.ppermute(value, "gz", swap) for value, swap in zip(send[:2], swaps["gz"])]
    deep = [lax.ppermute(value, "gz", swap) for value, swap in zip(send[2:], swaps["gz"])]

    wide = field_scratch(2 * CX, LANES)
    near = field_scratch(2 * CX, near_layout.lanes)
    half, per = MODES // 2, MX * MY * MZ
    whole = shape_of(2 * CX, MODES, LANES)
    small = shape_of(2 * CX, MODES, near_layout.lanes)
    small_code = shape_of(2 * CX, 1, near_layout.lanes)
    source, payload = call(
        partial(near_kernel, sizes), 7,
        [shape_of(CX, MODES, near_layout.lanes), shape_of(half, TILE)],
        near * 2 + [pltpu.VMEM(s.shape, f32) for s in (small, small, small_code)],
        place_ref, own, *along_y, *shallow, *weights,
    )
    mid = (mats_mid.reshape(per) + 1).astype(f32)
    coarse = (mats_coarse.reshape(MX // 2, 1, MY // 2, 1, MZ // 2, 1) + 1).astype(f32)
    coarse = jnp.broadcast_to(coarse, (MX // 2, 2, MY // 2, 2, MZ // 2, 2)).reshape(per)
    tail = jnp.broadcast_to(jnp.concatenate([mid, coarse])[None], (8, TILE))

    def along_z(value):
        turns = [[(i, i ^ s) for i in range(n_gz)] for s in range(1, n_gz)]
        return jnp.stack([value] + [lax.ppermute(value, "gz", turn) for turn in turns])

    def to_all(column):
        flips = [
            [(i * n_gy + j, (i ^ dx) * n_gy + (j ^ dy)) for i in range(n_gx) for j in range(n_gy)]
            for dx, dy in ((1, 0), (0, 2), (1, 2))
        ]
        here = jnp.stack([column] + [lax.ppermute(column, ("gx", "gy"), flip) for flip in flips])
        return here, lax.ppermute(here, "gy", [(j, j ^ 1) for j in range(n_gy)])

    column = along_z(jnp.concatenate([payload, tail], axis=0))
    gain, code, near_gain, near_code = call(
        partial(gain_kernel, sizes), 6,
        [whole, shape_of(2 * CX, 1, LANES), small, small_code],
        [pltpu.VMEM(whole.shape, f32)],
        place_ref, own, *along_y, *deep, weights[3], After(payload),
    )
    solved = call(deep_kernel, 7, whole, wide, place_ref, gain, code, weights[0], After(column))
    planes, lanes = grid[0], grid[1] * grid[2]
    payload, solved, mid_code, coarse_code = call(
        partial(second_kernel, sizes, grid), 37,
        [shape_of(half, TILE), small, shape_of(planes, 1, lanes), shape_of(1, planes * lanes // 8)],
        wide * 2 + near * 2 + mid_scratch(grid),
        place_ref, *to_all(column), gain, code, solved,
        near_gain, near_code, source, *weights, limit=32,
    )
    result = call(
        partial(third_kernel, sizes, grid), 18,
        shape_of(MODES, BLOCK),
        near * 2 + mid_scratch(grid),
        place_ref, *to_all(along_z(payload)), mid_code, coarse_code, near_gain, near_code, solved, *weights,
    )
    return result[None, None, None]


def solution(mesh):
    placed = (
        P("gx", "gy", "gz", None, None),
        P(),
        P(),
        P(),
        P("gx", "gy", "gz", None),
        P("gx", "gy", "gz", None),
        P("gx", "gy", "gz", None),
    )
    sizes = tuple(mesh.shape[a] for a in ("gx", "gy", "gz"))
    wide = sizes[0] == 2 and sizes[1] == 4 and sizes[2] * MY * MZ * 2 == TILE
    return jax.shard_map(
        partial(wide_device, sizes) if wide else per_device,
        mesh=mesh,
        in_specs=placed,
        out_specs=P("gx", "gy", "gz", None, None),
        check_vma=False,
    )
```

profile of v0, /device:TPU:0, one launch (start us, length us, event | category | flops | bytes accessed | tf_op | source)
XLA Modules:
  0.0 140.8 jit_solution(1341153948446148200)
XLA Ops:
  0.0 3.0 %collective-permute-start.1 = (s32[1,512]{1,0:T(1,128)}, s32[1,512]{1,0:T(1,128)S(1)}, u32[]{:S(2)}, u32[]{:S(2)}) collective-permute-start(s32[1,512]{1,0:T(1,128)} %bitcast.30), channel_id=1, source_target_pairs={{0,16},{16,0},{1,17},{17,1},{2,18},{18,2},{3,19},{19,3},{4,20},{20... | collective-permute-start | bytes 6152 | tf_op jit(solution)/shard_map/ppermute | solution.py:919
  3.0 0.1 collective-permute-start
  3.1 1.0 copy-done.3
  4.0 6.0 %shard_map.75.scaled = f32[4,64,64]{2,1,0:T(8,128)S(1)} custom-call(f32[4,64,64]{2,1,0:T(8,128)S(1)} %copy-done.3), custom_call_target="tpu_custom_call" | custom-call | flops 6000000000 | bytes 18000000 | tf_op jit(solution)/shard_map/pallas_call | solution.py:891
  10.0 0.0 copy-done.6
  10.0 0.1 pad_add_fusion.place_ref
  10.1 0.1 convert_element_type.20
  10.2 0.1 broadcast_in_dim.6
  10.3 0.1 reshape.29
  10.4 0.0 collective-permute-done.1.other_materials
  10.4 0.0 collective-permute-done.other
  10.4 0.0 copy-done.2
  10.4 0.6 shard_map.73.own
  11.0 0.0 copy-start.7
  11.0 0.7 collective-permute-start.3
  11.7 3.2 %collective-permute-start.2 = (f32[8,72,128]{2,1,0:T(8,128)S(1)}, f32[8,72,128]{2,1,0:T(8,128)S(1)}, u32[]{:S(2)}, u32[]{:S(2)}) collective-permute-start(f32[8,72,128]{2,1,0:T(8,128)S(1)} %shard_map.73.own), channel_id=1, source_target_pairs={{0,4},{4,0},{8,12},{12,8},{1,5},{5,1},{9,13},{13,9},{2,6},{6,2},{1... | collective-permute-start | bytes 884744 | tf_op jit(solution)/shard_map/ppermute | solution.py:928
  15.0 0.0 copy-done
  15.0 0.0 copy-done.4
  15.0 0.6 shard_map.76
  15.6 0.0 collective-permute-done.3.second.y1
  15.6 0.5 collective-permute-done.2.first.y0
  16.2 2.1 %shard_map.74 = (f32[3,72,128]{2,1,0:T(8,128)S(1)}, f32[3,72,128]{2,1,0:T(8,128)S(1)}, f32[16,72,128]{2,1,0:T(8,128)S(1)}, f32[16,72,128]{2,1,0:T(8,128)S(1)}) custom-call(s32[3]{0:T(128)S(1)} %pad_add_fusion.place_ref, f32[8,72,128]{2,1,0:T(8,128)S(1)} %shard_map.73.own, f32[8,72,128]{2,1,0:T(8,128)S(1)} %collective-permute-done.2.first.y0, ...), custom_call_target="tpu_custom_call" | custom-call | flops 1500000000 | bytes 4500000 | tf_op jit(solution)/shard_map/pallas_call | solution.py:891
  18.3 1.6 %collective-permute-start.4 = (f32[3,72,128]{2,1,0:T(8,128)S(1)}, f32[3,72,128]{2,1,0:T(8,128)S(1)}, u32[]{:S(2)}, u32[]{:S(2)}) collective-permute-start(f32[3,72,128]{2,1,0:T(8,128)S(1)} %get-tuple-element.25), channel_id=1, source_target_pairs={{0,1},{1,0},{2,3},{3,2},{4,5},{5,4},{6,7},{7,6},{8,9},{9,8},{10,11... | collective-permute-start | bytes 331784 | tf_op jit(solution)/shard_map/ppermute | solution.py:932
  19.9 0.7 collective-permute-start.5
  20.6 0.1 pad_maximum_fusion.5
  20.6 4.4 %collective-permute-start.13 = (f32[16,72,128]{2,1,0:T(8,128)S(1)}, f32[16,72,128]{2,1,0:T(8,128)S(1)}, u32[]{:S(2)}, u32[]{:S(2)}) collective-permute-start(f32[16,72,128]{2,1,0:T(8,128)S(1)} %get-tuple-element.34), channel_id=1, source_target_pairs={{0,1},{1,0},{2,3},{3,2},{4,5},{5,4},{6,7},{7,6},{8,9},{9,8},{10,11... | collective-permute-start | bytes 1769480 | tf_op jit(solution)/shard_map/ppermute | solution.py:933
  25.0 0.9 collective-permute-start.14
  25.9 0.0 collective-permute-done.4.z0
  25.9 0.0 collective-permute-done.5.z1
  25.9 8.0 %shard_map.77 = (f32[8,64,256]{2,1,0:T(8,128)S(1)}, f32[32,128]{1,0:T(8,128)S(1)}) custom-call(s32[3]{0:T(128)S(1)} %pad_add_fusion.place_ref, f32[8,72,128]{2,1,0:T(8,128)S(1)} %shard_map.73.own, f32[8,72,128]{2,1,0:T(8,128)S(1)} %collective-permute-done.2.first.y0, f32[8,72,128]{2,1,0:T(8,128)S(1)} %collective-permute-done.3.second.y1, ...), custom_call_target="tpu_custom_call" | custom-call | flops 7000000000 | bytes 21000000 | tf_op jit(solution)/shard_map/pallas_call | solution.py:891
  33.9 3.2 %collective-permute-start.7 = (f32[40,128]{1,0:T(8,128)S(1)}, f32[40,128]{1,0:T(8,128)S(1)}, u32[]{:S(2)}, u32[]{:S(2)}) collective-permute-start(f32[40,128]{1,0:T(8,128)S(1)} %get-tuple-element.50), channel_id=1, source_target_pairs={{0,2},{1,3},{2,0},{3,1},{4,6},{5,7},{6,4},{7,5},{8,10},{9,11},{10,... | collective-permute-start | bytes 61448 | tf_op jit(solution)/shard_map/ppermute | solution.py:954
  37.2 0.0 collective-permute-start.6
  37.2 1.5 %collective-permute-start.8 = (f32[40,128]{1,0:T(8,128)S(1)}, f32[40,128]{1,0:T(8,128)S(1)}, u32[]{:S(2)}, u32[]{:S(2)}) collective-permute-start(f32[40,128]{1,0:T(8,128)S(1)} %get-tuple-element.50), channel_id=1, source_target_pairs={{0,3},{1,2},{2,1},{3,0},{4,7},{5,6},{6,5},{7,4},{8,11},{9,10},{10,... | collective-permute-start | bytes 61448 | tf_op jit(solution)/shard_map/ppermute | solution.py:954
  38.7 3.1 %collective-permute-done.7 = f32[40,128]{1,0:T(8,128)S(1)} collective-permute-done((f32[40,128]{1,0:T(8,128)S(1)}, f32[40,128]{1,0:T(8,128)S(1)}, u32[]{:S(2)}, u32[]{:S(2)}) %collective-permute-start.7) | collective-permute-done | bytes 20512 | tf_op jit(solution)/shard_map/ppermute | solution.py:954
  41.8 0.0 collective-permute-done.6
  41.8 1.1 collective-permute-done.8
  42.9 6.9 %collective-permute-start.11 = (f32[4,40,128]{2,1,0:T(8,128)S(1)}, f32[4,40,128]{2,1,0:T(8,128)S(1)}, u32[]{:S(2)}, u32[]{:S(2)}) collective-permute-start(f32[4,40,128]{2,1,0:T(8,128)S(1)} %get-tuple-element.46.after), channel_id=1, source_target_pairs={{0,24},{4,28},{8,16},{12,20},{16,8},{20,12},{24,0},{28,4},{1,25},{... | collective-permute-start | bytes 245768 | tf_op jit(solution)/shard_map/ppermute | solution.py:961
  49.8 0.0 collective-permute-start.10
  49.8 0.6 collective-permute-start.9
  50.4 1.8 %collective-permute-done.11 = f32[4,40,128]{2,1,0:T(8,128)S(1)} collective-permute-done((f32[4,40,128]{2,1,0:T(8,128)S(1)}, f32[4,40,128]{2,1,0:T(8,128)S(1)}, u32[]{:S(2)}, u32[]{:S(2)}) %collective-permute-start.11) | collective-permute-done | bytes 81952 | tf_op jit(solution)/shard_map/ppermute | solution.py:961
  52.2 2.0 %collective-permute-done.10 = f32[4,40,128]{2,1,0:T(8,128)S(1)} collective-permute-done((f32[4,40,128]{2,1,0:T(8,128)S(1)}, f32[4,40,128]{2,1,0:T(8,128)S(1)}, u32[]{:S(2)}, u32[]{:S(2)}) %collective-permute-start.10) | collective-permute-done | bytes 81952 | tf_op jit(solution)/shard_map/ppermute | solution.py:961
  54.2 0.0 collective-permute-done.9
  54.2 0.1 collective-permute-start.12
  54.3 0.0 collective-permute-done.13.z0
  54.3 0.0 collective-permute-done.14.z1
  54.3 6.4 %shard_map.78 = (f32[16,64,512]{2,1,0:T(8,128)S(1)}, f32[16,1,512]{2,1,0:T(1,128)S(1)}, f32[16,64,256]{2,1,0:T(8,128)S(1)}, f32[16,1,256]{2,1,0:T(1,128)S(1)}) custom-call(s32[3]{0:T(128)S(1)} %pad_add_fusion.place_ref, f32[8,72,128]{2,1,0:T(8,128)S(1)} %shard_map.73.own, f32[8,72,128]{2,1,0:T(8,128)S(1)} %collective-permute-done.2.first.y0, ...), custom_call_target="tpu_custom_call" | custom-call | flops 6000000000 | bytes 18000000 | tf_op jit(solution)/shard_map/pallas_call | solution.py:891
  60.8 6.4 %shard_map.79.solved = f32[16,64,512]{2,1,0:T(8,128)S(1)} custom-call(s32[3]{0:T(128)S(1)} %pad_add_fusion.place_ref, f32[16,64,512]{2,1,0:T(8,128)S(1)} %get-tuple-element.36.gain, f32[16,1,512]{2,1,0:T(1,128)S(1)} %get-tuple-element.37.code, bf16[256,1152]{1,0:T(8,128)(2,1)S(1)} %get-tuple-element.27.wg, f32[4,40,128]{2,1,0:T(8,128)S(1)} %get-tuple-element.46.after), custom_call_target="tpu_custom_call" | custom-call | flops 7000000000 | bytes 21000000 | tf_op jit(solution)/shard_map/pallas_call | solution.py:891
  67.2 0.0 collective-permute-done.12.sibling
  67.2 37.4 %shard_map.80 = (f32[32,128]{1,0:T(8,128)S(1)}, f32[16,64,256]{2,1,0:T(8,128)S(1)}, f32[8,1,256]{2,1,0:T(1,128)S(1)}, f32[1,256]{1,0:T(1,128)S(1)}) custom-call(s32[3]{0:T(128)S(1)} %pad_add_fusion.place_ref, f32[4,4,40,128]{3,2,1,0:T(8,128)S(1)} %pad_maximum_fusion.here, f32[4,4,40,128]{3,2,1,0:T(8,128)S(1)} %collective-permute-done.12.sibling, ...), custom_call_target="tpu_custom_call" | custom-call | flops 36999999488 | bytes 111000000 | tf_op jit(solution)/shard_map/pallas_call | solution.py:891
  104.6 1.6 %collective-permute-start.17 = (f32[32,128]{1,0:T(8,128)S(1)}, f32[32,128]{1,0:T(8,128)S(1)}, u32[]{:S(2)}, u32[]{:S(2)}) collective-permute-start(f32[32,128]{1,0:T(8,128)S(1)} %get-tuple-element.41), channel_id=1, source_target_pairs={{0,3},{1,2},{2,1},{3,0},{4,7},{5,6},{6,5},{7,4},{8,11},{9,10},{10,... | collective-permute-start | bytes 49160 | tf_op jit(solution)/shard_map/ppermute | solution.py:954
  106.2 0.1 collective-permute-start.16
  106.4 2.7 %collective-permute-start.15 = (f32[32,128]{1,0:T(8,128)S(1)}, f32[32,128]{1,0:T(8,128)S(1)}, u32[]{:S(2)}, u32[]{:S(2)}) collective-permute-start(f32[32,128]{1,0:T(8,128)S(1)} %get-tuple-element.41), channel_id=1, source_target_pairs={{0,1},{1,0},{2,3},{3,2},{4,5},{5,4},{6,7},{7,6},{8,9},{9,8},{10,11... | collective-permute-start | bytes 49160 | tf_op jit(solution)/shard_map/ppermute | solution.py:954
  109.1 1.3 collective-permute-done.17
  110.4 0.5 collective-permute-done.16
  110.9 0.1 collective-permute-done.15
  111.0 2.1 %collective-permute-start.19 = (f32[4,32,128]{2,1,0:T(8,128)S(1)}, f32[4,32,128]{2,1,0:T(8,128)S(1)}, u32[]{:S(2)}, u32[]{:S(2)}) collective-permute-start(f32[4,32,128]{2,1,0:T(8,128)S(1)} %get-tuple-element.48), channel_id=1, source_target_pairs={{0,8},{4,12},{8,0},{12,4},{16,24},{20,28},{24,16},{28,20},{1,9},{5... | collective-permute-start | bytes 196616 | tf_op jit(solution)/shard_map/ppermute | solution.py:961
  113.0 0.5 collective-permute-start.18
  113.6 1.0 collective-permute-start.20
  114.6 0.7 collective-permute-done.19
  115.3 2.0 %collective-permute-done.18 = f32[4,32,128]{2,1,0:T(8,128)S(1)} collective-permute-done((f32[4,32,128]{2,1,0:T(8,128)S(1)}, f32[4,32,128]{2,1,0:T(8,128)S(1)}, u32[]{:S(2)}, u32[]{:S(2)}) %collective-permute-start.18) | collective-permute-done | bytes 65568 | tf_op jit(solution)/shard_map/ppermute | solution.py:961
  117.3 1.4 %collective-permute-done.20 = f32[4,32,128]{2,1,0:T(8,128)S(1)} collective-permute-done((f32[4,32,128]{2,1,0:T(8,128)S(1)}, f32[4,32,128]{2,1,0:T(8,128)S(1)}, u32[]{:S(2)}, u32[]{:S(2)}) %collective-permute-start.20) | collective-permute-done | bytes 65568 | tf_op jit(solution)/shard_map/ppermute | solution.py:961
  118.8 0.1 collective-permute-start.21
  118.8 1.5 %collective-permute-done.21.sibling = f32[4,4,32,128]{3,2,1,0:T(8,128)S(1)} collective-permute-done((f32[4,4,32,128]{3,2,1,0:T(8,128)S(1)}, f32[4,4,32,128]{3,2,1,0:T(8,128)S(1)}, u32[]{:S(2)}, u32[]{:S(2)}) %collective-permute-start.21) | collective-permute-done | bytes 262176 | tf_op jit(solution)/shard_map/ppermute | solution.py:962
  120.4 20.4 %shard_map.81 = f32[64,512]{1,0:T(8,128)} custom-call(s32[3]{0:T(128)S(1)} %pad_add_fusion.place_ref, f32[4,4,32,128]{3,2,1,0:T(8,128)S(1)} %pad_maximum_fusion.1.here, f32[4,4,32,128]{3,2,1,0:T(8,128)S(1)} %collective-permute-done.21.sibling, f32[8,1,256]{2,1,0:T(1,128)S(1)} %get-tuple-element.42.mid_code, f32[1,256]{1,0:T(1,128)S(1)} %get-tuple-element.43.coarse_code, ...), custom_call_target="tpu_custom_call" | custom-call | flops 17999998976 | bytes 54000000 | tf_op jit(solution)/shard_map/pallas_call | solution.py:891
  (18 shorter events, 0.1 us)
Async XLA Ops:
  0.0 10.4 %collective-permute-start.1 = (s32[1,512]{1,0:T(1,128)}, s32[1,512]{1,0:T(1,128)S(1)}, u32[]{:S(2)}, u32[]{:S(2)}) collective-permute-start(s32[1,512]{1,0:T(1,128)} %bitcast.30), channel_id=1, source_target_pairs={{0,16},{16,0},{1,17},{17,1},{2,18},{18,2},{3,19},{19,3},{4,20},{20... | collective-permute-start | bytes 6152 | tf_op jit(solution)/shard_map/ppermute | solution.py:919
  3.0 7.5 %copy-start.2 = (f32[1,1,1,64,512]{4,3,2,1,0:T(8,128)S(1)}, f32[1,1,1,64,512]{4,3,2,1,0:T(8,128)}, u32[]{:S(2)}) copy-start(f32[1,1,1,64,512]{4,3,2,1,0:T(8,128)} %param.7) | copy-start | bytes 393220
  3.0 12.0 %copy-start = (f32[6,4,64,64]{3,2,1,0:T(8,128)S(1)}, f32[6,4,64,64]{3,2,1,0:T(8,128)}, u32[]{:S(2)}) copy-start(f32[6,4,64,64]{3,2,1,0:T(8,128)} %face.1) | copy-start | bytes 1179652
  3.0 12.0 %copy-start.1 = (f32[8,64,64]{2,1,0:T(8,128)S(1)}, f32[8,64,64]{2,1,0:T(8,128)}, u32[]{:S(2)}) copy-start(f32[8,64,64]{2,1,0:T(8,128)} %prolong.1) | copy-start | bytes 393220
  3.0 7.4 %collective-permute-start = (f32[64,512]{1,0:T(8,128)}, f32[64,512]{1,0:T(8,128)S(1)}, u32[]{:S(2)}, u32[]{:S(2)}) collective-permute-start(f32[64,512]{1,0:T(8,128)} %bitcast.28), channel_id=1, source_target_pairs={{0,16},{16,0},{1,17},{17,1},{2,18},{18,2},{3,19},{19,3},{4,20},{20... | collective-permute-start | bytes 393224 | tf_op jit(solution)/shard_map/ppermute | solution.py:919
  3.1 1.0 copy-start.3
  4.0 6.0 %copy-start.6 = (s32[1,1,1,8]{3,2,1,0:T(1,128)S(1)}, s32[1,1,1,8]{3,2,1,0:T(1,128)}, u32[]{:S(2)}) copy-start(s32[1,1,1,8]{3,2,1,0:T(1,128)} %param.13) | copy-start | bytes 100
  4.0 6.4 %copy-start.5 = (s32[1,1,1,512]{3,2,1,0:T(1,128)S(1)}, s32[1,1,1,512]{3,2,1,0:T(1,128)}, u32[]{:S(2)}) copy-start(s32[1,1,1,512]{3,2,1,0:T(1,128)} %param.11) | copy-start | bytes 6148
  4.0 10.9 %copy-start.4 = (f32[4,64,64]{2,1,0:T(8,128)S(1)}, f32[4,64,64]{2,1,0:T(8,128)}, u32[]{:S(2)}) copy-start(f32[4,64,64]{2,1,0:T(8,128)} %diag.3) | copy-start | bytes 196612
  11.0 4.6 %copy-start.7 = (s32[1,1,1,64]{3,2,1,0:T(1,128)S(1)}, s32[1,1,1,64]{3,2,1,0:T(1,128)}, u32[]{:S(2)}) copy-start(s32[1,1,1,64]{3,2,1,0:T(1,128)} %param.12) | copy-start | bytes 772
  11.0 4.6 %collective-permute-start.3 = (f32[8,72,128]{2,1,0:T(8,128)S(1)}, f32[8,72,128]{2,1,0:T(8,128)S(1)}, u32[]{:S(2)}, u32[]{:S(2)}) collective-permute-start(f32[8,72,128]{2,1,0:T(8,128)S(1)} %shard_map.73.own), channel_id=1, source_target_pairs={{0,0},{4,8},{8,4},{12,12},{1,1},{5,9},{9,5},{13,13},{2,2},{6,10},{... | collective-permute-start | bytes 884744 | tf_op jit(solution)/shard_map/ppermute | solution.py:928
  11.7 4.5 %collective-permute-start.2 = (f32[8,72,128]{2,1,0:T(8,128)S(1)}, f32[8,72,128]{2,1,0:T(8,128)S(1)}, u32[]{:S(2)}, u32[]{:S(2)}) collective-permute-start(f32[8,72,128]{2,1,0:T(8,128)S(1)} %shard_map.73.own), channel_id=1, source_target_pairs={{0,4},{4,0},{8,12},{12,8},{1,5},{5,1},{9,13},{13,9},{2,6},{6,2},{1... | collective-permute-start | bytes 884744 | tf_op jit(solution)/shard_map/ppermute | solution.py:928
  18.3 7.7 %collective-permute-start.4 = (f32[3,72,128]{2,1,0:T(8,128)S(1)}, f32[3,72,128]{2,1,0:T(8,128)S(1)}, u32[]{:S(2)}, u32[]{:S(2)}) collective-permute-start(f32[3,72,128]{2,1,0:T(8,128)S(1)} %get-tuple-element.25), channel_id=1, source_target_pairs={{0,1},{1,0},{2,3},{3,2},{4,5},{5,4},{6,7},{7,6},{8,9},{9,8},{10,11... | collective-permute-start | bytes 331784 | tf_op jit(solution)/shard_map/ppermute | solution.py:932
  19.9 6.0 %collective-permute-start.5 = (f32[3,72,128]{2,1,0:T(8,128)S(1)}, f32[3,72,128]{2,1,0:T(8,128)S(1)}, u32[]{:S(2)}, u32[]{:S(2)}) collective-permute-start(f32[3,72,128]{2,1,0:T(8,128)S(1)} %get-tuple-element.26), channel_id=1, source_target_pairs={{0,0},{1,2},{2,1},{3,3},{4,4},{5,6},{6,5},{7,7},{8,8},{9,10},{10,9... | collective-permute-start | bytes 331784 | tf_op jit(solution)/shard_map/ppermute | solution.py:932
  20.6 33.7 %collective-permute-start.13 = (f32[16,72,128]{2,1,0:T(8,128)S(1)}, f32[16,72,128]{2,1,0:T(8,128)S(1)}, u32[]{:S(2)}, u32[]{:S(2)}) collective-permute-start(f32[16,72,128]{2,1,0:T(8,128)S(1)} %get-tuple-element.34), channel_id=1, source_target_pairs={{0,1},{1,0},{2,3},{3,2},{4,5},{5,4},{6,7},{7,6},{8,9},{9,8},{10,11... | collective-permute-start | bytes 1769480 | tf_op jit(solution)/shard_map/ppermute | solution.py:933
  25.0 29.3 %collective-permute-start.14 = (f32[16,72,128]{2,1,0:T(8,128)S(1)}, f32[16,72,128]{2,1,0:T(8,128)S(1)}, u32[]{:S(2)}, u32[]{:S(2)}) collective-permute-start(f32[16,72,128]{2,1,0:T(8,128)S(1)} %get-tuple-element.35), channel_id=1, source_target_pairs={{0,0},{1,2},{2,1},{3,3},{4,4},{5,6},{6,5},{7,7},{8,8},{9,10},{10,9... | collective-permute-start | bytes 1769480 | tf_op jit(solution)/shard_map/ppermute | solution.py:933
  33.9 7.9 %collective-permute-start.7 = (f32[40,128]{1,0:T(8,128)S(1)}, f32[40,128]{1,0:T(8,128)S(1)}, u32[]{:S(2)}, u32[]{:S(2)}) collective-permute-start(f32[40,128]{1,0:T(8,128)S(1)} %get-tuple-element.50), channel_id=1, source_target_pairs={{0,2},{1,3},{2,0},{3,1},{4,6},{5,7},{6,4},{7,5},{8,10},{9,11},{10,... | collective-permute-start | bytes 61448 | tf_op jit(solution)/shard_map/ppermute | solution.py:954
  37.2 4.6 %collective-permute-start.6 = (f32[40,128]{1,0:T(8,128)S(1)}, f32[40,128]{1,0:T(8,128)S(1)}, u32[]{:S(2)}, u32[]{:S(2)}) collective-permute-start(f32[40,128]{1,0:T(8,128)S(1)} %get-tuple-element.50), channel_id=1, source_target_pairs={{0,1},{1,0},{2,3},{3,2},{4,5},{5,4},{6,7},{7,6},{8,9},{9,8},{10,11... | collective-permute-start | bytes 61448 | tf_op jit(solution)/shard_map/ppermute | solution.py:954
  37.2 5.7 %collective-permute-start.8 = (f32[40,128]{1,0:T(8,128)S(1)}, f32[40,128]{1,0:T(8,128)S(1)}, u32[]{:S(2)}, u32[]{:S(2)}) collective-permute-start(f32[40,128]{1,0:T(8,128)S(1)} %get-tuple-element.50), channel_id=1, source_target_pairs={{0,3},{1,2},{2,1},{3,0},{4,7},{5,6},{6,5},{7,4},{8,11},{9,10},{10,... | collective-permute-start | bytes 61448 | tf_op jit(solution)/shard_map/ppermute | solution.py:954
  42.9 9.3 %collective-permute-start.11 = (f32[4,40,128]{2,1,0:T(8,128)S(1)}, f32[4,40,128]{2,1,0:T(8,128)S(1)}, u32[]{:S(2)}, u32[]{:S(2)}) collective-permute-start(f32[4,40,128]{2,1,0:T(8,128)S(1)} %get-tuple-element.46.after), channel_id=1, source_target_pairs={{0,24},{4,28},{8,16},{12,20},{16,8},{20,12},{24,0},{28,4},{1,25},{... | collective-permute-start | bytes 245768 | tf_op jit(solution)/shard_map/ppermute | solution.py:961
  49.8 4.4 %collective-permute-start.10 = (f32[4,40,128]{2,1,0:T(8,128)S(1)}, f32[4,40,128]{2,1,0:T(8,128)S(1)}, u32[]{:S(2)}, u32[]{:S(2)}) collective-permute-start(f32[4,40,128]{2,1,0:T(8,128)S(1)} %get-tuple-element.46.after), channel_id=1, source_target_pairs={{0,8},{4,12},{8,0},{12,4},{16,24},{20,28},{24,16},{28,20},{1,9},{5... | collective-permute-start | bytes 245768 | tf_op jit(solution)/shard_map/ppermute | solution.py:961
  49.8 4.4 %collective-permute-start.9 = (f32[4,40,128]{2,1,0:T(8,128)S(1)}, f32[4,40,128]{2,1,0:T(8,128)S(1)}, u32[]{:S(2)}, u32[]{:S(2)}) collective-permute-start(f32[4,40,128]{2,1,0:T(8,128)S(1)} %get-tuple-element.46.after), channel_id=1, source_target_pairs={{0,16},{4,20},{8,24},{12,28},{16,0},{20,4},{24,8},{28,12},{1,17},{... | collective-permute-start | bytes 245768 | tf_op jit(solution)/shard_map/ppermute | solution.py:961
  54.2 13.0 %collective-permute-start.12 = (f32[4,4,40,128]{3,2,1,0:T(8,128)S(1)}, f32[4,4,40,128]{3,2,1,0:T(8,128)S(1)}, u32[]{:S(2)}, u32[]{:S(2)}) collective-permute-start(f32[4,4,40,128]{3,2,1,0:T(8,128)S(1)} %pad_maximum_fusion.here), channel_id=1, source_target_pairs={{0,4},{4,0},{8,12},{12,8},{1,5},{5,1},{9,13},{13,9},{2,6},{6,2},{1... | collective-permute-start | bytes 983048 | tf_op jit(solution)/shard_map/ppermute | solution.py:962
  104.6 5.7 %collective-permute-start.17 = (f32[32,128]{1,0:T(8,128)S(1)}, f32[32,128]{1,0:T(8,128)S(1)}, u32[]{:S(2)}, u32[]{:S(2)}) collective-permute-start(f32[32,128]{1,0:T(8,128)S(1)} %get-tuple-element.41), channel_id=1, source_target_pairs={{0,3},{1,2},{2,1},{3,0},{4,7},{5,6},{6,5},{7,4},{8,11},{9,10},{10,... | collective-permute-start | bytes 49160 | tf_op jit(solution)/shard_map/ppermute | solution.py:954
  106.2 4.7 %collective-permute-start.16 = (f32[32,128]{1,0:T(8,128)S(1)}, f32[32,128]{1,0:T(8,128)S(1)}, u32[]{:S(2)}, u32[]{:S(2)}) collective-permute-start(f32[32,128]{1,0:T(8,128)S(1)} %get-tuple-element.41), channel_id=1, source_target_pairs={{0,2},{1,3},{2,0},{3,1},{4,6},{5,7},{6,4},{7,5},{8,10},{9,11},{10,... | collective-permute-start | bytes 49160 | tf_op jit(solution)/shard_map/ppermute | solution.py:954
  106.4 4.6 %collective-permute-start.15 = (f32[32,128]{1,0:T(8,128)S(1)}, f32[32,128]{1,0:T(8,128)S(1)}, u32[]{:S(2)}, u32[]{:S(2)}) collective-permute-start(f32[32,128]{1,0:T(8,128)S(1)} %get-tuple-element.41), channel_id=1, source_target_pairs={{0,1},{1,0},{2,3},{3,2},{4,5},{5,4},{6,7},{7,6},{8,9},{9,8},{10,11... | collective-permute-start | bytes 49160 | tf_op jit(solution)/shard_map/ppermute | solution.py:954
  111.0 4.3 %collective-permute-start.19 = (f32[4,32,128]{2,1,0:T(8,128)S(1)}, f32[4,32,128]{2,1,0:T(8,128)S(1)}, u32[]{:S(2)}, u32[]{:S(2)}) collective-permute-start(f32[4,32,128]{2,1,0:T(8,128)S(1)} %get-tuple-element.48), channel_id=1, source_target_pairs={{0,8},{4,12},{8,0},{12,4},{16,24},{20,28},{24,16},{28,20},{1,9},{5... | collective-permute-start | bytes 196616 | tf_op jit(solution)/shard_map/ppermute | solution.py:961
  113.0 4.3 %collective-permute-start.18 = (f32[4,32,128]{2,1,0:T(8,128)S(1)}, f32[4,32,128]{2,1,0:T(8,128)S(1)}, u32[]{:S(2)}, u32[]{:S(2)}) collective-permute-start(f32[4,32,128]{2,1,0:T(8,128)S(1)} %get-tuple-element.48), channel_id=1, source_target_pairs={{0,16},{4,20},{8,24},{12,28},{16,0},{20,4},{24,8},{28,12},{1,17},{... | collective-permute-start | bytes 196616 | tf_op jit(solution)/shard_map/ppermute | solution.py:961
  113.6 5.2 %collective-permute-start.20 = (f32[4,32,128]{2,1,0:T(8,128)S(1)}, f32[4,32,128]{2,1,0:T(8,128)S(1)}, u32[]{:S(2)}, u32[]{:S(2)}) collective-permute-start(f32[4,32,128]{2,1,0:T(8,128)S(1)} %get-tuple-element.48), channel_id=1, source_target_pairs={{0,24},{4,28},{8,16},{12,20},{16,8},{20,12},{24,0},{28,4},{1,25},{... | collective-permute-start | bytes 196616 | tf_op jit(solution)/shard_map/ppermute | solution.py:961
  118.8 1.6 %collective-permute-start.21 = (f32[4,4,32,128]{3,2,1,0:T(8,128)S(1)}, f32[4,4,32,128]{3,2,1,0:T(8,128)S(1)}, u32[]{:S(2)}, u32[]{:S(2)}) collective-permute-start(f32[4,4,32,128]{3,2,1,0:T(8,128)S(1)} %pad_maximum_fusion.1.here), channel_id=1, source_target_pairs={{0,4},{4,0},{8,12},{12,8},{1,5},{5,1},{9,13},{13,9},{2,6},{6,2},{1... | collective-permute-start | bytes 786440 | tf_op jit(solution)/shard_map/ppermute | solution.py:962
where the time goes:
time: 141 us
  Pallas kernels  87.9 us (62%)
  starting transfers between devices  35 us (25%)
  waiting for transfers between devices  16.1 us (11%)
    pallas_call x9, Pallas kernels, call(): pl.pallas_call(kernel, out_shape=out_shape, in_specs=specs, out_specs=jax...  87.9 us
    ppermute x6, starting transfers between devices, to_all(): lax.ppermute(column, ('gx', 'gy'), flip)  11.1 us
    ppermute x6, starting transfers between devices, along_z(): lax.ppermute(value, 'gz', turn)  9.24 us
    ppermute x6, waiting for transfers between devices, to_all(): lax.ppermute(column, ('gx', 'gy'), flip)  7.94 us
    ppermute x4, starting transfers between devices, wide_device(): lax.ppermute(value, 'gz', swap)  7.56 us
    ppermute x6, waiting for transfers between devices, along_z(): lax.ppermute(value, 'gz', turn)  6.06 us
    ppermute x2, starting transfers between devices, wide_device(): along_y = [lax.ppermute(own, 'gy', swap) for swap in swaps['gy']]  3.92 us
    ppermute x2, starting transfers between devices, wide_device(): others = (lax.ppermute(values, 'gx', swap), lax.ppermute(kinds, 'gx', swap))  3.05 us
  transfers between devices with their start and end apart: 22, of which 12 were waited for; matrix products, arithmetic and copies ran while one was open for 0% of the time, Pallas kernels for 19%

commit v1 on v0

--- a/solution.py
+++ b/solution.py
@@ -745,7 +745,7 @@
     payload[...] = fine_residual(second, mine, source, wr, wa, wd, code)
 
 
-def gain_kernel(sizes, place_ref, own, y0, y1, z0, z1, wi, payload, gain, code, near_gain, near_code, whole):
+def gain_kernel(sizes, place_ref, own, y0, y1, z0, z1, wi, payload, gain, code, near_gain, near_code, passed, whole):
     def put(x, value, material):
         whole[x], code[x] = value, material
 
@@ -761,9 +761,11 @@
             near_code[start + j] = dot(jnp.broadcast_to(code[start + j], (8, LANES)).astype(bf16), to_near)[:1]
 
     grouped(0, 2 * CX, 4, begin)
-
-
-def deep_kernel(place_ref, gain, code, wg, after, solved, *scratch):
+    passed[...] = payload[...]
+
+
+def deep_kernel(place_ref, gain, code, wg, column, solved, passed, *scratch):
+    passed[...] = column[...]
     first = wide_layout.field(scratch)
     first.clear_ends()
     for x in range(2 * CX):
@@ -884,9 +886,7 @@
 
 def call(kernel, cost_us, out_shape, scratch, *args, limit=16):
     vmem, smem = pl.BlockSpec(memory_space=pltpu.VMEM), pl.BlockSpec(memory_space=pltpu.SMEM)
-    unused = pl.BlockSpec(memory_space=pl.ANY)
-    specs = [unused if isinstance(a, After) else smem if a.dtype == jnp.int32 and a.ndim == 1 else vmem for a in args]
-    args = [a.value if isinstance(a, After) else a for a in args]
+    specs = [smem if a.dtype == jnp.int32 and a.ndim == 1 else vmem for a in args]
     cost = pl.CostEstimate(flops=int(cost_us * 1e9), bytes_accessed=int(cost_us * 3e6), transcendentals=0)
     return pl.pallas_call(
         kernel,
@@ -897,11 +897,6 @@
         cost_estimate=cost,
         compiler_params=pltpu.CompilerParams(vmem_limit_bytes=limit * 1024 * 1024),
     )(*args)
-
-
-class After:
-    def __init__(self, value):
-        self.value = value
 
 
 def shape_of(*dims):
@@ -951,37 +946,47 @@
 
     def along_z(value):
         turns = [[(i, i ^ s) for i in range(n_gz)] for s in range(1, n_gz)]
-        return jnp.stack([value] + [lax.ppermute(value, "gz", turn) for turn in turns])
-
-    def to_all(column):
+        return [lax.ppermute(value, "gz", turn) for turn in turns]
+
+    def across(column):
         flips = [
             [(i * n_gy + j, (i ^ dx) * n_gy + (j ^ dy)) for i in range(n_gx) for j in range(n_gy)]
             for dx, dy in ((1, 0), (0, 2), (1, 2))
         ]
-        here = jnp.stack([column] + [lax.ppermute(column, ("gx", "gy"), flip) for flip in flips])
+        return [lax.ppermute(column, ("gx", "gy"), flip) for flip in flips]
+
+    def with_sibling(here):
         return here, lax.ppermute(here, "gy", [(j, j ^ 1) for j in range(n_gy)])
 
-    column = along_z(jnp.concatenate([payload, tail], axis=0))
-    gain, code, near_gain, near_code = call(
+    payload = jnp.concatenate([payload, tail], axis=0)
+    turned = along_z(payload)
+    gain, code, near_gain, near_code, payload = call(
         partial(gain_kernel, sizes), 6,
-        [whole, shape_of(2 * CX, 1, LANES), small, small_code],
+        [whole, shape_of(2 * CX, 1, LANES), small, small_code, shape_of(*payload.shape)],
         [pltpu.VMEM(whole.shape, f32)],
-        place_ref, own, *along_y, *deep, weights[3], After(payload),
-    )
-    solved = call(deep_kernel, 7, whole, wide, place_ref, gain, code, weights[0], After(column))
+        place_ref, own, *along_y, *deep, weights[3], payload,
+    )
+    column = jnp.stack([payload] + turned)
+    flipped = across(column)
+    solved, column = call(
+        deep_kernel, 7, [whole, shape_of(*column.shape)], wide, place_ref, gain, code, weights[0], column
+    )
+    gathered = with_sibling(jnp.stack([column] + flipped))
     planes, lanes = grid[0], grid[1] * grid[2]
     payload, solved, mid_code, coarse_code = call(
         partial(second_kernel, sizes, grid), 37,
         [shape_of(half, TILE), small, shape_of(planes, 1, lanes), shape_of(1, planes * lanes // 8)],
         wide * 2 + near * 2 + mid_scratch(grid),
-        place_ref, *to_all(column), gain, code, solved,
+        place_ref, *gathered, gain, code, solved,
         near_gain, near_code, source, *weights, limit=32,
     )
+    column = jnp.stack([payload] + along_z(payload))
+    gathered = with_sibling(jnp.stack([column] + across(column)))
     result = call(
         partial(third_kernel, sizes, grid), 18,
         shape_of(MODES, BLOCK),
         near * 2 + mid_scratch(grid),
-        place_ref, *to_all(along_z(payload)), mid_code, coarse_code, near_gain, near_code, solved, *weights,
+        place_ref, *gathered, mid_code, coarse_code, near_gain, near_code, solved, *weights,
     )
     return result[None, None, None]
 

time: 141 us -> 135 us (0.957)
  waiting for transfers between devices: 16.1 us -> 11.4 us
    ppermute x14, waiting for transfers between devices: 15.5 us -> 10.9 us  [the longest x6 5.09 us: across(): return [lax.ppermute(column, ('gx', 'gy'), flip) for flip in flips]]
  transfers between devices with their start and end apart: 22 -> 22, of which waited for: 12 -> 8; matrix products, arithmetic and copies ran while one was open for 0% -> 0% of each run, Pallas kernels for 19% -> 20%
where the time goes in v1:
time: 135 us
  Pallas kernels  87.9 us (65%)
  starting transfers between devices  34.1 us (25%)
  waiting for transfers between devices  11.4 us (8%)
    pallas_call x9, Pallas kernels, call(): pl.pallas_call(kernel, out_shape=out_shape, in_specs=specs, out_specs=jax...  87.9 us
    ppermute x6, starting transfers between devices, across(): return [lax.ppermute(column, ('gx', 'gy'), flip) for flip in flips]  10.6 us
    ppermute x6, starting transfers between devices, along_z(): return [lax.ppermute(value, 'gz', turn) for turn in turns]  8.91 us
    ppermute x4, starting transfers between devices, wide_device(): lax.ppermute(value, 'gz', swap)  7.56 us
    ppermute x6, waiting for transfers between devices, across(): return [lax.ppermute(column, ('gx', 'gy'), flip) for flip in flips]  5.09 us
    ppermute x2, starting transfers between devices, wide_device(): along_y = [lax.ppermute(own, 'gy', swap) for swap in swaps['gy']]  3.92 us
    ppermute x2, waiting for transfers between devices, with_sibling(): return (here, lax.ppermute(here, 'gy', [(j, j ^ 1) for j in range(n_gy)]))  3.14 us
    ppermute x2, starting transfers between devices, wide_device(): others = (lax.ppermute(values, 'gx', swap), lax.ppermute(kinds, 'gx', swap))  3.05 us
  transfers between devices with their start and end apart: 22, of which 8 were waited for; matrix products, arithmetic and copies ran while one was open for 0% of the time, Pallas kernels for 20%

profile of v1, /device:TPU:0, one launch (start us, length us, event | category | flops | bytes accessed | tf_op | source)
XLA Modules:
  0.0 135.2 jit_solution(9862290041895462329)
XLA Ops:
  0.0 3.0 %collective-permute-start.1 = (s32[1,512]{1,0:T(1,128)}, s32[1,512]{1,0:T(1,128)S(1)}, u32[]{:S(2)}, u32[]{:S(2)}) collective-permute-start(s32[1,512]{1,0:T(1,128)} %bitcast.30), channel_id=1, source_target_pairs={{0,16},{16,0},{1,17},{17,1},{2,18},{18,2},{3,19},{19,3},{4,20},{20... | collective-permute-start | bytes 6152 | tf_op jit(solution)/shard_map/ppermute | solution.py:914
  3.0 0.1 collective-permute-start
  3.1 1.0 copy-done.3
  4.0 6.0 %shard_map.75.scaled = f32[4,64,64]{2,1,0:T(8,128)S(1)} custom-call(f32[4,64,64]{2,1,0:T(8,128)S(1)} %copy-done.3), custom_call_target="tpu_custom_call" | custom-call | flops 6000000000 | bytes 18000000 | tf_op jit(solution)/shard_map/pallas_call | solution.py:891
  10.0 0.0 copy-done.6
  10.0 0.1 pad_add_fusion.place_ref
  10.1 0.1 convert_element_type.20
  10.2 0.1 broadcast_in_dim.6
  10.3 0.1 reshape.29
  10.4 0.0 collective-permute-done.1.other_materials
  10.4 0.0 collective-permute-done.other
  10.4 0.0 copy-done.2
  10.4 0.0 copy-done.5
  10.4 0.6 shard_map.73.own
  11.0 0.0 copy-start.7
  11.0 0.7 collective-permute-start.3
  11.7 3.2 %collective-permute-start.2 = (f32[8,72,128]{2,1,0:T(8,128)S(1)}, f32[8,72,128]{2,1,0:T(8,128)S(1)}, u32[]{:S(2)}, u32[]{:S(2)}) collective-permute-start(f32[8,72,128]{2,1,0:T(8,128)S(1)} %shard_map.73.own), channel_id=1, source_target_pairs={{0,4},{4,0},{8,12},{12,8},{1,5},{5,1},{9,13},{13,9},{2,6},{6,2},{1... | collective-permute-start | bytes 884744 | tf_op jit(solution)/shard_map/ppermute | solution.py:923
  15.0 0.0 copy-done
  15.0 0.6 shard_map.76
  15.6 0.0 collective-permute-done.3.second.y1
  15.6 0.5 collective-permute-done.2.first.y0
  16.2 2.1 %shard_map.74 = (f32[3,72,128]{2,1,0:T(8,128)S(1)}, f32[3,72,128]{2,1,0:T(8,128)S(1)}, f32[16,72,128]{2,1,0:T(8,128)S(1)}, f32[16,72,128]{2,1,0:T(8,128)S(1)}) custom-call(s32[3]{0:T(128)S(1)} %pad_add_fusion.place_ref, f32[8,72,128]{2,1,0:T(8,128)S(1)} %shard_map.73.own, f32[8,72,128]{2,1,0:T(8,128)S(1)} %collective-permute-done.2.first.y0, ...), custom_call_target="tpu_custom_call" | custom-call | flops 1500000000 | bytes 4500000 | tf_op jit(solution)/shard_map/pallas_call | solution.py:891
  18.2 1.6 %collective-permute-start.6 = (f32[3,72,128]{2,1,0:T(8,128)S(1)}, f32[3,72,128]{2,1,0:T(8,128)S(1)}, u32[]{:S(2)}, u32[]{:S(2)}) collective-permute-start(f32[3,72,128]{2,1,0:T(8,128)S(1)} %get-tuple-element.31), channel_id=1, source_target_pairs={{0,1},{1,0},{2,3},{3,2},{4,5},{5,4},{6,7},{7,6},{8,9},{9,8},{10,11... | collective-permute-start | bytes 331784 | tf_op jit(solution)/shard_map/ppermute | solution.py:927
  19.9 0.7 collective-permute-start.7
  20.6 0.1 pad_maximum_fusion.5
  20.6 4.4 %collective-permute-start.4 = (f32[16,72,128]{2,1,0:T(8,128)S(1)}, f32[16,72,128]{2,1,0:T(8,128)S(1)}, u32[]{:S(2)}, u32[]{:S(2)}) collective-permute-start(f32[16,72,128]{2,1,0:T(8,128)S(1)} %get-tuple-element.28), channel_id=1, source_target_pairs={{0,1},{1,0},{2,3},{3,2},{4,5},{5,4},{6,7},{7,6},{8,9},{9,8},{10,11... | collective-permute-start | bytes 1769480 | tf_op jit(solution)/shard_map/ppermute | solution.py:928
  25.0 0.9 collective-permute-start.5
  25.9 0.0 collective-permute-done.6.z0
  25.9 0.0 collective-permute-done.7.z1
  25.9 8.0 %shard_map.77 = (f32[8,64,256]{2,1,0:T(8,128)S(1)}, f32[32,128]{1,0:T(8,128)S(1)}) custom-call(s32[3]{0:T(128)S(1)} %pad_add_fusion.place_ref, f32[8,72,128]{2,1,0:T(8,128)S(1)} %shard_map.73.own, f32[8,72,128]{2,1,0:T(8,128)S(1)} %collective-permute-done.2.first.y0, f32[8,72,128]{2,1,0:T(8,128)S(1)} %collective-permute-done.3.second.y1, ...), custom_call_target="tpu_custom_call" | custom-call | flops 7000000000 | bytes 21000000 | tf_op jit(solution)/shard_map/pallas_call | solution.py:891
  33.9 1.0 collective-permute-start.10
  34.9 2.3 %collective-permute-start.9 = (f32[40,128]{1,0:T(8,128)S(1)}, f32[40,128]{1,0:T(8,128)S(1)}, u32[]{:S(2)}, u32[]{:S(2)}) collective-permute-start(f32[40,128]{1,0:T(8,128)S(1)} %pad_maximum_fusion.4.payload), channel_id=1, source_target_pairs={{0,2},{1,3},{2,0},{3,1},{4,6},{5,7},{6,4},{7,5},{8,10},{9,11},{10,... | collective-permute-start | bytes 61448 | tf_op jit(solution)/shard_map/ppermute | solution.py:949
  37.3 1.1 collective-permute-start.8
  38.4 0.0 collective-permute-done.4.z0
  38.4 0.0 collective-permute-done.5.z1
  38.4 6.4 %shard_map.78 = (f32[16,64,512]{2,1,0:T(8,128)S(1)}, f32[16,1,512]{2,1,0:T(1,128)S(1)}, f32[16,64,256]{2,1,0:T(8,128)S(1)}, f32[16,1,256]{2,1,0:T(1,128)S(1)}, f32[40,128]{1,0:T(8,128)S(1)}) custom-call(s32[3]{0:T(128)S(1)} %pad_add_fusion.place_ref, f32[8,72,128]{2,1,0:T(8,128)S(1)} %shard_map.73.own, f32[8,72,128]{2,1,0:T(8,128)S(1)} %collective-permute-done.2.first.y0, ...), custom_call_target="tpu_custom_call" | custom-call | flops 6000000000 | bytes 18000000 | tf_op jit(solution)/shard_map/pallas_call | solution.py:891
  44.8 0.0 collective-permute-done.10
  44.8 0.0 collective-permute-done.9
  44.8 0.0 collective-permute-done.8
  44.9 6.4 %collective-permute-start.13 = (f32[4,40,128]{2,1,0:T(8,128)S(1)}, f32[4,40,128]{2,1,0:T(8,128)S(1)}, u32[]{:S(2)}, u32[]{:S(2)}) collective-permute-start(f32[4,40,128]{2,1,0:T(8,128)S(1)} %pad_maximum_fusion.2.column), channel_id=1, source_target_pairs={{0,24},{4,28},{8,16},{12,20},{16,8},{20,12},{24,0},{28,4},{1,25},{... | collective-permute-start | bytes 245768 | tf_op jit(solution)/shard_map/ppermute | solution.py:956
  51.2 0.0 collective-permute-start.12
  51.2 0.6 collective-permute-start.11
  51.9 6.4 %shard_map.79 = (f32[16,64,512]{2,1,0:T(8,128)S(1)}, f32[4,40,128]{2,1,0:T(8,128)S(1)}) custom-call(s32[3]{0:T(128)S(1)} %pad_add_fusion.place_ref, f32[16,64,512]{2,1,0:T(8,128)S(1)} %get-tuple-element.39.gain, f32[16,1,512]{2,1,0:T(1,128)S(1)} %get-tuple-element.40.code, bf16[256,1152]{1,0:T(8,128)(2,1)S(1)} %get-tuple-element.33.wg, ...), custom_call_target="tpu_custom_call" | custom-call | flops 7000000000 | bytes 21000000 | tf_op jit(solution)/shard_map/pallas_call | solution.py:891
  58.3 0.0 collective-permute-done.13
  58.3 0.0 collective-permute-done.12
  58.3 0.0 collective-permute-done.11
  58.4 0.1 collective-permute-start.14
  58.4 1.6 %collective-permute-done.14.sibling = f32[4,4,40,128]{3,2,1,0:T(8,128)S(1)} collective-permute-done((f32[4,4,40,128]{3,2,1,0:T(8,128)S(1)}, f32[4,4,40,128]{3,2,1,0:T(8,128)S(1)}, u32[]{:S(2)}, u32[]{:S(2)}) %collective-permute-start.14) | collective-permute-done | bytes 327712 | tf_op jit(solution)/shard_map/ppermute | solution.py:959
  60.0 37.4 %shard_map.80 = (f32[32,128]{1,0:T(8,128)S(1)}, f32[16,64,256]{2,1,0:T(8,128)S(1)}, f32[8,1,256]{2,1,0:T(1,128)S(1)}, f32[1,256]{1,0:T(1,128)S(1)}) custom-call(s32[3]{0:T(128)S(1)} %pad_add_fusion.place_ref, f32[4,4,40,128]{3,2,1,0:T(8,128)S(1)} %pad_maximum_fusion.here, f32[4,4,40,128]{3,2,1,0:T(8,128)S(1)} %collective-permute-done.14.sibling, ...), custom_call_target="tpu_custom_call" | custom-call | flops 36999999488 | bytes 111000000 | tf_op jit(solution)/shard_map/pallas_call | solution.py:891
  97.5 2.4 %collective-permute-start.17 = (f32[32,128]{1,0:T(8,128)S(1)}, f32[32,128]{1,0:T(8,128)S(1)}, u32[]{:S(2)}, u32[]{:S(2)}) collective-permute-start(f32[32,128]{1,0:T(8,128)S(1)} %get-tuple-element.47), channel_id=1, source_target_pairs={{0,3},{1,2},{2,1},{3,0},{4,7},{5,6},{6,5},{7,4},{8,11},{9,10},{10,... | collective-permute-start | bytes 49160 | tf_op jit(solution)/shard_map/ppermute | solution.py:949
  99.9 0.6 collective-permute-start.16
  100.5 1.4 %collective-permute-start.15 = (f32[32,128]{1,0:T(8,128)S(1)}, f32[32,128]{1,0:T(8,128)S(1)}, u32[]{:S(2)}, u32[]{:S(2)}) collective-permute-start(f32[32,128]{1,0:T(8,128)S(1)} %get-tuple-element.47), channel_id=1, source_target_pairs={{0,1},{1,0},{2,3},{3,2},{4,5},{5,4},{6,7},{7,6},{8,9},{9,8},{10,11... | collective-permute-start | bytes 49160 | tf_op jit(solution)/shard_map/ppermute | solution.py:949
  101.9 1.2 collective-permute-done.17
  103.1 1.5 %collective-permute-done.16 = f32[32,128]{1,0:T(8,128)S(1)} collective-permute-done((f32[32,128]{1,0:T(8,128)S(1)}, f32[32,128]{1,0:T(8,128)S(1)}, u32[]{:S(2)}, u32[]{:S(2)}) %collective-permute-start.16) | collective-permute-done | bytes 16416 | tf_op jit(solution)/shard_map/ppermute | solution.py:949
  104.5 0.0 collective-permute-done.15
  104.5 1.9 %collective-permute-start.19 = (f32[4,32,128]{2,1,0:T(8,128)S(1)}, f32[4,32,128]{2,1,0:T(8,128)S(1)}, u32[]{:S(2)}, u32[]{:S(2)}) collective-permute-start(f32[4,32,128]{2,1,0:T(8,128)S(1)} %get-tuple-element.52), channel_id=1, source_target_pairs={{0,8},{4,12},{8,0},{12,4},{16,24},{20,28},{24,16},{28,20},{1,9},{5... | collective-permute-start | bytes 196616 | tf_op jit(solution)/shard_map/ppermute | solution.py:956
  106.5 1.5 %collective-permute-start.18 = (f32[4,32,128]{2,1,0:T(8,128)S(1)}, f32[4,32,128]{2,1,0:T(8,128)S(1)}, u32[]{:S(2)}, u32[]{:S(2)}) collective-permute-start(f32[4,32,128]{2,1,0:T(8,128)S(1)} %get-tuple-element.52), channel_id=1, source_target_pairs={{0,16},{4,20},{8,24},{12,28},{16,0},{20,4},{24,8},{28,12},{1,17},{... | collective-permute-start | bytes 196616 | tf_op jit(solution)/shard_map/ppermute | solution.py:956
  108.0 0.1 collective-permute-start.20
  108.1 1.0 collective-permute-done.19
  109.1 2.0 %collective-permute-done.18 = f32[4,32,128]{2,1,0:T(8,128)S(1)} collective-permute-done((f32[4,32,128]{2,1,0:T(8,128)S(1)}, f32[4,32,128]{2,1,0:T(8,128)S(1)}, u32[]{:S(2)}, u32[]{:S(2)}) %collective-permute-start.18) | collective-permute-done | bytes 65568 | tf_op jit(solution)/shard_map/ppermute | solution.py:956
  111.1 2.1 %collective-permute-done.20 = f32[4,32,128]{2,1,0:T(8,128)S(1)} collective-permute-done((f32[4,32,128]{2,1,0:T(8,128)S(1)}, f32[4,32,128]{2,1,0:T(8,128)S(1)}, u32[]{:S(2)}, u32[]{:S(2)}) %collective-permute-start.20) | collective-permute-done | bytes 65568 | tf_op jit(solution)/shard_map/ppermute | solution.py:956
  113.2 0.1 collective-permute-start.21
  113.3 1.5 %collective-permute-done.21.sibling = f32[4,4,32,128]{3,2,1,0:T(8,128)S(1)} collective-permute-done((f32[4,4,32,128]{3,2,1,0:T(8,128)S(1)}, f32[4,4,32,128]{3,2,1,0:T(8,128)S(1)}, u32[]{:S(2)}, u32[]{:S(2)}) %collective-permute-start.21) | collective-permute-done | bytes 262176 | tf_op jit(solution)/shard_map/ppermute | solution.py:959
  114.8 20.4 %shard_map.81 = f32[64,512]{1,0:T(8,128)} custom-call(s32[3]{0:T(128)S(1)} %pad_add_fusion.place_ref, f32[4,4,32,128]{3,2,1,0:T(8,128)S(1)} %pad_maximum_fusion.1.here, f32[4,4,32,128]{3,2,1,0:T(8,128)S(1)} %collective-permute-done.21.sibling, f32[8,1,256]{2,1,0:T(1,128)S(1)} %get-tuple-element.48.mid_code, f32[1,256]{1,0:T(1,128)S(1)} %get-tuple-element.49.coarse_code, ...), custom_call_target="tpu_custom_call" | custom-call | flops 17999998976 | bytes 54000000 | tf_op jit(solution)/shard_map/pallas_call | solution.py:891
  (18 shorter events, 0.1 us)
Async XLA Ops:
  0.0 10.4 %collective-permute-start.1 = (s32[1,512]{1,0:T(1,128)}, s32[1,512]{1,0:T(1,128)S(1)}, u32[]{:S(2)}, u32[]{:S(2)}) collective-permute-start(s32[1,512]{1,0:T(1,128)} %bitcast.30), channel_id=1, source_target_pairs={{0,16},{16,0},{1,17},{17,1},{2,18},{18,2},{3,19},{19,3},{4,20},{20... | collective-permute-start | bytes 6152 | tf_op jit(solution)/shard_map/ppermute | solution.py:914
  3.0 7.5 %copy-start.2 = (f32[1,1,1,64,512]{4,3,2,1,0:T(8,128)S(1)}, f32[1,1,1,64,512]{4,3,2,1,0:T(8,128)}, u32[]{:S(2)}) copy-start(f32[1,1,1,64,512]{4,3,2,1,0:T(8,128)} %param.7) | copy-start | bytes 393220
  3.0 12.0 %copy-start = (f32[6,4,64,64]{3,2,1,0:T(8,128)S(1)}, f32[6,4,64,64]{3,2,1,0:T(8,128)}, u32[]{:S(2)}) copy-start(f32[6,4,64,64]{3,2,1,0:T(8,128)} %face.1) | copy-start | bytes 1179652
  3.0 12.0 %copy-start.1 = (f32[8,64,64]{2,1,0:T(8,128)S(1)}, f32[8,64,64]{2,1,0:T(8,128)}, u32[]{:S(2)}) copy-start(f32[8,64,64]{2,1,0:T(8,128)} %prolong.1) | copy-start | bytes 393220
  3.0 7.4 %collective-permute-start = (f32[64,512]{1,0:T(8,128)}, f32[64,512]{1,0:T(8,128)S(1)}, u32[]{:S(2)}, u32[]{:S(2)}) collective-permute-start(f32[64,512]{1,0:T(8,128)} %bitcast.28), channel_id=1, source_target_pairs={{0,16},{16,0},{1,17},{17,1},{2,18},{18,2},{3,19},{19,3},{4,20},{20... | collective-permute-start | bytes 393224 | tf_op jit(solution)/shard_map/ppermute | solution.py:914
  3.1 1.0 copy-start.3
  4.0 6.0 %copy-start.6 = (s32[1,1,1,8]{3,2,1,0:T(1,128)S(1)}, s32[1,1,1,8]{3,2,1,0:T(1,128)}, u32[]{:S(2)}) copy-start(s32[1,1,1,8]{3,2,1,0:T(1,128)} %param.13) | copy-start | bytes 100
  4.0 6.4 %copy-start.5 = (s32[1,1,1,512]{3,2,1,0:T(1,128)S(1)}, s32[1,1,1,512]{3,2,1,0:T(1,128)}, u32[]{:S(2)}) copy-start(s32[1,1,1,512]{3,2,1,0:T(1,128)} %param.11) | copy-start | bytes 6148
  4.0 10.9 %copy-start.4 = (f32[4,64,64]{2,1,0:T(8,128)S(1)}, f32[4,64,64]{2,1,0:T(8,128)}, u32[]{:S(2)}) copy-start(f32[4,64,64]{2,1,0:T(8,128)} %diag.3) | copy-start | bytes 196612
  11.0 4.6 %copy-start.7 = (s32[1,1,1,64]{3,2,1,0:T(1,128)S(1)}, s32[1,1,1,64]{3,2,1,0:T(1,128)}, u32[]{:S(2)}) copy-start(s32[1,1,1,64]{3,2,1,0:T(1,128)} %param.12) | copy-start | bytes 772
  11.0 4.6 %collective-permute-start.3 = (f32[8,72,128]{2,1,0:T(8,128)S(1)}, f32[8,72,128]{2,1,0:T(8,128)S(1)}, u32[]{:S(2)}, u32[]{:S(2)}) collective-permute-start(f32[8,72,128]{2,1,0:T(8,128)S(1)} %shard_map.73.own), channel_id=1, source_target_pairs={{0,0},{4,8},{8,4},{12,12},{1,1},{5,9},{9,5},{13,13},{2,2},{6,10},{... | collective-permute-start | bytes 884744 | tf_op jit(solution)/shard_map/ppermute | solution.py:923
  11.7 4.5 %collective-permute-start.2 = (f32[8,72,128]{2,1,0:T(8,128)S(1)}, f32[8,72,128]{2,1,0:T(8,128)S(1)}, u32[]{:S(2)}, u32[]{:S(2)}) collective-permute-start(f32[8,72,128]{2,1,0:T(8,128)S(1)} %shard_map.73.own), channel_id=1, source_target_pairs={{0,4},{4,0},{8,12},{12,8},{1,5},{5,1},{9,13},{13,9},{2,6},{6,2},{1... | collective-permute-start | bytes 884744 | tf_op jit(solution)/shard_map/ppermute | solution.py:923
  18.2 7.7 %collective-permute-start.6 = (f32[3,72,128]{2,1,0:T(8,128)S(1)}, f32[3,72,128]{2,1,0:T(8,128)S(1)}, u32[]{:S(2)}, u32[]{:S(2)}) collective-permute-start(f32[3,72,128]{2,1,0:T(8,128)S(1)} %get-tuple-element.31), channel_id=1, source_target_pairs={{0,1},{1,0},{2,3},{3,2},{4,5},{5,4},{6,7},{7,6},{8,9},{9,8},{10,11... | collective-permute-start | bytes 331784 | tf_op jit(solution)/shard_map/ppermute | solution.py:927
  19.9 6.0 %collective-permute-start.7 = (f32[3,72,128]{2,1,0:T(8,128)S(1)}, f32[3,72,128]{2,1,0:T(8,128)S(1)}, u32[]{:S(2)}, u32[]{:S(2)}) collective-permute-start(f32[3,72,128]{2,1,0:T(8,128)S(1)} %get-tuple-element.32), channel_id=1, source_target_pairs={{0,0},{1,2},{2,1},{3,3},{4,4},{5,6},{6,5},{7,7},{8,8},{9,10},{10,9... | collective-permute-start | bytes 331784 | tf_op jit(solution)/shard_map/ppermute | solution.py:927
  20.6 17.8 %collective-permute-start.4 = (f32[16,72,128]{2,1,0:T(8,128)S(1)}, f32[16,72,128]{2,1,0:T(8,128)S(1)}, u32[]{:S(2)}, u32[]{:S(2)}) collective-permute-start(f32[16,72,128]{2,1,0:T(8,128)S(1)} %get-tuple-element.28), channel_id=1, source_target_pairs={{0,1},{1,0},{2,3},{3,2},{4,5},{5,4},{6,7},{7,6},{8,9},{9,8},{10,11... | collective-permute-start | bytes 1769480 | tf_op jit(solution)/shard_map/ppermute | solution.py:928
  25.0 13.4 %collective-permute-start.5 = (f32[16,72,128]{2,1,0:T(8,128)S(1)}, f32[16,72,128]{2,1,0:T(8,128)S(1)}, u32[]{:S(2)}, u32[]{:S(2)}) collective-permute-start(f32[16,72,128]{2,1,0:T(8,128)S(1)} %get-tuple-element.29), channel_id=1, source_target_pairs={{0,0},{1,2},{2,1},{3,3},{4,4},{5,6},{6,5},{7,7},{8,8},{9,10},{10,9... | collective-permute-start | bytes 1769480 | tf_op jit(solution)/shard_map/ppermute | solution.py:928
  33.9 10.9 %collective-permute-start.10 = (f32[40,128]{1,0:T(8,128)S(1)}, f32[40,128]{1,0:T(8,128)S(1)}, u32[]{:S(2)}, u32[]{:S(2)}) collective-permute-start(f32[40,128]{1,0:T(8,128)S(1)} %pad_maximum_fusion.4.payload), channel_id=1, source_target_pairs={{0,3},{1,2},{2,1},{3,0},{4,7},{5,6},{6,5},{7,4},{8,11},{9,10},{10,... | collective-permute-start | bytes 61448 | tf_op jit(solution)/shard_map/ppermute | solution.py:949
  34.9 9.9 %collective-permute-start.9 = (f32[40,128]{1,0:T(8,128)S(1)}, f32[40,128]{1,0:T(8,128)S(1)}, u32[]{:S(2)}, u32[]{:S(2)}) collective-permute-start(f32[40,128]{1,0:T(8,128)S(1)} %pad_maximum_fusion.4.payload), channel_id=1, source_target_pairs={{0,2},{1,3},{2,0},{3,1},{4,6},{5,7},{6,4},{7,5},{8,10},{9,11},{10,... | collective-permute-start | bytes 61448 | tf_op jit(solution)/shard_map/ppermute | solution.py:949
  37.3 7.6 %collective-permute-start.8 = (f32[40,128]{1,0:T(8,128)S(1)}, f32[40,128]{1,0:T(8,128)S(1)}, u32[]{:S(2)}, u32[]{:S(2)}) collective-permute-start(f32[40,128]{1,0:T(8,128)S(1)} %pad_maximum_fusion.4.payload), channel_id=1, source_target_pairs={{0,1},{1,0},{2,3},{3,2},{4,5},{5,4},{6,7},{7,6},{8,9},{9,8},{10,11... | collective-permute-start | bytes 61448 | tf_op jit(solution)/shard_map/ppermute | solution.py:949
  44.9 13.4 %collective-permute-start.13 = (f32[4,40,128]{2,1,0:T(8,128)S(1)}, f32[4,40,128]{2,1,0:T(8,128)S(1)}, u32[]{:S(2)}, u32[]{:S(2)}) collective-permute-start(f32[4,40,128]{2,1,0:T(8,128)S(1)} %pad_maximum_fusion.2.column), channel_id=1, source_target_pairs={{0,24},{4,28},{8,16},{12,20},{16,8},{20,12},{24,0},{28,4},{1,25},{... | collective-permute-start | bytes 245768 | tf_op jit(solution)/shard_map/ppermute | solution.py:956
  51.2 7.1 %collective-permute-start.12 = (f32[4,40,128]{2,1,0:T(8,128)S(1)}, f32[4,40,128]{2,1,0:T(8,128)S(1)}, u32[]{:S(2)}, u32[]{:S(2)}) collective-permute-start(f32[4,40,128]{2,1,0:T(8,128)S(1)} %pad_maximum_fusion.2.column), channel_id=1, source_target_pairs={{0,8},{4,12},{8,0},{12,4},{16,24},{20,28},{24,16},{28,20},{1,9},{5... | collective-permute-start | bytes 245768 | tf_op jit(solution)/shard_map/ppermute | solution.py:956
  51.2 7.1 %collective-permute-start.11 = (f32[4,40,128]{2,1,0:T(8,128)S(1)}, f32[4,40,128]{2,1,0:T(8,128)S(1)}, u32[]{:S(2)}, u32[]{:S(2)}) collective-permute-start(f32[4,40,128]{2,1,0:T(8,128)S(1)} %pad_maximum_fusion.2.column), channel_id=1, source_target_pairs={{0,16},{4,20},{8,24},{12,28},{16,0},{20,4},{24,8},{28,12},{1,17},{... | collective-permute-start | bytes 245768 | tf_op jit(solution)/shard_map/ppermute | solution.py:956
  58.4 1.7 %collective-permute-start.14 = (f32[4,4,40,128]{3,2,1,0:T(8,128)S(1)}, f32[4,4,40,128]{3,2,1,0:T(8,128)S(1)}, u32[]{:S(2)}, u32[]{:S(2)}) collective-permute-start(f32[4,4,40,128]{3,2,1,0:T(8,128)S(1)} %pad_maximum_fusion.here), channel_id=1, source_target_pairs={{0,4},{4,0},{8,12},{12,8},{1,5},{5,1},{9,13},{13,9},{2,6},{6,2},{1... | collective-permute-start | bytes 983048 | tf_op jit(solution)/shard_map/ppermute | solution.py:959
  97.5 5.6 %collective-permute-start.17 = (f32[32,128]{1,0:T(8,128)S(1)}, f32[32,128]{1,0:T(8,128)S(1)}, u32[]{:S(2)}, u32[]{:S(2)}) collective-permute-start(f32[32,128]{1,0:T(8,128)S(1)} %get-tuple-element.47), channel_id=1, source_target_pairs={{0,3},{1,2},{2,1},{3,0},{4,7},{5,6},{6,5},{7,4},{8,11},{9,10},{10,... | collective-permute-start | bytes 49160 | tf_op jit(solution)/shard_map/ppermute | solution.py:949
  99.9 4.6 %collective-permute-start.16 = (f32[32,128]{1,0:T(8,128)S(1)}, f32[32,128]{1,0:T(8,128)S(1)}, u32[]{:S(2)}, u32[]{:S(2)}) collective-permute-start(f32[32,128]{1,0:T(8,128)S(1)} %get-tuple-element.47), channel_id=1, source_target_pairs={{0,2},{1,3},{2,0},{3,1},{4,6},{5,7},{6,4},{7,5},{8,10},{9,11},{10,... | collective-permute-start | bytes 49160 | tf_op jit(solution)/shard_map/ppermute | solution.py:949
  100.5 4.0 %collective-permute-start.15 = (f32[32,128]{1,0:T(8,128)S(1)}, f32[32,128]{1,0:T(8,128)S(1)}, u32[]{:S(2)}, u32[]{:S(2)}) collective-permute-start(f32[32,128]{1,0:T(8,128)S(1)} %get-tuple-element.47), channel_id=1, source_target_pairs={{0,1},{1,0},{2,3},{3,2},{4,5},{5,4},{6,7},{7,6},{8,9},{9,8},{10,11... | collective-permute-start | bytes 49160 | tf_op jit(solution)/shard_map/ppermute | solution.py:949
  104.5 4.6 %collective-permute-start.19 = (f32[4,32,128]{2,1,0:T(8,128)S(1)}, f32[4,32,128]{2,1,0:T(8,128)S(1)}, u32[]{:S(2)}, u32[]{:S(2)}) collective-permute-start(f32[4,32,128]{2,1,0:T(8,128)S(1)} %get-tuple-element.52), channel_id=1, source_target_pairs={{0,8},{4,12},{8,0},{12,4},{16,24},{20,28},{24,16},{28,20},{1,9},{5... | collective-permute-start | bytes 196616 | tf_op jit(solution)/shard_map/ppermute | solution.py:956
  106.5 4.6 %collective-permute-start.18 = (f32[4,32,128]{2,1,0:T(8,128)S(1)}, f32[4,32,128]{2,1,0:T(8,128)S(1)}, u32[]{:S(2)}, u32[]{:S(2)}) collective-permute-start(f32[4,32,128]{2,1,0:T(8,128)S(1)} %get-tuple-element.52), channel_id=1, source_target_pairs={{0,16},{4,20},{8,24},{12,28},{16,0},{20,4},{24,8},{28,12},{1,17},{... | collective-permute-start | bytes 196616 | tf_op jit(solution)/shard_map/ppermute | solution.py:956
  108.0 5.2 %collective-permute-start.20 = (f32[4,32,128]{2,1,0:T(8,128)S(1)}, f32[4,32,128]{2,1,0:T(8,128)S(1)}, u32[]{:S(2)}, u32[]{:S(2)}) collective-permute-start(f32[4,32,128]{2,1,0:T(8,128)S(1)} %get-tuple-element.52), channel_id=1, source_target_pairs={{0,24},{4,28},{8,16},{12,20},{16,8},{20,12},{24,0},{28,4},{1,25},{... | collective-permute-start | bytes 196616 | tf_op jit(solution)/shard_map/ppermute | solution.py:956
  113.2 1.6 %collective-permute-start.21 = (f32[4,4,32,128]{3,2,1,0:T(8,128)S(1)}, f32[4,4,32,128]{3,2,1,0:T(8,128)S(1)}, u32[]{:S(2)}, u32[]{:S(2)}) collective-permute-start(f32[4,4,32,128]{3,2,1,0:T(8,128)S(1)} %pad_maximum_fusion.1.here), channel_id=1, source_target_pairs={{0,4},{4,0},{8,12},{12,8},{1,5},{5,1},{9,13},{13,9},{2,6},{6,2},{1... | collective-permute-start | bytes 786440 | tf_op jit(solution)/shard_map/ppermute | solution.py:959

commit v2 on v1

--- a/solution.py
+++ b/solution.py
@@ -235,17 +235,17 @@
     return jnp.concatenate([high, high, low], axis=1)
 
 
-def inverse_kernel(diag, scaled):
+def inverse_kernel(pivots, scale, diag, *refs):
     a = diag[...]
     row_id = iota((1, MODES, 1), 1)
     lane_id = iota((1, 1, MODES), 2)
-    for k in range(MODES):
+    for k in pivots:
         pivot = 1.0 / a[:, k:k + 1, k:k + 1]
         on_row, on_lane = row_id == k, lane_id == k
         row = jnp.where(on_lane, pivot, a[:, k:k + 1, :] * pivot)
         column = a[:, :, k:k + 1]
         a = jnp.where(on_row, row, jnp.where(on_lane, 0.0, a) - column * row)
-    scaled[...] = relax_weight * a
+    refs[-1][...] = scale * a
 
 
 def weights_kernel(scaled, diag, face, prolong, wg, wa, wd, wi, wr, wp):
@@ -264,8 +264,9 @@
     wp[...] = thirds(jnp.concatenate([prolong[c] for c in range(8)], axis=0))
 
 
-def invert(diag_blocks):
-    return call(inverse_kernel, 6, shape_of(*diag_blocks.shape), [], diag_blocks)
+def invert_part(pivots, scale, blocks, *after):
+    kernel = partial(inverse_kernel, pivots, scale)
+    return call(kernel, 3, shape_of(*blocks.shape), [], blocks, *after, unread=len(after))
 
 
 def make_weights(scaled, diag_blocks, face_blocks, prolong):
@@ -277,6 +278,7 @@
 
 
 SHALLOW = SWEEPS
+FIRST_PIVOTS = MODES // 2
 PAIRS = CX
 SLOT = CY * CZ
 
@@ -309,7 +311,7 @@
     return jnp.where(inside, start + y + halo - depth, -(1 << 20))
 
 
-def prepare_kernel(place_ref, values, other, materials, other_materials, out):
+def prepare_kernel(place_ref, values, other, materials, other_materials, half_way, out):
     mine = place_ref[0]
     for half, (block, kinds) in enumerate(((values, materials), (other, other_materials))):
         first = (mine ^ half) * (BLOCK // TILE)
@@ -325,7 +327,7 @@
     return jnp.where(place == 1, 1, jnp.where(place // 2 == odd, 2, 0))
 
 
-def pack_kernel(place_ref, own, first, second, thin_first, thin_second, thick_first, thick_second):
+def pack_kernel(place_ref, own, first, second, scaled, thin_first, thin_second, thick_first, thick_second):
     column = iota((1, 4 * TILE), 1)
     lane, kind = column % TILE, column // TILE
     row = iota((3 * TILE, 4 * TILE), 0)
@@ -884,9 +886,10 @@
         result[:, pair * TILE:(pair + 1) * TILE] = total
 
 
-def call(kernel, cost_us, out_shape, scratch, *args, limit=16):
+def call(kernel, cost_us, out_shape, scratch, *args, limit=16, unread=0):
     vmem, smem = pl.BlockSpec(memory_space=pltpu.VMEM), pl.BlockSpec(memory_space=pltpu.SMEM)
-    specs = [smem if a.dtype == jnp.int32 and a.ndim == 1 else vmem for a in args]
+    specs = [smem if a.dtype == jnp.int32 and a.ndim == 1 else vmem for a in args[:len(args) - unread]]
+    specs += [pl.BlockSpec(memory_space=pl.ANY)] * unread
     cost = pl.CostEstimate(flops=int(cost_us * 1e9), bytes_accessed=int(cost_us * 3e6), transcendentals=0)
     return pl.pallas_call(
         kernel,
@@ -912,18 +915,20 @@
     values, kinds = right_side.reshape(MODES, BLOCK), mats_fine.reshape(1, BLOCK)
     swap = [(0, 1), (1, 0)]
     others = lax.ppermute(values, "gx", swap), lax.ppermute(kinds, "gx", swap)
-    scaled = invert(diag_blocks)
+    half_way = invert_part(range(FIRST_PIVOTS), 1.0, diag_blocks)
     own = call(
-        prepare_kernel, 0.5, shape_of(2 * tiles, ROWS, TILE), [], place_ref, values, others[0], kinds, others[1]
+        prepare_kernel, 0.5, shape_of(2 * tiles, ROWS, TILE), [],
+        place_ref, values, others[0], kinds, others[1], half_way, unread=1,
     )
     swaps = {}
     for axis, n in zip(axes, sizes):
         inner = [pair for i in range(1, n - 1, 2) for pair in ((i, i + 1), (i + 1, i))]
         swaps[axis] = [(i, i ^ 1) for i in range(n)], [(0, 0)] + inner + [(n - 1, n - 1)]
     along_y = [lax.ppermute(own, "gy", swap) for swap in swaps["gy"]]
+    scaled = invert_part(range(FIRST_PIVOTS, MODES), relax_weight, half_way, own)
     weights = make_weights(scaled, diag_blocks, face_blocks, prolong)
     thin, thick = shape_of(SHALLOW_TILES, ROWS, TILE), shape_of(2 * PAIRS, ROWS, TILE)
-    send = call(pack_kernel, 1.5, [thin, thin, thick, thick], [], place_ref, own, *along_y)
+    send = call(pack_kernel, 1.5, [thin, thin, thick, thick], [], place_ref, own, *along_y, scaled, unread=1)
     shallow = [lax.ppermute(value, "gz", swap) for value, swap in zip(send[:2], swaps["gz"])]
     deep = [lax.ppermute(value, "gz", swap) for value, swap in zip(send[2:], swaps["gz"])]
 

time: 135 us -> 133 us (0.985)
  starting transfers between devices: 34.1 us -> 32.4 us
    ppermute x6, starting transfers between devices: 10.6 us -> 7.13 us  [across(): return [lax.ppermute(column, ('gx', 'gy'), flip) for flip in flips]]
    ppermute x6, waiting for transfers between devices: 5.09 us -> 2.57 us  [across(): return [lax.ppermute(column, ('gx', 'gy'), flip) for flip in flips]]
    ppermute x6, starting transfers between devices: 8.91 us -> 10.9 us  [along_z(): return [lax.ppermute(value, 'gz', turn) for turn in turns]]
    pallas_call x9 -> x10, Pallas kernels: 87.9 us -> 87.9 us  [call(): pl.pallas_call(kernel, out_shape=out_shape, in_specs=specs, out_specs=jax...]
  transfers between devices with their start and end apart: 22 -> 22, of which waited for: 8 -> 9; matrix products, arithmetic and copies ran while one was open for 0% -> 0% of each run, Pallas kernels for 20% -> 21%
where the time goes in v2:
time: 133 us
  Pallas kernels  87.9 us (66%)
  starting transfers between devices  32.4 us (24%)
  waiting for transfers between devices  11.1 us (8%)
    pallas_call x10, Pallas kernels, call(): pl.pallas_call(kernel, out_shape=out_shape, in_specs=specs, out_specs=jax...  87.9 us
    ppermute x6, starting transfers between devices, along_z(): return [lax.ppermute(value, 'gz', turn) for turn in turns]  10.9 us
    ppermute x4, starting transfers between devices, wide_device(): lax.ppermute(value, 'gz', swap)  7.62 us
    ppermute x6, starting transfers between devices, across(): return [lax.ppermute(column, ('gx', 'gy'), flip) for flip in flips]  7.13 us
    ppermute x6, waiting for transfers between devices, along_z(): return [lax.ppermute(value, 'gz', turn) for turn in turns]  3.75 us
    ppermute x2, starting transfers between devices, wide_device(): along_y = [lax.ppermute(own, 'gy', swap) for swap in swaps['gy']]  3.58 us
    ppermute x2, waiting for transfers between devices, with_sibling(): return (here, lax.ppermute(here, 'gy', [(j, j ^ 1) for j in range(n_gy)]))  3.14 us
    ppermute x2, starting transfers between devices, wide_device(): others = (lax.ppermute(values, 'gx', swap), lax.ppermute(kinds, 'gx', swap))  3.03 us
  transfers between devices with their start and end apart: 22, of which 9 were waited for; matrix products, arithmetic and copies ran while one was open for 0% of the time, Pallas kernels for 21%

profile of v2, /device:TPU:0, one launch (start us, length us, event | category | flops | bytes accessed | tf_op | source)
XLA Modules:
  0.0 133.2 jit_solution(4961195659750612999)
XLA Ops:
  0.0 3.0 %collective-permute-start.1 = (s32[1,512]{1,0:T(1,128)}, s32[1,512]{1,0:T(1,128)S(1)}, u32[]{:S(2)}, u32[]{:S(2)}) collective-permute-start(s32[1,512]{1,0:T(1,128)} %bitcast.30), channel_id=1, source_target_pairs={{0,16},{16,0},{1,17},{17,1},{2,18},{18,2},{3,19},{19,3},{4,20},{20... | collective-permute-start | bytes 6152 | tf_op jit(solution)/shard_map/ppermute | solution.py:917
  3.0 0.1 collective-permute-start
  3.0 0.9 copy-done.3
  3.9 2.9 %shard_map.73.half_way.diag = f32[4,64,64]{2,1,0:T(8,128)S(1)} custom-call(f32[4,64,64]{2,1,0:T(8,128)S(1)} %copy-done.3), custom_call_target="tpu_custom_call" | custom-call | flops 3000000000 | bytes 9000000 | tf_op jit(solution)/shard_map/pallas_call | solution.py:894
  6.9 0.0 copy-done.6
  6.9 0.1 pad_add_fusion.place_ref
  7.0 0.0 collective-permute-done.1.other_materials
  7.0 1.2 collective-permute-done.other
  8.2 0.6 shard_map.74.refs_0_.own
  8.7 0.7 collective-permute-start.3
  9.4 2.9 %collective-permute-start.2 = (f32[8,72,128]{2,1,0:T(8,128)S(1)}, f32[8,72,128]{2,1,0:T(8,128)S(1)}, u32[]{:S(2)}, u32[]{:S(2)}) collective-permute-start(f32[8,72,128]{2,1,0:T(8,128)S(1)} %shard_map.74.refs_0_.own), channel_id=1, source_target_pairs={{0,4},{4,0},{8,12},{12,8},{1,5},{5,1},{9,13},{13,9},{2,6},{6,2},{1... | collective-permute-start | bytes 884744 | tf_op jit(solution)/shard_map/ppermute | solution.py:927
  12.3 0.1 convert_element_type.20
  12.4 0.1 broadcast_in_dim.6
  12.5 0.1 reshape.29
  12.6 3.0 %shard_map.75.scaled = f32[4,64,64]{2,1,0:T(8,128)S(1)} custom-call(f32[4,64,64]{2,1,0:T(8,128)S(1)} %shard_map.73.half_way.diag, f32[8,72,128]{2,1,0:T(8,128)S(1)} %shard_map.74.refs_0_.own), custom_call_target="tpu_custom_call" | custom-call | flops 3000000000 | bytes 9000000 | tf_op jit(solution)/shard_map/pallas_call | solution.py:894
  15.7 0.0 copy-start
  15.7 0.0 copy-start.1
  15.7 0.0 copy-start.4
  15.7 0.0 collective-permute-done.3.second.y1
  15.7 0.0 collective-permute-done.2.first.y0
  15.7 2.1 %shard_map.76 = (f32[3,72,128]{2,1,0:T(8,128)S(1)}, f32[3,72,128]{2,1,0:T(8,128)S(1)}, f32[16,72,128]{2,1,0:T(8,128)S(1)}, f32[16,72,128]{2,1,0:T(8,128)S(1)}) custom-call(s32[3]{0:T(128)S(1)} %pad_add_fusion.place_ref, f32[8,72,128]{2,1,0:T(8,128)S(1)} %shard_map.74.refs_0_.own, f32[8,72,128]{2,1,0:T(8,128)S(1)} %collective-permute-done.2.first.y0, ...), custom_call_target="tpu_custom_call" | custom-call | flops 1500000000 | bytes 4500000 | tf_op jit(solution)/shard_map/pallas_call | solution.py:894
  17.8 1.6 %collective-permute-start.6 = (f32[3,72,128]{2,1,0:T(8,128)S(1)}, f32[3,72,128]{2,1,0:T(8,128)S(1)}, u32[]{:S(2)}, u32[]{:S(2)}) collective-permute-start(f32[3,72,128]{2,1,0:T(8,128)S(1)} %get-tuple-element.31), channel_id=1, source_target_pairs={{0,1},{1,0},{2,3},{3,2},{4,5},{5,4},{6,7},{7,6},{8,9},{9,8},{10,11... | collective-permute-start | bytes 331784 | tf_op jit(solution)/shard_map/ppermute | solution.py:932
  19.5 0.7 collective-permute-start.7
  20.1 0.1 pad_maximum_fusion.5
  20.2 0.6 shard_map.77
  20.8 4.5 %collective-permute-start.4 = (f32[16,72,128]{2,1,0:T(8,128)S(1)}, f32[16,72,128]{2,1,0:T(8,128)S(1)}, u32[]{:S(2)}, u32[]{:S(2)}) collective-permute-start(f32[16,72,128]{2,1,0:T(8,128)S(1)} %get-tuple-element.28), channel_id=1, source_target_pairs={{0,1},{1,0},{2,3},{3,2},{4,5},{5,4},{6,7},{7,6},{8,9},{9,8},{10,11... | collective-permute-start | bytes 1769480 | tf_op jit(solution)/shard_map/ppermute | solution.py:933
  25.3 0.9 collective-permute-start.5
  26.1 0.0 collective-permute-done.6.z0
  26.1 0.0 collective-permute-done.7.z1
  26.2 8.0 %shard_map.78 = (f32[8,64,256]{2,1,0:T(8,128)S(1)}, f32[32,128]{1,0:T(8,128)S(1)}) custom-call(s32[3]{0:T(128)S(1)} %pad_add_fusion.place_ref, f32[8,72,128]{2,1,0:T(8,128)S(1)} %shard_map.74.refs_0_.own, f32[8,72,128]{2,1,0:T(8,128)S(1)} %collective-permute-done.2.first.y0, f32[8,72,128]{2,1,0:T(8,128)S(1)} %collective-permute-done.3.second.y1, ...), custom_call_target="tpu_custom_call" | custom-call | flops 7000000000 | bytes 21000000 | tf_op jit(solution)/shard_map/pallas_call | solution.py:894
  34.2 1.3 collective-permute-start.10
  35.4 2.5 %collective-permute-start.9 = (f32[40,128]{1,0:T(8,128)S(1)}, f32[40,128]{1,0:T(8,128)S(1)}, u32[]{:S(2)}, u32[]{:S(2)}) collective-permute-start(f32[40,128]{1,0:T(8,128)S(1)} %pad_maximum_fusion.4.payload), channel_id=1, source_target_pairs={{0,2},{1,3},{2,0},{3,1},{4,6},{5,7},{6,4},{7,5},{8,10},{9,11},{10,... | collective-permute-start | bytes 61448 | tf_op jit(solution)/shard_map/ppermute | solution.py:954
  37.9 0.7 collective-permute-start.8
  38.6 0.5 collective-permute-done.4.z0
  39.1 0.0 collective-permute-done.5.z1
  39.1 6.4 %shard_map.79 = (f32[16,64,512]{2,1,0:T(8,128)S(1)}, f32[16,1,512]{2,1,0:T(1,128)S(1)}, f32[16,64,256]{2,1,0:T(8,128)S(1)}, f32[16,1,256]{2,1,0:T(1,128)S(1)}, f32[40,128]{1,0:T(8,128)S(1)}) custom-call(s32[3]{0:T(128)S(1)} %pad_add_fusion.place_ref, f32[8,72,128]{2,1,0:T(8,128)S(1)} %shard_map.74.refs_0_.own, ...), custom_call_target="tpu_custom_call" | custom-call | flops 6000000000 | bytes 18000000 | tf_op jit(solution)/shard_map/pallas_call | solution.py:894
  45.5 0.0 collective-permute-done.10
  45.5 0.0 collective-permute-done.9
  45.6 0.0 collective-permute-done.8
  45.6 2.4 %collective-permute-start.13 = (f32[4,40,128]{2,1,0:T(8,128)S(1)}, f32[4,40,128]{2,1,0:T(8,128)S(1)}, u32[]{:S(2)}, u32[]{:S(2)}) collective-permute-start(f32[4,40,128]{2,1,0:T(8,128)S(1)} %pad_maximum_fusion.2.column), channel_id=1, source_target_pairs={{0,24},{4,28},{8,16},{12,20},{16,8},{20,12},{24,0},{28,4},{1,25},{... | collective-permute-start | bytes 245768 | tf_op jit(solution)/shard_map/ppermute | solution.py:961
  48.0 0.0 collective-permute-start.12
  48.0 1.2 collective-permute-start.11
  49.2 6.4 %shard_map.80 = (f32[16,64,512]{2,1,0:T(8,128)S(1)}, f32[4,40,128]{2,1,0:T(8,128)S(1)}) custom-call(s32[3]{0:T(128)S(1)} %pad_add_fusion.place_ref, f32[16,64,512]{2,1,0:T(8,128)S(1)} %get-tuple-element.39.gain, f32[16,1,512]{2,1,0:T(1,128)S(1)} %get-tuple-element.40.code, bf16[256,1152]{1,0:T(8,128)(2,1)S(1)} %get-tuple-element.33.wg, ...), custom_call_target="tpu_custom_call" | custom-call | flops 7000000000 | bytes 21000000 | tf_op jit(solution)/shard_map/pallas_call | solution.py:894
  55.6 0.0 collective-permute-done.13
  55.6 0.0 collective-permute-done.12
  55.6 0.0 collective-permute-done.11
  55.6 0.1 collective-permute-start.14
  55.7 1.6 %collective-permute-done.14.sibling = f32[4,4,40,128]{3,2,1,0:T(8,128)S(1)} collective-permute-done((f32[4,4,40,128]{3,2,1,0:T(8,128)S(1)}, f32[4,4,40,128]{3,2,1,0:T(8,128)S(1)}, u32[]{:S(2)}, u32[]{:S(2)}) %collective-permute-start.14) | collective-permute-done | bytes 327712 | tf_op jit(solution)/shard_map/ppermute | solution.py:964
  57.3 37.4 %shard_map.81 = (f32[32,128]{1,0:T(8,128)S(1)}, f32[16,64,256]{2,1,0:T(8,128)S(1)}, f32[8,1,256]{2,1,0:T(1,128)S(1)}, f32[1,256]{1,0:T(1,128)S(1)}) custom-call(s32[3]{0:T(128)S(1)} %pad_add_fusion.place_ref, f32[4,4,40,128]{3,2,1,0:T(8,128)S(1)} %pad_maximum_fusion.here, f32[4,4,40,128]{3,2,1,0:T(8,128)S(1)} %collective-permute-done.14.sibling, ...), custom_call_target="tpu_custom_call" | custom-call | flops 36999999488 | bytes 111000000 | tf_op jit(solution)/shard_map/pallas_call | solution.py:894
  94.7 2.2 %collective-permute-start.17 = (f32[32,128]{1,0:T(8,128)S(1)}, f32[32,128]{1,0:T(8,128)S(1)}, u32[]{:S(2)}, u32[]{:S(2)}) collective-permute-start(f32[32,128]{1,0:T(8,128)S(1)} %get-tuple-element.47), channel_id=1, source_target_pairs={{0,3},{1,2},{2,1},{3,0},{4,7},{5,6},{6,5},{7,4},{8,11},{9,10},{10,... | collective-permute-start | bytes 49160 | tf_op jit(solution)/shard_map/ppermute | solution.py:954
  97.0 4.2 %collective-permute-start.16 = (f32[32,128]{1,0:T(8,128)S(1)}, f32[32,128]{1,0:T(8,128)S(1)}, u32[]{:S(2)}, u32[]{:S(2)}) collective-permute-start(f32[32,128]{1,0:T(8,128)S(1)} %get-tuple-element.47), channel_id=1, source_target_pairs={{0,2},{1,3},{2,0},{3,1},{4,6},{5,7},{6,4},{7,5},{8,10},{9,11},{10,... | collective-permute-start | bytes 49160 | tf_op jit(solution)/shard_map/ppermute | solution.py:954
  101.2 0.0 collective-permute-start.15
  101.2 0.0 collective-permute-done.17
  101.2 2.1 %collective-permute-done.16 = f32[32,128]{1,0:T(8,128)S(1)} collective-permute-done((f32[32,128]{1,0:T(8,128)S(1)}, f32[32,128]{1,0:T(8,128)S(1)}, u32[]{:S(2)}, u32[]{:S(2)}) %collective-permute-start.16) | collective-permute-done | bytes 16416 | tf_op jit(solution)/shard_map/ppermute | solution.py:954
  103.3 1.7 %collective-permute-done.15 = f32[32,128]{1,0:T(8,128)S(1)} collective-permute-done((f32[32,128]{1,0:T(8,128)S(1)}, f32[32,128]{1,0:T(8,128)S(1)}, u32[]{:S(2)}, u32[]{:S(2)}) %collective-permute-start.15) | collective-permute-done | bytes 16416 | tf_op jit(solution)/shard_map/ppermute | solution.py:954
  105.0 0.1 collective-permute-start.19
  105.0 0.9 collective-permute-start.18
  105.9 2.6 %collective-permute-start.20 = (f32[4,32,128]{2,1,0:T(8,128)S(1)}, f32[4,32,128]{2,1,0:T(8,128)S(1)}, u32[]{:S(2)}, u32[]{:S(2)}) collective-permute-start(f32[4,32,128]{2,1,0:T(8,128)S(1)} %get-tuple-element.52), channel_id=1, source_target_pairs={{0,24},{4,28},{8,16},{12,20},{16,8},{20,12},{24,0},{28,4},{1,25},{... | collective-permute-start | bytes 196616 | tf_op jit(solution)/shard_map/ppermute | solution.py:961
  108.5 0.8 collective-permute-done.19
  109.3 0.1 collective-permute-done.18
  109.4 1.7 %collective-permute-done.20 = f32[4,32,128]{2,1,0:T(8,128)S(1)} collective-permute-done((f32[4,32,128]{2,1,0:T(8,128)S(1)}, f32[4,32,128]{2,1,0:T(8,128)S(1)}, u32[]{:S(2)}, u32[]{:S(2)}) %collective-permute-start.20) | collective-permute-done | bytes 65568 | tf_op jit(solution)/shard_map/ppermute | solution.py:961
  111.1 0.1 collective-permute-start.21
  111.2 1.5 %collective-permute-done.21.sibling = f32[4,4,32,128]{3,2,1,0:T(8,128)S(1)} collective-permute-done((f32[4,4,32,128]{3,2,1,0:T(8,128)S(1)}, f32[4,4,32,128]{3,2,1,0:T(8,128)S(1)}, u32[]{:S(2)}, u32[]{:S(2)}) %collective-permute-start.21) | collective-permute-done | bytes 262176 | tf_op jit(solution)/shard_map/ppermute | solution.py:964
  112.7 20.4 %shard_map.82 = f32[64,512]{1,0:T(8,128)} custom-call(s32[3]{0:T(128)S(1)} %pad_add_fusion.place_ref, f32[4,4,32,128]{3,2,1,0:T(8,128)S(1)} %pad_maximum_fusion.1.here, f32[4,4,32,128]{3,2,1,0:T(8,128)S(1)} %collective-permute-done.21.sibling, f32[8,1,256]{2,1,0:T(1,128)S(1)} %get-tuple-element.48.mid_code, f32[1,256]{1,0:T(1,128)S(1)} %get-tuple-element.49.coarse_code, ...), custom_call_target="tpu_custom_call" | custom-call | flops 17999998976 | bytes 54000000 | tf_op jit(solution)/shard_map/pallas_call | solution.py:894
  (19 shorter events, 0.1 us)
Async XLA Ops:
  0.0 7.0 %collective-permute-start.1 = (s32[1,512]{1,0:T(1,128)}, s32[1,512]{1,0:T(1,128)S(1)}, u32[]{:S(2)}, u32[]{:S(2)}) collective-permute-start(s32[1,512]{1,0:T(1,128)} %bitcast.30), channel_id=1, source_target_pairs={{0,16},{16,0},{1,17},{17,1},{2,18},{18,2},{3,19},{19,3},{4,20},{20... | collective-permute-start | bytes 6152 | tf_op jit(solution)/shard_map/ppermute | solution.py:917
  3.0 5.2 %copy-start.2 = (f32[1,1,1,64,512]{4,3,2,1,0:T(8,128)S(1)}, f32[1,1,1,64,512]{4,3,2,1,0:T(8,128)}, u32[]{:S(2)}) copy-start(f32[1,1,1,64,512]{4,3,2,1,0:T(8,128)} %param.7) | copy-start | bytes 393220
  3.0 5.2 %collective-permute-start = (f32[64,512]{1,0:T(8,128)}, f32[64,512]{1,0:T(8,128)S(1)}, u32[]{:S(2)}, u32[]{:S(2)}) collective-permute-start(f32[64,512]{1,0:T(8,128)} %bitcast.28), channel_id=1, source_target_pairs={{0,16},{16,0},{1,17},{17,1},{2,18},{18,2},{3,19},{19,3},{4,20},{20... | collective-permute-start | bytes 393224 | tf_op jit(solution)/shard_map/ppermute | solution.py:917
  3.0 0.9 copy-start.3
  3.9 2.9 %copy-start.6 = (s32[1,1,1,64]{3,2,1,0:T(1,128)S(1)}, s32[1,1,1,64]{3,2,1,0:T(1,128)}, u32[]{:S(2)}) copy-start(s32[1,1,1,64]{3,2,1,0:T(1,128)} %param.12) | copy-start | bytes 772
  3.9 4.2 %copy-start.5 = (s32[1,1,1,512]{3,2,1,0:T(1,128)S(1)}, s32[1,1,1,512]{3,2,1,0:T(1,128)}, u32[]{:S(2)}) copy-start(s32[1,1,1,512]{3,2,1,0:T(1,128)} %param.11) | copy-start | bytes 6148
  3.9 8.4 %copy-start.7 = (s32[1,1,1,8]{3,2,1,0:T(1,128)S(1)}, s32[1,1,1,8]{3,2,1,0:T(1,128)}, u32[]{:S(2)}) copy-start(s32[1,1,1,8]{3,2,1,0:T(1,128)} %param.13) | copy-start | bytes 100
  8.7 7.0 %collective-permute-start.3 = (f32[8,72,128]{2,1,0:T(8,128)S(1)}, f32[8,72,128]{2,1,0:T(8,128)S(1)}, u32[]{:S(2)}, u32[]{:S(2)}) collective-permute-start(f32[8,72,128]{2,1,0:T(8,128)S(1)} %shard_map.74.refs_0_.own), channel_id=1, source_target_pairs={{0,0},{4,8},{8,4},{12,12},{1,1},{5,9},{9,5},{13,13},{2,2},{6,10},{... | collective-permute-start | bytes 884744 | tf_op jit(solution)/shard_map/ppermute | solution.py:927
  9.4 6.3 %collective-permute-start.2 = (f32[8,72,128]{2,1,0:T(8,128)S(1)}, f32[8,72,128]{2,1,0:T(8,128)S(1)}, u32[]{:S(2)}, u32[]{:S(2)}) collective-permute-start(f32[8,72,128]{2,1,0:T(8,128)S(1)} %shard_map.74.refs_0_.own), channel_id=1, source_target_pairs={{0,4},{4,0},{8,12},{12,8},{1,5},{5,1},{9,13},{13,9},{2,6},{6,2},{1... | collective-permute-start | bytes 884744 | tf_op jit(solution)/shard_map/ppermute | solution.py:927
  15.7 4.5 %copy-start = (f32[6,4,64,64]{3,2,1,0:T(8,128)S(1)}, f32[6,4,64,64]{3,2,1,0:T(8,128)}, u32[]{:S(2)}) copy-start(f32[6,4,64,64]{3,2,1,0:T(8,128)} %face.1) | copy-start | bytes 1179652
  15.7 4.5 %copy-start.1 = (f32[8,64,64]{2,1,0:T(8,128)S(1)}, f32[8,64,64]{2,1,0:T(8,128)}, u32[]{:S(2)}) copy-start(f32[8,64,64]{2,1,0:T(8,128)} %prolong.1) | copy-start | bytes 393220
  15.7 4.5 %copy-start.4 = (f32[4,64,64]{2,1,0:T(8,128)S(1)}, f32[4,64,64]{2,1,0:T(8,128)}, u32[]{:S(2)}) copy-start(f32[4,64,64]{2,1,0:T(8,128)} %diag.3) | copy-start | bytes 196612
  17.8 8.3 %collective-permute-start.6 = (f32[3,72,128]{2,1,0:T(8,128)S(1)}, f32[3,72,128]{2,1,0:T(8,128)S(1)}, u32[]{:S(2)}, u32[]{:S(2)}) collective-permute-start(f32[3,72,128]{2,1,0:T(8,128)S(1)} %get-tuple-element.31), channel_id=1, source_target_pairs={{0,1},{1,0},{2,3},{3,2},{4,5},{5,4},{6,7},{7,6},{8,9},{9,8},{10,11... | collective-permute-start | bytes 331784 | tf_op jit(solution)/shard_map/ppermute | solution.py:932
  19.5 6.7 %collective-permute-start.7 = (f32[3,72,128]{2,1,0:T(8,128)S(1)}, f32[3,72,128]{2,1,0:T(8,128)S(1)}, u32[]{:S(2)}, u32[]{:S(2)}) collective-permute-start(f32[3,72,128]{2,1,0:T(8,128)S(1)} %get-tuple-element.32), channel_id=1, source_target_pairs={{0,0},{1,2},{2,1},{3,3},{4,4},{5,6},{6,5},{7,7},{8,8},{9,10},{10,9... | collective-permute-start | bytes 331784 | tf_op jit(solution)/shard_map/ppermute | solution.py:932
  20.8 18.3 %collective-permute-start.4 = (f32[16,72,128]{2,1,0:T(8,128)S(1)}, f32[16,72,128]{2,1,0:T(8,128)S(1)}, u32[]{:S(2)}, u32[]{:S(2)}) collective-permute-start(f32[16,72,128]{2,1,0:T(8,128)S(1)} %get-tuple-element.28), channel_id=1, source_target_pairs={{0,1},{1,0},{2,3},{3,2},{4,5},{5,4},{6,7},{7,6},{8,9},{9,8},{10,11... | collective-permute-start | bytes 1769480 | tf_op jit(solution)/shard_map/ppermute | solution.py:933
  25.3 13.8 %collective-permute-start.5 = (f32[16,72,128]{2,1,0:T(8,128)S(1)}, f32[16,72,128]{2,1,0:T(8,128)S(1)}, u32[]{:S(2)}, u32[]{:S(2)}) collective-permute-start(f32[16,72,128]{2,1,0:T(8,128)S(1)} %get-tuple-element.29), channel_id=1, source_target_pairs={{0,0},{1,2},{2,1},{3,3},{4,4},{5,6},{6,5},{7,7},{8,8},{9,10},{10,9... | collective-permute-start | bytes 1769480 | tf_op jit(solution)/shard_map/ppermute | solution.py:933
  34.2 11.4 %collective-permute-start.10 = (f32[40,128]{1,0:T(8,128)S(1)}, f32[40,128]{1,0:T(8,128)S(1)}, u32[]{:S(2)}, u32[]{:S(2)}) collective-permute-start(f32[40,128]{1,0:T(8,128)S(1)} %pad_maximum_fusion.4.payload), channel_id=1, source_target_pairs={{0,3},{1,2},{2,1},{3,0},{4,7},{5,6},{6,5},{7,4},{8,11},{9,10},{10,... | collective-permute-start | bytes 61448 | tf_op jit(solution)/shard_map/ppermute | solution.py:954
  35.4 10.1 %collective-permute-start.9 = (f32[40,128]{1,0:T(8,128)S(1)}, f32[40,128]{1,0:T(8,128)S(1)}, u32[]{:S(2)}, u32[]{:S(2)}) collective-permute-start(f32[40,128]{1,0:T(8,128)S(1)} %pad_maximum_fusion.4.payload), channel_id=1, source_target_pairs={{0,2},{1,3},{2,0},{3,1},{4,6},{5,7},{6,4},{7,5},{8,10},{9,11},{10,... | collective-permute-start | bytes 61448 | tf_op jit(solution)/shard_map/ppermute | solution.py:954
  37.9 7.7 %collective-permute-start.8 = (f32[40,128]{1,0:T(8,128)S(1)}, f32[40,128]{1,0:T(8,128)S(1)}, u32[]{:S(2)}, u32[]{:S(2)}) collective-permute-start(f32[40,128]{1,0:T(8,128)S(1)} %pad_maximum_fusion.4.payload), channel_id=1, source_target_pairs={{0,1},{1,0},{2,3},{3,2},{4,5},{5,4},{6,7},{7,6},{8,9},{9,8},{10,11... | collective-permute-start | bytes 61448 | tf_op jit(solution)/shard_map/ppermute | solution.py:954
  45.6 10.0 %collective-permute-start.13 = (f32[4,40,128]{2,1,0:T(8,128)S(1)}, f32[4,40,128]{2,1,0:T(8,128)S(1)}, u32[]{:S(2)}, u32[]{:S(2)}) collective-permute-start(f32[4,40,128]{2,1,0:T(8,128)S(1)} %pad_maximum_fusion.2.column), channel_id=1, source_target_pairs={{0,24},{4,28},{8,16},{12,20},{16,8},{20,12},{24,0},{28,4},{1,25},{... | collective-permute-start | bytes 245768 | tf_op jit(solution)/shard_map/ppermute | solution.py:961
  48.0 7.6 %collective-permute-start.12 = (f32[4,40,128]{2,1,0:T(8,128)S(1)}, f32[4,40,128]{2,1,0:T(8,128)S(1)}, u32[]{:S(2)}, u32[]{:S(2)}) collective-permute-start(f32[4,40,128]{2,1,0:T(8,128)S(1)} %pad_maximum_fusion.2.column), channel_id=1, source_target_pairs={{0,8},{4,12},{8,0},{12,4},{16,24},{20,28},{24,16},{28,20},{1,9},{5... | collective-permute-start | bytes 245768 | tf_op jit(solution)/shard_map/ppermute | solution.py:961
  48.0 7.6 %collective-permute-start.11 = (f32[4,40,128]{2,1,0:T(8,128)S(1)}, f32[4,40,128]{2,1,0:T(8,128)S(1)}, u32[]{:S(2)}, u32[]{:S(2)}) collective-permute-start(f32[4,40,128]{2,1,0:T(8,128)S(1)} %pad_maximum_fusion.2.column), channel_id=1, source_target_pairs={{0,16},{4,20},{8,24},{12,28},{16,0},{20,4},{24,8},{28,12},{1,17},{... | collective-permute-start | bytes 245768 | tf_op jit(solution)/shard_map/ppermute | solution.py:961
  55.6 1.7 %collective-permute-start.14 = (f32[4,4,40,128]{3,2,1,0:T(8,128)S(1)}, f32[4,4,40,128]{3,2,1,0:T(8,128)S(1)}, u32[]{:S(2)}, u32[]{:S(2)}) collective-permute-start(f32[4,4,40,128]{3,2,1,0:T(8,128)S(1)} %pad_maximum_fusion.here), channel_id=1, source_target_pairs={{0,4},{4,0},{8,12},{12,8},{1,5},{5,1},{9,13},{13,9},{2,6},{6,2},{1... | collective-permute-start | bytes 983048 | tf_op jit(solution)/shard_map/ppermute | solution.py:964
  94.7 6.5 %collective-permute-start.17 = (f32[32,128]{1,0:T(8,128)S(1)}, f32[32,128]{1,0:T(8,128)S(1)}, u32[]{:S(2)}, u32[]{:S(2)}) collective-permute-start(f32[32,128]{1,0:T(8,128)S(1)} %get-tuple-element.47), channel_id=1, source_target_pairs={{0,3},{1,2},{2,1},{3,0},{4,7},{5,6},{6,5},{7,4},{8,11},{9,10},{10,... | collective-permute-start | bytes 49160 | tf_op jit(solution)/shard_map/ppermute | solution.py:954
  97.0 6.3 %collective-permute-start.16 = (f32[32,128]{1,0:T(8,128)S(1)}, f32[32,128]{1,0:T(8,128)S(1)}, u32[]{:S(2)}, u32[]{:S(2)}) collective-permute-start(f32[32,128]{1,0:T(8,128)S(1)} %get-tuple-element.47), channel_id=1, source_target_pairs={{0,2},{1,3},{2,0},{3,1},{4,6},{5,7},{6,4},{7,5},{8,10},{9,11},{10,... | collective-permute-start | bytes 49160 | tf_op jit(solution)/shard_map/ppermute | solution.py:954
  101.2 3.7 %collective-permute-start.15 = (f32[32,128]{1,0:T(8,128)S(1)}, f32[32,128]{1,0:T(8,128)S(1)}, u32[]{:S(2)}, u32[]{:S(2)}) collective-permute-start(f32[32,128]{1,0:T(8,128)S(1)} %get-tuple-element.47), channel_id=1, source_target_pairs={{0,1},{1,0},{2,3},{3,2},{4,5},{5,4},{6,7},{7,6},{8,9},{9,8},{10,11... | collective-permute-start | bytes 49160 | tf_op jit(solution)/shard_map/ppermute | solution.py:954
  105.0 4.3 %collective-permute-start.19 = (f32[4,32,128]{2,1,0:T(8,128)S(1)}, f32[4,32,128]{2,1,0:T(8,128)S(1)}, u32[]{:S(2)}, u32[]{:S(2)}) collective-permute-start(f32[4,32,128]{2,1,0:T(8,128)S(1)} %get-tuple-element.52), channel_id=1, source_target_pairs={{0,8},{4,12},{8,0},{12,4},{16,24},{20,28},{24,16},{28,20},{1,9},{5... | collective-permute-start | bytes 196616 | tf_op jit(solution)/shard_map/ppermute | solution.py:961
  105.0 4.3 %collective-permute-start.18 = (f32[4,32,128]{2,1,0:T(8,128)S(1)}, f32[4,32,128]{2,1,0:T(8,128)S(1)}, u32[]{:S(2)}, u32[]{:S(2)}) collective-permute-start(f32[4,32,128]{2,1,0:T(8,128)S(1)} %get-tuple-element.52), channel_id=1, source_target_pairs={{0,16},{4,20},{8,24},{12,28},{16,0},{20,4},{24,8},{28,12},{1,17},{... | collective-permute-start | bytes 196616 | tf_op jit(solution)/shard_map/ppermute | solution.py:961
  105.9 5.2 %collective-permute-start.20 = (f32[4,32,128]{2,1,0:T(8,128)S(1)}, f32[4,32,128]{2,1,0:T(8,128)S(1)}, u32[]{:S(2)}, u32[]{:S(2)}) collective-permute-start(f32[4,32,128]{2,1,0:T(8,128)S(1)} %get-tuple-element.52), channel_id=1, source_target_pairs={{0,24},{4,28},{8,16},{12,20},{16,8},{20,12},{24,0},{28,4},{1,25},{... | collective-permute-start | bytes 196616 | tf_op jit(solution)/shard_map/ppermute | solution.py:961
  111.1 1.6 %collective-permute-start.21 = (f32[4,4,32,128]{3,2,1,0:T(8,128)S(1)}, f32[4,4,32,128]{3,2,1,0:T(8,128)S(1)}, u32[]{:S(2)}, u32[]{:S(2)}) collective-permute-start(f32[4,4,32,128]{3,2,1,0:T(8,128)S(1)} %pad_maximum_fusion.1.here), channel_id=1, source_target_pairs={{0,4},{4,0},{8,12},{12,8},{1,5},{5,1},{9,13},{13,9},{2,6},{6,2},{1... | collective-permute-start | bytes 786440 | tf_op jit(solution)/shard_map/ppermute | solution.py:964

commit v3 on v2

--- a/solution.py
+++ b/solution.py
@@ -280,6 +280,7 @@
 SHALLOW = SWEEPS
 FIRST_PIVOTS = MODES // 2
 PAIRS = CX
+THICK = CX + HALO - 1
 SLOT = CY * CZ
 
 
@@ -290,7 +291,7 @@
 SHALLOW_LANES = sum(layer_rows(d, SHALLOW) for d in range(1, SHALLOW + 1))
 DEEP_LANES = sum(layer_rows(d, HALO) for d in range(1, HALO + 1))
 PER_TILE = TILE // (2 * SHALLOW_LANES)
-SHALLOW_TILES = -(-PAIRS // PER_TILE)
+SHALLOW_TILES = -(-(THICK // 2) // PER_TILE)
 
 
 def layer_of(index, first, last, halo):
@@ -327,12 +328,19 @@
     return jnp.where(place == 1, 1, jnp.where(place // 2 == odd, 2, 0))
 
 
+def pairs_skipped(place_ref):
+    return place_ref[0] * ((2 * CX - THICK) // 2)
+
+
 def pack_kernel(place_ref, own, first, second, scaled, thin_first, thin_second, thick_first, thick_second):
     column = iota((1, 4 * TILE), 1)
     lane, kind = column % TILE, column // TILE
     row = iota((3 * TILE, 4 * TILE), 0)
     odd_y, odd_z = place_ref[1] & 1, place_ref[2] & 1
-    parts = [jnp.concatenate([r[pair] for r in (first, own, second)], axis=1) for pair in range(PAIRS)]
+    skipped = pairs_skipped(place_ref)
+    parts = [
+        jnp.concatenate([r[skipped + pair] for r in (first, own, second)], axis=1) for pair in range(THICK // 2)
+    ]
     parts = split(jnp.concatenate(parts, axis=0))
     shallow = 0.0
     for odd in range(2):
@@ -351,7 +359,7 @@
         selector = where_equal(row, jnp.where(valid == 1, source, -1))
         packed = dot(parts[0], selector) + dot(parts[1], selector)
         shallow = shallow + packed[:, :2 * TILE]
-        for pair in range(PAIRS):
+        for pair in range(THICK // 2):
             rows = packed[pair * ROWS:(pair + 1) * ROWS]
             thick_first[2 * pair + odd], thick_second[2 * pair + odd] = rows[:, 2 * TILE:3 * TILE], rows[:, 3 * TILE:]
     for tile in range(SHALLOW_TILES):
@@ -359,7 +367,7 @@
             strip = 0.0
             for slot in range(PER_TILE):
                 pair = tile * PER_TILE + slot
-                if pair < PAIRS:
+                if pair < THICK // 2:
                     piece = shallow[pair * ROWS:(pair + 1) * ROWS, kind * TILE:(kind + 1) * TILE]
                     strip = strip + (pltpu.roll(piece, slot * 2 * SHALLOW_LANES, 1) if slot else piece)
             out[tile] = strip
@@ -389,6 +397,7 @@
     depth = jnp.where(z < 0, -z, z - (CZ - 1))
     middle = (z >= 0) & (z < CZ)
     strip = jnp.where(jnp.where(z < 0, 0, 1) == odd_z, 1, 0)
+    skipped = pairs_skipped(place_ref)
     if shallow:
         outer = lane_of(depth, y, 1, SHALLOW, SHALLOW) + 3 * TILE + strip * (TILE // 2)
         step = SHALLOW_LANES
@@ -404,7 +413,10 @@
             for i in range(pairs):
                 pair = start + i
                 line = [r[pair] for r in (along_y[0], own, along_y[1])]
-                line += [shallow_strip(*along_z, pair)] if shallow else [r[2 * pair + odd] for r in along_z]
+                if shallow:
+                    line += [shallow_strip(*along_z, pair - skipped)]
+                else:
+                    line += [r[jnp.clip(2 * (pair - skipped) + odd, 0, THICK - 1)] for r in along_z]
                 parts.append(jnp.concatenate(line, axis=1))
             parts = split(jnp.concatenate(parts, axis=0))
         source = jnp.where(middle, inner + odd * SLOT, outer + odd * step)
@@ -696,7 +708,8 @@
         for j, value in enumerate(values):
             field.put(2 * first + j, value)
 
-    grouped(gx * ((CX - depth) // 2), (CX + depth) // 2, max(group_size(layout.lanes) // 3, 1), body)
+    pairs = (CX + depth) // 2
+    grouped(gx * ((CX - depth) // 2), pairs, -(-pairs // 2), body)
 
 
 def fine_residual(field, own, source, wr, wa, wd, code):
@@ -850,10 +863,14 @@
         elif depth == NEAR:
             sweep(first, None, start, count, wg, gain, code, narrow)
         else:
-            sweep(now, other, start, count, wg, near_gain, near_code)
+            def store(x, value, target=other):
+                target.put(x, value)
+                if depth == SWEEPS:
+                    result[x] = value
+
+            sweep(now, other, start, count, wg, near_gain, near_code, store)
             now, other = other, now
     payload[...] = fine_residual(now, gx * CX, source, wr, wa, wd, near_code)
-    result[...] = now.full[1:1 + 2 * CX]
 
 
 def third_kernel(sizes, grid, place_ref, here, sibling, mid_code, coarse_code, near_gain, near_code, solved,
@@ -927,7 +944,7 @@
     along_y = [lax.ppermute(own, "gy", swap) for swap in swaps["gy"]]
     scaled = invert_part(range(FIRST_PIVOTS, MODES), relax_weight, half_way, own)
     weights = make_weights(scaled, diag_blocks, face_blocks, prolong)
-    thin, thick = shape_of(SHALLOW_TILES, ROWS, TILE), shape_of(2 * PAIRS, ROWS, TILE)
+    thin, thick = shape_of(SHALLOW_TILES, ROWS, TILE), shape_of(THICK, ROWS, TILE)
     send = call(pack_kernel, 1.5, [thin, thin, thick, thick], [], place_ref, own, *along_y, scaled, unread=1)
     shallow = [lax.ppermute(value, "gz", swap) for value, swap in zip(send[:2], swaps["gz"])]
     deep = [lax.ppermute(value, "gz", swap) for value, swap in zip(send[2:], swaps["gz"])]

time: 133 us -> 131 us (0.985)
    ppermute x6, starting transfers between devices: 10.9 us -> 9.13 us  [along_z(): return [lax.ppermute(value, 'gz', turn) for turn in turns]]
where the time goes in v3:
time: 131 us
  Pallas kernels  87.2 us (67%)
  starting transfers between devices  31.1 us (24%)
  waiting for transfers between devices  11.1 us (8%)
    pallas_call x10, Pallas kernels, call(): pl.pallas_call(kernel, out_shape=out_shape, in_specs=specs, out_specs=jax...  87.2 us
    ppermute x6, starting transfers between devices, along_z(): return [lax.ppermute(value, 'gz', turn) for turn in turns]  9.13 us
    ppermute x4, starting transfers between devices, wide_device(): lax.ppermute(value, 'gz', swap)  7.62 us
    ppermute x6, starting transfers between devices, across(): return [lax.ppermute(column, ('gx', 'gy'), flip) for flip in flips]  7.6 us
    ppermute x6, waiting for transfers between devices, along_z(): return [lax.ppermute(value, 'gz', turn) for turn in turns]  3.75 us
    ppermute x2, starting transfers between devices, wide_device(): along_y = [lax.ppermute(own, 'gy', swap) for swap in swaps['gy']]  3.58 us
    ppermute x2, waiting for transfers between devices, with_sibling(): return (here, lax.ppermute(here, 'gy', [(j, j ^ 1) for j in range(n_gy)]))  3.14 us
    ppermute x2, starting transfers between devices, wide_device(): others = (lax.ppermute(values, 'gx', swap), lax.ppermute(kinds, 'gx', swap))  3.03 us
  transfers between devices with their start and end apart: 22, of which 9 were waited for; matrix products, arithmetic and copies ran while one was open for 0% of the time, Pallas kernels for 21%

profile of v3, /device:TPU:0, one launch (start us, length us, event | category | flops | bytes accessed | tf_op | source)
XLA Modules:
  0.0 131.1 jit_solution(5579356833265951399)
XLA Ops:
  0.0 3.0 %collective-permute-start.1 = (s32[1,512]{1,0:T(1,128)}, s32[1,512]{1,0:T(1,128)S(1)}, u32[]{:S(2)}, u32[]{:S(2)}) collective-permute-start(s32[1,512]{1,0:T(1,128)} %bitcast.30), channel_id=1, source_target_pairs={{0,16},{16,0},{1,17},{17,1},{2,18},{18,2},{3,19},{19,3},{4,20},{20... | collective-permute-start | bytes 6152 | tf_op jit(solution)/shard_map/ppermute | solution.py:934
  3.0 0.1 collective-permute-start
  3.0 0.9 copy-done.3
  3.9 2.9 %shard_map.73.half_way.diag = f32[4,64,64]{2,1,0:T(8,128)S(1)} custom-call(f32[4,64,64]{2,1,0:T(8,128)S(1)} %copy-done.3), custom_call_target="tpu_custom_call" | custom-call | flops 3000000000 | bytes 9000000 | tf_op jit(solution)/shard_map/pallas_call | solution.py:911
  6.9 0.1 pad_add_fusion.place_ref
  7.0 0.0 collective-permute-done.1.other_materials
  7.0 1.2 collective-permute-done.other
  8.2 0.0 copy-done.5
  8.2 0.6 shard_map.74.refs_0_.own
  8.7 0.7 collective-permute-start.3
  9.4 2.9 %collective-permute-start.2 = (f32[8,72,128]{2,1,0:T(8,128)S(1)}, f32[8,72,128]{2,1,0:T(8,128)S(1)}, u32[]{:S(2)}, u32[]{:S(2)}) collective-permute-start(f32[8,72,128]{2,1,0:T(8,128)S(1)} %shard_map.74.refs_0_.own), channel_id=1, source_target_pairs={{0,4},{4,0},{8,12},{12,8},{1,5},{5,1},{9,13},{13,9},{2,6},{6,2},{1... | collective-permute-start | bytes 884744 | tf_op jit(solution)/shard_map/ppermute | solution.py:944
  12.3 0.1 convert_element_type.20
  12.4 0.1 broadcast_in_dim.6
  12.5 0.1 reshape.29
  12.6 3.0 %shard_map.75.scaled = f32[4,64,64]{2,1,0:T(8,128)S(1)} custom-call(f32[4,64,64]{2,1,0:T(8,128)S(1)} %shard_map.73.half_way.diag, f32[8,72,128]{2,1,0:T(8,128)S(1)} %shard_map.74.refs_0_.own), custom_call_target="tpu_custom_call" | custom-call | flops 3000000000 | bytes 9000000 | tf_op jit(solution)/shard_map/pallas_call | solution.py:911
  15.7 0.0 copy-start
  15.7 0.0 copy-start.1
  15.7 0.0 copy-start.4
  15.7 0.0 collective-permute-done.3.second.y1
  15.7 0.0 collective-permute-done.2.first.y0
  15.7 1.9 %shard_map.76 = (f32[3,72,128]{2,1,0:T(8,128)S(1)}, f32[3,72,128]{2,1,0:T(8,128)S(1)}, f32[14,72,128]{2,1,0:T(8,128)S(1)}, f32[14,72,128]{2,1,0:T(8,128)S(1)}) custom-call(s32[3]{0:T(128)S(1)} %pad_add_fusion.place_ref, f32[8,72,128]{2,1,0:T(8,128)S(1)} %shard_map.74.refs_0_.own, f32[8,72,128]{2,1,0:T(8,128)S(1)} %collective-permute-done.2.first.y0, ...), custom_call_target="tpu_custom_call" | custom-call | flops 1500000000 | bytes 4500000 | tf_op jit(solution)/shard_map/pallas_call | solution.py:911
  17.7 1.6 %collective-permute-start.6 = (f32[3,72,128]{2,1,0:T(8,128)S(1)}, f32[3,72,128]{2,1,0:T(8,128)S(1)}, u32[]{:S(2)}, u32[]{:S(2)}) collective-permute-start(f32[3,72,128]{2,1,0:T(8,128)S(1)} %get-tuple-element.31), channel_id=1, source_target_pairs={{0,1},{1,0},{2,3},{3,2},{4,5},{5,4},{6,7},{7,6},{8,9},{9,8},{10,11... | collective-permute-start | bytes 331784 | tf_op jit(solution)/shard_map/ppermute | solution.py:949
  19.3 0.7 collective-permute-start.7
  20.0 0.1 pad_maximum_fusion.5
  20.1 0.6 shard_map.77
  20.7 4.5 %collective-permute-start.4 = (f32[14,72,128]{2,1,0:T(8,128)S(1)}, f32[14,72,128]{2,1,0:T(8,128)S(1)}, u32[]{:S(2)}, u32[]{:S(2)}) collective-permute-start(f32[14,72,128]{2,1,0:T(8,128)S(1)} %get-tuple-element.28), channel_id=1, source_target_pairs={{0,1},{1,0},{2,3},{3,2},{4,5},{5,4},{6,7},{7,6},{8,9},{9,8},{10,11... | collective-permute-start | bytes 1548296 | tf_op jit(solution)/shard_map/ppermute | solution.py:950
  25.1 0.9 collective-permute-start.5
  26.0 0.0 collective-permute-done.6.z0
  26.0 0.0 collective-permute-done.7.z1
  26.0 8.0 %shard_map.78 = (f32[8,64,256]{2,1,0:T(8,128)S(1)}, f32[32,128]{1,0:T(8,128)S(1)}) custom-call(s32[3]{0:T(128)S(1)} %pad_add_fusion.place_ref, f32[8,72,128]{2,1,0:T(8,128)S(1)} %shard_map.74.refs_0_.own, f32[8,72,128]{2,1,0:T(8,128)S(1)} %collective-permute-done.2.first.y0, f32[8,72,128]{2,1,0:T(8,128)S(1)} %collective-permute-done.3.second.y1, ...), custom_call_target="tpu_custom_call" | custom-call | flops 7000000000 | bytes 21000000 | tf_op jit(solution)/shard_map/pallas_call | solution.py:911
  34.0 1.3 collective-permute-start.10
  35.3 2.4 %collective-permute-start.9 = (f32[40,128]{1,0:T(8,128)S(1)}, f32[40,128]{1,0:T(8,128)S(1)}, u32[]{:S(2)}, u32[]{:S(2)}) collective-permute-start(f32[40,128]{1,0:T(8,128)S(1)} %pad_maximum_fusion.4.payload), channel_id=1, source_target_pairs={{0,2},{1,3},{2,0},{3,1},{4,6},{5,7},{6,4},{7,5},{8,10},{9,11},{10,... | collective-permute-start | bytes 61448 | tf_op jit(solution)/shard_map/ppermute | solution.py:971
  37.7 0.8 collective-permute-start.8
  38.5 0.0 collective-permute-done.4.z0
  38.5 0.0 collective-permute-done.5.z1
  38.5 6.4 %shard_map.79 = (f32[16,64,512]{2,1,0:T(8,128)S(1)}, f32[16,1,512]{2,1,0:T(1,128)S(1)}, f32[16,64,256]{2,1,0:T(8,128)S(1)}, f32[16,1,256]{2,1,0:T(1,128)S(1)}, f32[40,128]{1,0:T(8,128)S(1)}) custom-call(s32[3]{0:T(128)S(1)} %pad_add_fusion.place_ref, f32[8,72,128]{2,1,0:T(8,128)S(1)} %shard_map.74.refs_0_.own, ...), custom_call_target="tpu_custom_call" | custom-call | flops 6000000000 | bytes 18000000 | tf_op jit(solution)/shard_map/pallas_call | solution.py:911
  44.9 0.0 collective-permute-done.10
  44.9 0.0 collective-permute-done.9
  44.9 0.0 collective-permute-done.8
  44.9 2.9 %collective-permute-start.13 = (f32[4,40,128]{2,1,0:T(8,128)S(1)}, f32[4,40,128]{2,1,0:T(8,128)S(1)}, u32[]{:S(2)}, u32[]{:S(2)}) collective-permute-start(f32[4,40,128]{2,1,0:T(8,128)S(1)} %pad_maximum_fusion.2.column), channel_id=1, source_target_pairs={{0,24},{4,28},{8,16},{12,20},{16,8},{20,12},{24,0},{28,4},{1,25},{... | collective-permute-start | bytes 245768 | tf_op jit(solution)/shard_map/ppermute | solution.py:978
  47.8 0.0 collective-permute-start.12
  47.8 1.2 collective-permute-start.11
  49.0 6.4 %shard_map.80 = (f32[16,64,512]{2,1,0:T(8,128)S(1)}, f32[4,40,128]{2,1,0:T(8,128)S(1)}) custom-call(s32[3]{0:T(128)S(1)} %pad_add_fusion.place_ref, f32[16,64,512]{2,1,0:T(8,128)S(1)} %get-tuple-element.39.gain, f32[16,1,512]{2,1,0:T(1,128)S(1)} %get-tuple-element.40.code, bf16[256,1152]{1,0:T(8,128)(2,1)S(1)} %get-tuple-element.33.wg, ...), custom_call_target="tpu_custom_call" | custom-call | flops 7000000000 | bytes 21000000 | tf_op jit(solution)/shard_map/pallas_call | solution.py:911
  55.4 0.0 collective-permute-done.13
  55.4 0.0 collective-permute-done.12
  55.4 0.0 collective-permute-done.11
  55.5 0.1 collective-permute-start.14
  55.5 1.6 %collective-permute-done.14.sibling = f32[4,4,40,128]{3,2,1,0:T(8,128)S(1)} collective-permute-done((f32[4,4,40,128]{3,2,1,0:T(8,128)S(1)}, f32[4,4,40,128]{3,2,1,0:T(8,128)S(1)}, u32[]{:S(2)}, u32[]{:S(2)}) %collective-permute-start.14) | collective-permute-done | bytes 327712 | tf_op jit(solution)/shard_map/ppermute | solution.py:981
  57.2 36.9 %shard_map.81 = (f32[32,128]{1,0:T(8,128)S(1)}, f32[16,64,256]{2,1,0:T(8,128)S(1)}, f32[8,1,256]{2,1,0:T(1,128)S(1)}, f32[1,256]{1,0:T(1,128)S(1)}) custom-call(s32[3]{0:T(128)S(1)} %pad_add_fusion.place_ref, f32[4,4,40,128]{3,2,1,0:T(8,128)S(1)} %pad_maximum_fusion.here, f32[4,4,40,128]{3,2,1,0:T(8,128)S(1)} %collective-permute-done.14.sibling, ...), custom_call_target="tpu_custom_call" | custom-call | flops 36999999488 | bytes 111000000 | tf_op jit(solution)/shard_map/pallas_call | solution.py:911
  94.1 2.2 %collective-permute-start.17 = (f32[32,128]{1,0:T(8,128)S(1)}, f32[32,128]{1,0:T(8,128)S(1)}, u32[]{:S(2)}, u32[]{:S(2)}) collective-permute-start(f32[32,128]{1,0:T(8,128)S(1)} %get-tuple-element.47), channel_id=1, source_target_pairs={{0,3},{1,2},{2,1},{3,0},{4,7},{5,6},{6,5},{7,4},{8,11},{9,10},{10,... | collective-permute-start | bytes 49160 | tf_op jit(solution)/shard_map/ppermute | solution.py:971
  96.3 2.4 %collective-permute-start.16 = (f32[32,128]{1,0:T(8,128)S(1)}, f32[32,128]{1,0:T(8,128)S(1)}, u32[]{:S(2)}, u32[]{:S(2)}) collective-permute-start(f32[32,128]{1,0:T(8,128)S(1)} %get-tuple-element.47), channel_id=1, source_target_pairs={{0,2},{1,3},{2,0},{3,1},{4,6},{5,7},{6,4},{7,5},{8,10},{9,11},{10,... | collective-permute-start | bytes 49160 | tf_op jit(solution)/shard_map/ppermute | solution.py:971
  98.8 0.0 collective-permute-start.15
  98.8 1.0 collective-permute-done.17
  99.8 1.2 collective-permute-done.16
  101.0 1.5 %collective-permute-done.15 = f32[32,128]{1,0:T(8,128)S(1)} collective-permute-done((f32[32,128]{1,0:T(8,128)S(1)}, f32[32,128]{1,0:T(8,128)S(1)}, u32[]{:S(2)}, u32[]{:S(2)}) %collective-permute-start.15) | collective-permute-done | bytes 16416 | tf_op jit(solution)/shard_map/ppermute | solution.py:971
  102.5 0.6 collective-permute-start.19
  103.1 0.8 collective-permute-start.18
  103.9 2.2 %collective-permute-start.20 = (f32[4,32,128]{2,1,0:T(8,128)S(1)}, f32[4,32,128]{2,1,0:T(8,128)S(1)}, u32[]{:S(2)}, u32[]{:S(2)}) collective-permute-start(f32[4,32,128]{2,1,0:T(8,128)S(1)} %get-tuple-element.52), channel_id=1, source_target_pairs={{0,24},{4,28},{8,16},{12,20},{16,8},{20,12},{24,0},{28,4},{1,25},{... | collective-permute-start | bytes 196616 | tf_op jit(solution)/shard_map/ppermute | solution.py:978
  106.1 0.8 collective-permute-done.19
  106.9 0.5 collective-permute-done.18
  107.3 1.7 %collective-permute-done.20 = f32[4,32,128]{2,1,0:T(8,128)S(1)} collective-permute-done((f32[4,32,128]{2,1,0:T(8,128)S(1)}, f32[4,32,128]{2,1,0:T(8,128)S(1)}, u32[]{:S(2)}, u32[]{:S(2)}) %collective-permute-start.20) | collective-permute-done | bytes 65568 | tf_op jit(solution)/shard_map/ppermute | solution.py:978
  109.1 0.1 collective-permute-start.21
  109.2 1.5 %collective-permute-done.21.sibling = f32[4,4,32,128]{3,2,1,0:T(8,128)S(1)} collective-permute-done((f32[4,4,32,128]{3,2,1,0:T(8,128)S(1)}, f32[4,4,32,128]{3,2,1,0:T(8,128)S(1)}, u32[]{:S(2)}, u32[]{:S(2)}) %collective-permute-start.21) | collective-permute-done | bytes 262176 | tf_op jit(solution)/shard_map/ppermute | solution.py:981
  110.7 20.4 %shard_map.82 = f32[64,512]{1,0:T(8,128)} custom-call(s32[3]{0:T(128)S(1)} %pad_add_fusion.place_ref, f32[4,4,32,128]{3,2,1,0:T(8,128)S(1)} %pad_maximum_fusion.1.here, f32[4,4,32,128]{3,2,1,0:T(8,128)S(1)} %collective-permute-done.21.sibling, f32[8,1,256]{2,1,0:T(1,128)S(1)} %get-tuple-element.48.mid_code, f32[1,256]{1,0:T(1,128)S(1)} %get-tuple-element.49.coarse_code, ...), custom_call_target="tpu_custom_call" | custom-call | flops 17999998976 | bytes 54000000 | tf_op jit(solution)/shard_map/pallas_call | solution.py:911
  (19 shorter events, 0.1 us)
Async XLA Ops:
  0.0 7.0 %collective-permute-start.1 = (s32[1,512]{1,0:T(1,128)}, s32[1,512]{1,0:T(1,128)S(1)}, u32[]{:S(2)}, u32[]{:S(2)}) collective-permute-start(s32[1,512]{1,0:T(1,128)} %bitcast.30), channel_id=1, source_target_pairs={{0,16},{16,0},{1,17},{17,1},{2,18},{18,2},{3,19},{19,3},{4,20},{20... | collective-permute-start | bytes 6152 | tf_op jit(solution)/shard_map/ppermute | solution.py:934
  3.0 5.2 %copy-start.2 = (f32[1,1,1,64,512]{4,3,2,1,0:T(8,128)S(1)}, f32[1,1,1,64,512]{4,3,2,1,0:T(8,128)}, u32[]{:S(2)}) copy-start(f32[1,1,1,64,512]{4,3,2,1,0:T(8,128)} %param.7) | copy-start | bytes 393220
  3.0 5.2 %collective-permute-start = (f32[64,512]{1,0:T(8,128)}, f32[64,512]{1,0:T(8,128)S(1)}, u32[]{:S(2)}, u32[]{:S(2)}) collective-permute-start(f32[64,512]{1,0:T(8,128)} %bitcast.28), channel_id=1, source_target_pairs={{0,16},{16,0},{1,17},{17,1},{2,18},{18,2},{3,19},{19,3},{4,20},{20... | collective-permute-start | bytes 393224 | tf_op jit(solution)/shard_map/ppermute | solution.py:934
  3.0 0.9 copy-start.3
  3.9 2.9 %copy-start.6 = (s32[1,1,1,64]{3,2,1,0:T(1,128)S(1)}, s32[1,1,1,64]{3,2,1,0:T(1,128)}, u32[]{:S(2)}) copy-start(s32[1,1,1,64]{3,2,1,0:T(1,128)} %param.12) | copy-start | bytes 772
  3.9 4.2 %copy-start.5 = (s32[1,1,1,512]{3,2,1,0:T(1,128)S(1)}, s32[1,1,1,512]{3,2,1,0:T(1,128)}, u32[]{:S(2)}) copy-start(s32[1,1,1,512]{3,2,1,0:T(1,128)} %param.11) | copy-start | bytes 6148
  3.9 8.4 %copy-start.7 = (s32[1,1,1,8]{3,2,1,0:T(1,128)S(1)}, s32[1,1,1,8]{3,2,1,0:T(1,128)}, u32[]{:S(2)}) copy-start(s32[1,1,1,8]{3,2,1,0:T(1,128)} %param.13) | copy-start | bytes 100
  8.7 7.0 %collective-permute-start.3 = (f32[8,72,128]{2,1,0:T(8,128)S(1)}, f32[8,72,128]{2,1,0:T(8,128)S(1)}, u32[]{:S(2)}, u32[]{:S(2)}) collective-permute-start(f32[8,72,128]{2,1,0:T(8,128)S(1)} %shard_map.74.refs_0_.own), channel_id=1, source_target_pairs={{0,0},{4,8},{8,4},{12,12},{1,1},{5,9},{9,5},{13,13},{2,2},{6,10},{... | collective-permute-start | bytes 884744 | tf_op jit(solution)/shard_map/ppermute | solution.py:944
  9.4 6.3 %collective-permute-start.2 = (f32[8,72,128]{2,1,0:T(8,128)S(1)}, f32[8,72,128]{2,1,0:T(8,128)S(1)}, u32[]{:S(2)}, u32[]{:S(2)}) collective-permute-start(f32[8,72,128]{2,1,0:T(8,128)S(1)} %shard_map.74.refs_0_.own), channel_id=1, source_target_pairs={{0,4},{4,0},{8,12},{12,8},{1,5},{5,1},{9,13},{13,9},{2,6},{6,2},{1... | collective-permute-start | bytes 884744 | tf_op jit(solution)/shard_map/ppermute | solution.py:944
  15.7 4.4 %copy-start = (f32[6,4,64,64]{3,2,1,0:T(8,128)S(1)}, f32[6,4,64,64]{3,2,1,0:T(8,128)}, u32[]{:S(2)}) copy-start(f32[6,4,64,64]{3,2,1,0:T(8,128)} %face.1) | copy-start | bytes 1179652
  15.7 4.4 %copy-start.1 = (f32[8,64,64]{2,1,0:T(8,128)S(1)}, f32[8,64,64]{2,1,0:T(8,128)}, u32[]{:S(2)}) copy-start(f32[8,64,64]{2,1,0:T(8,128)} %prolong.1) | copy-start | bytes 393220
  15.7 4.4 %copy-start.4 = (f32[4,64,64]{2,1,0:T(8,128)S(1)}, f32[4,64,64]{2,1,0:T(8,128)}, u32[]{:S(2)}) copy-start(f32[4,64,64]{2,1,0:T(8,128)} %diag.3) | copy-start | bytes 196612
  17.7 8.3 %collective-permute-start.6 = (f32[3,72,128]{2,1,0:T(8,128)S(1)}, f32[3,72,128]{2,1,0:T(8,128)S(1)}, u32[]{:S(2)}, u32[]{:S(2)}) collective-permute-start(f32[3,72,128]{2,1,0:T(8,128)S(1)} %get-tuple-element.31), channel_id=1, source_target_pairs={{0,1},{1,0},{2,3},{3,2},{4,5},{5,4},{6,7},{7,6},{8,9},{9,8},{10,11... | collective-permute-start | bytes 331784 | tf_op jit(solution)/shard_map/ppermute | solution.py:949
  19.3 6.7 %collective-permute-start.7 = (f32[3,72,128]{2,1,0:T(8,128)S(1)}, f32[3,72,128]{2,1,0:T(8,128)S(1)}, u32[]{:S(2)}, u32[]{:S(2)}) collective-permute-start(f32[3,72,128]{2,1,0:T(8,128)S(1)} %get-tuple-element.32), channel_id=1, source_target_pairs={{0,0},{1,2},{2,1},{3,3},{4,4},{5,6},{6,5},{7,7},{8,8},{9,10},{10,9... | collective-permute-start | bytes 331784 | tf_op jit(solution)/shard_map/ppermute | solution.py:949
  20.7 17.8 %collective-permute-start.4 = (f32[14,72,128]{2,1,0:T(8,128)S(1)}, f32[14,72,128]{2,1,0:T(8,128)S(1)}, u32[]{:S(2)}, u32[]{:S(2)}) collective-permute-start(f32[14,72,128]{2,1,0:T(8,128)S(1)} %get-tuple-element.28), channel_id=1, source_target_pairs={{0,1},{1,0},{2,3},{3,2},{4,5},{5,4},{6,7},{7,6},{8,9},{9,8},{10,11... | collective-permute-start | bytes 1548296 | tf_op jit(solution)/shard_map/ppermute | solution.py:950
  25.1 13.4 %collective-permute-start.5 = (f32[14,72,128]{2,1,0:T(8,128)S(1)}, f32[14,72,128]{2,1,0:T(8,128)S(1)}, u32[]{:S(2)}, u32[]{:S(2)}) collective-permute-start(f32[14,72,128]{2,1,0:T(8,128)S(1)} %get-tuple-element.29), channel_id=1, source_target_pairs={{0,0},{1,2},{2,1},{3,3},{4,4},{5,6},{6,5},{7,7},{8,8},{9,10},{10,9... | collective-permute-start | bytes 1548296 | tf_op jit(solution)/shard_map/ppermute | solution.py:950
  34.0 10.9 %collective-permute-start.10 = (f32[40,128]{1,0:T(8,128)S(1)}, f32[40,128]{1,0:T(8,128)S(1)}, u32[]{:S(2)}, u32[]{:S(2)}) collective-permute-start(f32[40,128]{1,0:T(8,128)S(1)} %pad_maximum_fusion.4.payload), channel_id=1, source_target_pairs={{0,3},{1,2},{2,1},{3,0},{4,7},{5,6},{6,5},{7,4},{8,11},{9,10},{10,... | collective-permute-start | bytes 61448 | tf_op jit(solution)/shard_map/ppermute | solution.py:971
  35.3 9.6 %collective-permute-start.9 = (f32[40,128]{1,0:T(8,128)S(1)}, f32[40,128]{1,0:T(8,128)S(1)}, u32[]{:S(2)}, u32[]{:S(2)}) collective-permute-start(f32[40,128]{1,0:T(8,128)S(1)} %pad_maximum_fusion.4.payload), channel_id=1, source_target_pairs={{0,2},{1,3},{2,0},{3,1},{4,6},{5,7},{6,4},{7,5},{8,10},{9,11},{10,... | collective-permute-start | bytes 61448 | tf_op jit(solution)/shard_map/ppermute | solution.py:971
  37.7 7.2 %collective-permute-start.8 = (f32[40,128]{1,0:T(8,128)S(1)}, f32[40,128]{1,0:T(8,128)S(1)}, u32[]{:S(2)}, u32[]{:S(2)}) collective-permute-start(f32[40,128]{1,0:T(8,128)S(1)} %pad_maximum_fusion.4.payload), channel_id=1, source_target_pairs={{0,1},{1,0},{2,3},{3,2},{4,5},{5,4},{6,7},{7,6},{8,9},{9,8},{10,11... | collective-permute-start | bytes 61448 | tf_op jit(solution)/shard_map/ppermute | solution.py:971
  44.9 10.5 %collective-permute-start.13 = (f32[4,40,128]{2,1,0:T(8,128)S(1)}, f32[4,40,128]{2,1,0:T(8,128)S(1)}, u32[]{:S(2)}, u32[]{:S(2)}) collective-permute-start(f32[4,40,128]{2,1,0:T(8,128)S(1)} %pad_maximum_fusion.2.column), channel_id=1, source_target_pairs={{0,24},{4,28},{8,16},{12,20},{16,8},{20,12},{24,0},{28,4},{1,25},{... | collective-permute-start | bytes 245768 | tf_op jit(solution)/shard_map/ppermute | solution.py:978
  47.8 7.6 %collective-permute-start.12 = (f32[4,40,128]{2,1,0:T(8,128)S(1)}, f32[4,40,128]{2,1,0:T(8,128)S(1)}, u32[]{:S(2)}, u32[]{:S(2)}) collective-permute-start(f32[4,40,128]{2,1,0:T(8,128)S(1)} %pad_maximum_fusion.2.column), channel_id=1, source_target_pairs={{0,8},{4,12},{8,0},{12,4},{16,24},{20,28},{24,16},{28,20},{1,9},{5... | collective-permute-start | bytes 245768 | tf_op jit(solution)/shard_map/ppermute | solution.py:978
  47.8 7.6 %collective-permute-start.11 = (f32[4,40,128]{2,1,0:T(8,128)S(1)}, f32[4,40,128]{2,1,0:T(8,128)S(1)}, u32[]{:S(2)}, u32[]{:S(2)}) collective-permute-start(f32[4,40,128]{2,1,0:T(8,128)S(1)} %pad_maximum_fusion.2.column), channel_id=1, source_target_pairs={{0,16},{4,20},{8,24},{12,28},{16,0},{20,4},{24,8},{28,12},{1,17},{... | collective-permute-start | bytes 245768 | tf_op jit(solution)/shard_map/ppermute | solution.py:978
  55.5 1.7 %collective-permute-start.14 = (f32[4,4,40,128]{3,2,1,0:T(8,128)S(1)}, f32[4,4,40,128]{3,2,1,0:T(8,128)S(1)}, u32[]{:S(2)}, u32[]{:S(2)}) collective-permute-start(f32[4,4,40,128]{3,2,1,0:T(8,128)S(1)} %pad_maximum_fusion.here), channel_id=1, source_target_pairs={{0,4},{4,0},{8,12},{12,8},{1,5},{5,1},{9,13},{13,9},{2,6},{6,2},{1... | collective-permute-start | bytes 983048 | tf_op jit(solution)/shard_map/ppermute | solution.py:981
  94.1 5.7 %collective-permute-start.17 = (f32[32,128]{1,0:T(8,128)S(1)}, f32[32,128]{1,0:T(8,128)S(1)}, u32[]{:S(2)}, u32[]{:S(2)}) collective-permute-start(f32[32,128]{1,0:T(8,128)S(1)} %get-tuple-element.47), channel_id=1, source_target_pairs={{0,3},{1,2},{2,1},{3,0},{4,7},{5,6},{6,5},{7,4},{8,11},{9,10},{10,... | collective-permute-start | bytes 49160 | tf_op jit(solution)/shard_map/ppermute | solution.py:971
  96.3 4.6 %collective-permute-start.16 = (f32[32,128]{1,0:T(8,128)S(1)}, f32[32,128]{1,0:T(8,128)S(1)}, u32[]{:S(2)}, u32[]{:S(2)}) collective-permute-start(f32[32,128]{1,0:T(8,128)S(1)} %get-tuple-element.47), channel_id=1, source_target_pairs={{0,2},{1,3},{2,0},{3,1},{4,6},{5,7},{6,4},{7,5},{8,10},{9,11},{10,... | collective-permute-start | bytes 49160 | tf_op jit(solution)/shard_map/ppermute | solution.py:971
  98.8 3.7 %collective-permute-start.15 = (f32[32,128]{1,0:T(8,128)S(1)}, f32[32,128]{1,0:T(8,128)S(1)}, u32[]{:S(2)}, u32[]{:S(2)}) collective-permute-start(f32[32,128]{1,0:T(8,128)S(1)} %get-tuple-element.47), channel_id=1, source_target_pairs={{0,1},{1,0},{2,3},{3,2},{4,5},{5,4},{6,7},{7,6},{8,9},{9,8},{10,11... | collective-permute-start | bytes 49160 | tf_op jit(solution)/shard_map/ppermute | solution.py:971
  102.5 4.3 %collective-permute-start.19 = (f32[4,32,128]{2,1,0:T(8,128)S(1)}, f32[4,32,128]{2,1,0:T(8,128)S(1)}, u32[]{:S(2)}, u32[]{:S(2)}) collective-permute-start(f32[4,32,128]{2,1,0:T(8,128)S(1)} %get-tuple-element.52), channel_id=1, source_target_pairs={{0,8},{4,12},{8,0},{12,4},{16,24},{20,28},{24,16},{28,20},{1,9},{5... | collective-permute-start | bytes 196616 | tf_op jit(solution)/shard_map/ppermute | solution.py:978
  103.1 4.3 %collective-permute-start.18 = (f32[4,32,128]{2,1,0:T(8,128)S(1)}, f32[4,32,128]{2,1,0:T(8,128)S(1)}, u32[]{:S(2)}, u32[]{:S(2)}) collective-permute-start(f32[4,32,128]{2,1,0:T(8,128)S(1)} %get-tuple-element.52), channel_id=1, source_target_pairs={{0,16},{4,20},{8,24},{12,28},{16,0},{20,4},{24,8},{28,12},{1,17},{... | collective-permute-start | bytes 196616 | tf_op jit(solution)/shard_map/ppermute | solution.py:978
  103.9 5.2 %collective-permute-start.20 = (f32[4,32,128]{2,1,0:T(8,128)S(1)}, f32[4,32,128]{2,1,0:T(8,128)S(1)}, u32[]{:S(2)}, u32[]{:S(2)}) collective-permute-start(f32[4,32,128]{2,1,0:T(8,128)S(1)} %get-tuple-element.52), channel_id=1, source_target_pairs={{0,24},{4,28},{8,16},{12,20},{16,8},{20,12},{24,0},{28,4},{1,25},{... | collective-permute-start | bytes 196616 | tf_op jit(solution)/shard_map/ppermute | solution.py:978
  109.1 1.6 %collective-permute-start.21 = (f32[4,4,32,128]{3,2,1,0:T(8,128)S(1)}, f32[4,4,32,128]{3,2,1,0:T(8,128)S(1)}, u32[]{:S(2)}, u32[]{:S(2)}) collective-permute-start(f32[4,4,32,128]{3,2,1,0:T(8,128)S(1)} %pad_maximum_fusion.1.here), channel_id=1, source_target_pairs={{0,4},{4,0},{8,12},{12,8},{1,5},{5,1},{9,13},{13,9},{2,6},{6,2},{1... | collective-permute-start | bytes 786440 | tf_op jit(solution)/shard_map/ppermute | solution.py:981

commit v4 on v3

--- a/solution.py
+++ b/solution.py
@@ -760,23 +760,30 @@
     payload[...] = fine_residual(second, mine, source, wr, wa, wd, code)
 
 
-def gain_kernel(sizes, place_ref, own, y0, y1, z0, z1, wi, payload, gain, code, near_gain, near_code, passed, whole):
+def gain_kernel(sizes, place_ref, own, y0, y1, z0, z1, wi, payload, gain, code, passed, whole):
     def put(x, value, material):
         whole[x], code[x] = value, material
 
     unpack(wide_layout, sizes, place_ref, own, (y0, y1), (z0, z1), 0, PAIRS, put, False)
-    to_near = near_selector()
 
     def begin(start, length):
         values = [pick(dot(wi[...], stack3(whole[start + j])), code[start + j], 1) for j in range(length)]
         for j, value in enumerate(values):
             gain[start + j] = value
-            near_gain[start + j] = place(value, to_near)
-        for j in range(length):
-            near_code[start + j] = dot(jnp.broadcast_to(code[start + j], (8, LANES)).astype(bf16), to_near)[:1]
 
     grouped(0, 2 * CX, 4, begin)
     passed[...] = payload[...]
+
+
+def narrow_kernel(place_ref, gain, code, solved, near_gain, near_code):
+    to_near = near_selector()
+
+    def body(start, length):
+        for j in range(length):
+            near_gain[start + j] = place(gain[start + j], to_near)
+            near_code[start + j] = dot(jnp.broadcast_to(code[start + j], (8, LANES)).astype(bf16), to_near)[:1]
+
+    grouped(place_ref[0] * (CX - NEAR), CX + NEAR, 4, body)
 
 
 def deep_kernel(place_ref, gain, code, wg, column, solved, passed, *scratch):
@@ -982,9 +989,9 @@
 
     payload = jnp.concatenate([payload, tail], axis=0)
     turned = along_z(payload)
-    gain, code, near_gain, near_code, payload = call(
+    gain, code, payload = call(
         partial(gain_kernel, sizes), 6,
-        [whole, shape_of(2 * CX, 1, LANES), small, small_code, shape_of(*payload.shape)],
+        [whole, shape_of(2 * CX, 1, LANES), shape_of(*payload.shape)],
         [pltpu.VMEM(whole.shape, f32)],
         place_ref, own, *along_y, *deep, weights[3], payload,
     )
@@ -994,6 +1001,7 @@
         deep_kernel, 7, [whole, shape_of(*column.shape)], wide, place_ref, gain, code, weights[0], column
     )
     gathered = with_sibling(jnp.stack([column] + flipped))
+    near_gain, near_code = call(narrow_kernel, 1, [small, small_code], [], place_ref, gain, code, solved, unread=1)
     planes, lanes = grid[0], grid[1] * grid[2]
     payload, solved, mid_code, coarse_code = call(
         partial(second_kernel, sizes, grid), 37,

time: 131 us -> 131 us (level)
  Pallas kernels: 87.2 us -> 89 us
  waiting for transfers between devices: 11.1 us -> 9.49 us
    pallas_call x10 -> x11, Pallas kernels: 87.2 us -> 89 us  [call(): pl.pallas_call(kernel, out_shape=out_shape, in_specs=specs, out_specs=jax...]
    ppermute x2, waiting for transfers between devices: 3.14 us -> 1.52 us  [with_sibling(): return (here, lax.ppermute(here, 'gy', [(j, j ^ 1) for j in range(n_gy)]))]
  transfers between devices with their start and end apart: 22 -> 22, of which waited for: 9 -> 8; matrix products, arithmetic and copies ran while one was open for 0% -> 0% of each run, Pallas kernels for 21% -> 21%
where the time goes in v4:
time: 131 us
  Pallas kernels  89 us (68%)
  starting transfers between devices  31.1 us (24%)
  waiting for transfers between devices  9.49 us (7%)
    pallas_call x11, Pallas kernels, call(): pl.pallas_call(kernel, out_shape=out_shape, in_specs=specs, out_specs=jax...  89 us
    ppermute x6, starting transfers between devices, along_z(): return [lax.ppermute(value, 'gz', turn) for turn in turns]  9.06 us
    ppermute x6, starting transfers between devices, across(): return [lax.ppermute(column, ('gx', 'gy'), flip) for flip in flips]  7.62 us
    ppermute x4, starting transfers between devices, wide_device(): lax.ppermute(value, 'gz', swap)  7.62 us
    ppermute x6, waiting for transfers between devices, along_z(): return [lax.ppermute(value, 'gz', turn) for turn in turns]  3.74 us
    ppermute x2, starting transfers between devices, wide_device(): along_y = [lax.ppermute(own, 'gy', swap) for swap in swaps['gy']]  3.58 us
    ppermute x6, waiting for transfers between devices, across(): return [lax.ppermute(column, ('gx', 'gy'), flip) for flip in flips]  3.04 us
    ppermute x2, starting transfers between devices, wide_device(): others = (lax.ppermute(values, 'gx', swap), lax.ppermute(kinds, 'gx', swap))  3.03 us
  transfers between devices with their start and end apart: 22, of which 8 were waited for; matrix products, arithmetic and copies ran while one was open for 0% of the time, Pallas kernels for 21%

profile of v4, /device:TPU:0, one launch (start us, length us, event | category | flops | bytes accessed | tf_op | source)
XLA Modules:
  0.0 131.3 jit_solution(5762313321676936028)
XLA Ops:
  0.0 3.0 %collective-permute-start.1 = (s32[1,512]{1,0:T(1,128)}, s32[1,512]{1,0:T(1,128)S(1)}, u32[]{:S(2)}, u32[]{:S(2)}) collective-permute-start(s32[1,512]{1,0:T(1,128)} %bitcast.30), channel_id=1, source_target_pairs={{0,16},{16,0},{1,17},{17,1},{2,18},{18,2},{3,19},{19,3},{4,20},{20... | collective-permute-start | bytes 6152 | tf_op jit(solution)/shard_map/ppermute | solution.py:941
  3.0 0.1 collective-permute-start
  3.0 0.9 copy-done.3
  3.9 2.9 %shard_map.73.half_way.diag = f32[4,64,64]{2,1,0:T(8,128)S(1)} custom-call(f32[4,64,64]{2,1,0:T(8,128)S(1)} %copy-done.3), custom_call_target="tpu_custom_call" | custom-call | flops 3000000000 | bytes 9000000 | tf_op jit(solution)/shard_map/pallas_call | solution.py:918
  6.9 0.1 pad_add_fusion.place_ref
  7.0 0.0 collective-permute-done.1.other_materials
  7.0 1.2 collective-permute-done.other
  8.2 0.6 shard_map.74.refs_0_.own
  8.7 0.7 collective-permute-start.3
  9.4 2.9 %collective-permute-start.2 = (f32[8,72,128]{2,1,0:T(8,128)S(1)}, f32[8,72,128]{2,1,0:T(8,128)S(1)}, u32[]{:S(2)}, u32[]{:S(2)}) collective-permute-start(f32[8,72,128]{2,1,0:T(8,128)S(1)} %shard_map.74.refs_0_.own), channel_id=1, source_target_pairs={{0,4},{4,0},{8,12},{12,8},{1,5},{5,1},{9,13},{13,9},{2,6},{6,2},{1... | collective-permute-start | bytes 884744 | tf_op jit(solution)/shard_map/ppermute | solution.py:951
  12.3 0.1 convert_element_type.20
  12.4 0.1 broadcast_in_dim.6
  12.5 0.1 reshape.29
  12.6 3.0 %shard_map.75.scaled = f32[4,64,64]{2,1,0:T(8,128)S(1)} custom-call(f32[4,64,64]{2,1,0:T(8,128)S(1)} %shard_map.73.half_way.diag, f32[8,72,128]{2,1,0:T(8,128)S(1)} %shard_map.74.refs_0_.own), custom_call_target="tpu_custom_call" | custom-call | flops 3000000000 | bytes 9000000 | tf_op jit(solution)/shard_map/pallas_call | solution.py:918
  15.7 0.0 copy-start
  15.7 0.0 copy-start.1
  15.7 0.0 copy-start.4
  15.7 0.0 collective-permute-done.3.second.y1
  15.7 0.0 collective-permute-done.2.first.y0
  15.7 1.9 %shard_map.76 = (f32[3,72,128]{2,1,0:T(8,128)S(1)}, f32[3,72,128]{2,1,0:T(8,128)S(1)}, f32[14,72,128]{2,1,0:T(8,128)S(1)}, f32[14,72,128]{2,1,0:T(8,128)S(1)}) custom-call(s32[3]{0:T(128)S(1)} %pad_add_fusion.place_ref, f32[8,72,128]{2,1,0:T(8,128)S(1)} %shard_map.74.refs_0_.own, f32[8,72,128]{2,1,0:T(8,128)S(1)} %collective-permute-done.2.first.y0, ...), custom_call_target="tpu_custom_call" | custom-call | flops 1500000000 | bytes 4500000 | tf_op jit(solution)/shard_map/pallas_call | solution.py:918
  17.7 1.6 %collective-permute-start.6 = (f32[3,72,128]{2,1,0:T(8,128)S(1)}, f32[3,72,128]{2,1,0:T(8,128)S(1)}, u32[]{:S(2)}, u32[]{:S(2)}) collective-permute-start(f32[3,72,128]{2,1,0:T(8,128)S(1)} %get-tuple-element.31), channel_id=1, source_target_pairs={{0,1},{1,0},{2,3},{3,2},{4,5},{5,4},{6,7},{7,6},{8,9},{9,8},{10,11... | collective-permute-start | bytes 331784 | tf_op jit(solution)/shard_map/ppermute | solution.py:956
  19.3 0.7 collective-permute-start.7
  20.0 0.1 pad_maximum_fusion.5
  20.1 0.6 shard_map.77
  20.7 4.5 %collective-permute-start.4 = (f32[14,72,128]{2,1,0:T(8,128)S(1)}, f32[14,72,128]{2,1,0:T(8,128)S(1)}, u32[]{:S(2)}, u32[]{:S(2)}) collective-permute-start(f32[14,72,128]{2,1,0:T(8,128)S(1)} %get-tuple-element.28), channel_id=1, source_target_pairs={{0,1},{1,0},{2,3},{3,2},{4,5},{5,4},{6,7},{7,6},{8,9},{9,8},{10,11... | collective-permute-start | bytes 1548296 | tf_op jit(solution)/shard_map/ppermute | solution.py:957
  25.1 0.9 collective-permute-start.5
  26.0 0.0 collective-permute-done.6.z0
  26.0 0.0 collective-permute-done.7.z1
  26.0 8.0 %shard_map.78 = (f32[8,64,256]{2,1,0:T(8,128)S(1)}, f32[32,128]{1,0:T(8,128)S(1)}) custom-call(s32[3]{0:T(128)S(1)} %pad_add_fusion.place_ref, f32[8,72,128]{2,1,0:T(8,128)S(1)} %shard_map.74.refs_0_.own, f32[8,72,128]{2,1,0:T(8,128)S(1)} %collective-permute-done.2.first.y0, f32[8,72,128]{2,1,0:T(8,128)S(1)} %collective-permute-done.3.second.y1, ...), custom_call_target="tpu_custom_call" | custom-call | flops 7000000000 | bytes 21000000 | tf_op jit(solution)/shard_map/pallas_call | solution.py:918
  34.1 1.3 collective-permute-start.10
  35.3 2.5 %collective-permute-start.9 = (f32[40,128]{1,0:T(8,128)S(1)}, f32[40,128]{1,0:T(8,128)S(1)}, u32[]{:S(2)}, u32[]{:S(2)}) collective-permute-start(f32[40,128]{1,0:T(8,128)S(1)} %pad_maximum_fusion.4.payload), channel_id=1, source_target_pairs={{0,2},{1,3},{2,0},{3,1},{4,6},{5,7},{6,4},{7,5},{8,10},{9,11},{10,... | collective-permute-start | bytes 61448 | tf_op jit(solution)/shard_map/ppermute | solution.py:978
  37.8 0.7 collective-permute-start.8
  38.5 0.0 collective-permute-done.4.z0
  38.5 0.0 collective-permute-done.5.z1
  38.5 4.4 %shard_map.79 = (f32[16,64,512]{2,1,0:T(8,128)S(1)}, f32[16,1,512]{2,1,0:T(1,128)S(1)}, f32[40,128]{1,0:T(8,128)S(1)}) custom-call(s32[3]{0:T(128)S(1)} %pad_add_fusion.place_ref, f32[8,72,128]{2,1,0:T(8,128)S(1)} %shard_map.74.refs_0_.own, f32[8,72,128]{2,1,0:T(8,128)S(1)} %collective-permute-done.2.first.y0, ...), custom_call_target="tpu_custom_call" | custom-call | flops 6000000000 | bytes 18000000 | tf_op jit(solution)/shard_map/pallas_call | solution.py:918
  43.0 0.0 collective-permute-done.10
  43.0 0.0 collective-permute-done.9
  43.0 0.0 collective-permute-done.8
  43.0 2.8 %collective-permute-start.13 = (f32[4,40,128]{2,1,0:T(8,128)S(1)}, f32[4,40,128]{2,1,0:T(8,128)S(1)}, u32[]{:S(2)}, u32[]{:S(2)}) collective-permute-start(f32[4,40,128]{2,1,0:T(8,128)S(1)} %pad_maximum_fusion.2.column), channel_id=1, source_target_pairs={{0,24},{4,28},{8,16},{12,20},{16,8},{20,12},{24,0},{28,4},{1,25},{... | collective-permute-start | bytes 245768 | tf_op jit(solution)/shard_map/ppermute | solution.py:985
  45.9 0.0 collective-permute-start.12
  45.9 1.2 collective-permute-start.11
  47.1 6.6 %shard_map.80 = (f32[16,64,512]{2,1,0:T(8,128)S(1)}, f32[4,40,128]{2,1,0:T(8,128)S(1)}) custom-call(s32[3]{0:T(128)S(1)} %pad_add_fusion.place_ref, f32[16,64,512]{2,1,0:T(8,128)S(1)} %get-tuple-element.39.gain, f32[16,1,512]{2,1,0:T(1,128)S(1)} %get-tuple-element.40.code, bf16[256,1152]{1,0:T(8,128)(2,1)S(1)} %get-tuple-element.33.wg, ...), custom_call_target="tpu_custom_call" | custom-call | flops 7000000000 | bytes 21000000 | tf_op jit(solution)/shard_map/pallas_call | solution.py:918
  53.7 0.0 collective-permute-done.13
  53.7 0.0 collective-permute-done.12
  53.7 0.0 collective-permute-done.11
  53.8 0.1 collective-permute-start.14
  53.8 2.5 %shard_map.81 = (f32[16,64,256]{2,1,0:T(8,128)S(1)}, f32[16,1,256]{2,1,0:T(1,128)S(1)}) custom-call(s32[3]{0:T(128)S(1)} %pad_add_fusion.place_ref, f32[16,64,512]{2,1,0:T(8,128)S(1)} %get-tuple-element.39.gain, f32[16,1,512]{2,1,0:T(1,128)S(1)} %get-tuple-element.40.code, f32[16,64,512]{2,1,0:T(8,128)S(1)} %get-tuple-element.43.solved), custom_call_target="tpu_custom_call" | custom-call | flops 1000000000 | bytes 3000000 | tf_op jit(solution)/shard_map/pallas_call | solution.py:918
  56.4 0.0 collective-permute-done.14.sibling
  56.4 37.7 %shard_map.82 = (f32[32,128]{1,0:T(8,128)S(1)}, f32[16,64,256]{2,1,0:T(8,128)S(1)}, f32[8,1,256]{2,1,0:T(1,128)S(1)}, f32[1,256]{1,0:T(1,128)S(1)}) custom-call(s32[3]{0:T(128)S(1)} %pad_add_fusion.place_ref, f32[4,4,40,128]{3,2,1,0:T(8,128)S(1)} %pad_maximum_fusion.here, f32[4,4,40,128]{3,2,1,0:T(8,128)S(1)} %collective-permute-done.14.sibling, ...), custom_call_target="tpu_custom_call" | custom-call | flops 36999999488 | bytes 111000000 | tf_op jit(solution)/shard_map/pallas_call | solution.py:918
  94.1 2.2 %collective-permute-start.17 = (f32[32,128]{1,0:T(8,128)S(1)}, f32[32,128]{1,0:T(8,128)S(1)}, u32[]{:S(2)}, u32[]{:S(2)}) collective-permute-start(f32[32,128]{1,0:T(8,128)S(1)} %get-tuple-element.47), channel_id=1, source_target_pairs={{0,3},{1,2},{2,1},{3,0},{4,7},{5,6},{6,5},{7,4},{8,11},{9,10},{10,... | collective-permute-start | bytes 49160 | tf_op jit(solution)/shard_map/ppermute | solution.py:978
  96.3 2.4 %collective-permute-start.16 = (f32[32,128]{1,0:T(8,128)S(1)}, f32[32,128]{1,0:T(8,128)S(1)}, u32[]{:S(2)}, u32[]{:S(2)}) collective-permute-start(f32[32,128]{1,0:T(8,128)S(1)} %get-tuple-element.47), channel_id=1, source_target_pairs={{0,2},{1,3},{2,0},{3,1},{4,6},{5,7},{6,4},{7,5},{8,10},{9,11},{10,... | collective-permute-start | bytes 49160 | tf_op jit(solution)/shard_map/ppermute | solution.py:978
  98.7 0.0 collective-permute-start.15
  98.7 1.0 collective-permute-done.17
  99.7 1.4 %collective-permute-done.16 = f32[32,128]{1,0:T(8,128)S(1)} collective-permute-done((f32[32,128]{1,0:T(8,128)S(1)}, f32[32,128]{1,0:T(8,128)S(1)}, u32[]{:S(2)}, u32[]{:S(2)}) %collective-permute-start.16) | collective-permute-done | bytes 16416 | tf_op jit(solution)/shard_map/ppermute | solution.py:978
  101.1 1.3 %collective-permute-done.15 = f32[32,128]{1,0:T(8,128)S(1)} collective-permute-done((f32[32,128]{1,0:T(8,128)S(1)}, f32[32,128]{1,0:T(8,128)S(1)}, u32[]{:S(2)}, u32[]{:S(2)}) %collective-permute-start.15) | collective-permute-done | bytes 16416 | tf_op jit(solution)/shard_map/ppermute | solution.py:978
  102.4 0.6 collective-permute-start.19
  103.1 0.8 collective-permute-start.18
  103.9 2.1 %collective-permute-start.20 = (f32[4,32,128]{2,1,0:T(8,128)S(1)}, f32[4,32,128]{2,1,0:T(8,128)S(1)}, u32[]{:S(2)}, u32[]{:S(2)}) collective-permute-start(f32[4,32,128]{2,1,0:T(8,128)S(1)} %get-tuple-element.52), channel_id=1, source_target_pairs={{0,24},{4,28},{8,16},{12,20},{16,8},{20,12},{24,0},{28,4},{1,25},{... | collective-permute-start | bytes 196616 | tf_op jit(solution)/shard_map/ppermute | solution.py:985
  106.0 1.0 collective-permute-done.19
  107.0 0.4 collective-permute-done.18
  107.5 1.6 %collective-permute-done.20 = f32[4,32,128]{2,1,0:T(8,128)S(1)} collective-permute-done((f32[4,32,128]{2,1,0:T(8,128)S(1)}, f32[4,32,128]{2,1,0:T(8,128)S(1)}, u32[]{:S(2)}, u32[]{:S(2)}) %collective-permute-start.20) | collective-permute-done | bytes 65568 | tf_op jit(solution)/shard_map/ppermute | solution.py:985
  109.0 0.1 collective-permute-start.21
  109.1 1.5 %collective-permute-done.21.sibling = f32[4,4,32,128]{3,2,1,0:T(8,128)S(1)} collective-permute-done((f32[4,4,32,128]{3,2,1,0:T(8,128)S(1)}, f32[4,4,32,128]{3,2,1,0:T(8,128)S(1)}, u32[]{:S(2)}, u32[]{:S(2)}) %collective-permute-start.21) | collective-permute-done | bytes 262176 | tf_op jit(solution)/shard_map/ppermute | solution.py:988
  110.6 20.6 %shard_map.83 = f32[64,512]{1,0:T(8,128)} custom-call(s32[3]{0:T(128)S(1)} %pad_add_fusion.place_ref, f32[4,4,32,128]{3,2,1,0:T(8,128)S(1)} %pad_maximum_fusion.1.here, f32[4,4,32,128]{3,2,1,0:T(8,128)S(1)} %collective-permute-done.21.sibling, f32[8,1,256]{2,1,0:T(1,128)S(1)} %get-tuple-element.48.mid_code, f32[1,256]{1,0:T(1,128)S(1)} %get-tuple-element.49.coarse_code, ...), custom_call_target="tpu_custom_call" | custom-call | flops 17999998976 | bytes 54000000 | tf_op jit(solution)/shard_map/pallas_call | solution.py:918
  (20 shorter events, 0.1 us)
Async XLA Ops:
  0.0 7.0 %collective-permute-start.1 = (s32[1,512]{1,0:T(1,128)}, s32[1,512]{1,0:T(1,128)S(1)}, u32[]{:S(2)}, u32[]{:S(2)}) collective-permute-start(s32[1,512]{1,0:T(1,128)} %bitcast.30), channel_id=1, source_target_pairs={{0,16},{16,0},{1,17},{17,1},{2,18},{18,2},{3,19},{19,3},{4,20},{20... | collective-permute-start | bytes 6152 | tf_op jit(solution)/shard_map/ppermute | solution.py:941
  3.0 5.2 %copy-start.2 = (f32[1,1,1,64,512]{4,3,2,1,0:T(8,128)S(1)}, f32[1,1,1,64,512]{4,3,2,1,0:T(8,128)}, u32[]{:S(2)}) copy-start(f32[1,1,1,64,512]{4,3,2,1,0:T(8,128)} %param.7) | copy-start | bytes 393220
  3.0 5.2 %collective-permute-start = (f32[64,512]{1,0:T(8,128)}, f32[64,512]{1,0:T(8,128)S(1)}, u32[]{:S(2)}, u32[]{:S(2)}) collective-permute-start(f32[64,512]{1,0:T(8,128)} %bitcast.28), channel_id=1, source_target_pairs={{0,16},{16,0},{1,17},{17,1},{2,18},{18,2},{3,19},{19,3},{4,20},{20... | collective-permute-start | bytes 393224 | tf_op jit(solution)/shard_map/ppermute | solution.py:941
  3.0 0.9 copy-start.3
  3.9 2.9 %copy-start.6 = (s32[1,1,1,64]{3,2,1,0:T(1,128)S(1)}, s32[1,1,1,64]{3,2,1,0:T(1,128)}, u32[]{:S(2)}) copy-start(s32[1,1,1,64]{3,2,1,0:T(1,128)} %param.12) | copy-start | bytes 772
  3.9 4.2 %copy-start.5 = (s32[1,1,1,512]{3,2,1,0:T(1,128)S(1)}, s32[1,1,1,512]{3,2,1,0:T(1,128)}, u32[]{:S(2)}) copy-start(s32[1,1,1,512]{3,2,1,0:T(1,128)} %param.11) | copy-start | bytes 6148
  3.9 8.4 %copy-start.7 = (s32[1,1,1,8]{3,2,1,0:T(1,128)S(1)}, s32[1,1,1,8]{3,2,1,0:T(1,128)}, u32[]{:S(2)}) copy-start(s32[1,1,1,8]{3,2,1,0:T(1,128)} %param.13) | copy-start | bytes 100
  8.7 7.0 %collective-permute-start.3 = (f32[8,72,128]{2,1,0:T(8,128)S(1)}, f32[8,72,128]{2,1,0:T(8,128)S(1)}, u32[]{:S(2)}, u32[]{:S(2)}) collective-permute-start(f32[8,72,128]{2,1,0:T(8,128)S(1)} %shard_map.74.refs_0_.own), channel_id=1, source_target_pairs={{0,0},{4,8},{8,4},{12,12},{1,1},{5,9},{9,5},{13,13},{2,2},{6,10},{... | collective-permute-start | bytes 884744 | tf_op jit(solution)/shard_map/ppermute | solution.py:951
  9.4 6.3 %collective-permute-start.2 = (f32[8,72,128]{2,1,0:T(8,128)S(1)}, f32[8,72,128]{2,1,0:T(8,128)S(1)}, u32[]{:S(2)}, u32[]{:S(2)}) collective-permute-start(f32[8,72,128]{2,1,0:T(8,128)S(1)} %shard_map.74.refs_0_.own), channel_id=1, source_target_pairs={{0,4},{4,0},{8,12},{12,8},{1,5},{5,1},{9,13},{13,9},{2,6},{6,2},{1... | collective-permute-start | bytes 884744 | tf_op jit(solution)/shard_map/ppermute | solution.py:951
  15.7 4.4 %copy-start = (f32[6,4,64,64]{3,2,1,0:T(8,128)S(1)}, f32[6,4,64,64]{3,2,1,0:T(8,128)}, u32[]{:S(2)}) copy-start(f32[6,4,64,64]{3,2,1,0:T(8,128)} %face.1) | copy-start | bytes 1179652
  15.7 4.4 %copy-start.1 = (f32[8,64,64]{2,1,0:T(8,128)S(1)}, f32[8,64,64]{2,1,0:T(8,128)}, u32[]{:S(2)}) copy-start(f32[8,64,64]{2,1,0:T(8,128)} %prolong.1) | copy-start | bytes 393220
  15.7 4.4 %copy-start.4 = (f32[4,64,64]{2,1,0:T(8,128)S(1)}, f32[4,64,64]{2,1,0:T(8,128)}, u32[]{:S(2)}) copy-start(f32[4,64,64]{2,1,0:T(8,128)} %diag.3) | copy-start | bytes 196612
  17.7 8.3 %collective-permute-start.6 = (f32[3,72,128]{2,1,0:T(8,128)S(1)}, f32[3,72,128]{2,1,0:T(8,128)S(1)}, u32[]{:S(2)}, u32[]{:S(2)}) collective-permute-start(f32[3,72,128]{2,1,0:T(8,128)S(1)} %get-tuple-element.31), channel_id=1, source_target_pairs={{0,1},{1,0},{2,3},{3,2},{4,5},{5,4},{6,7},{7,6},{8,9},{9,8},{10,11... | collective-permute-start | bytes 331784 | tf_op jit(solution)/shard_map/ppermute | solution.py:956
  19.3 6.7 %collective-permute-start.7 = (f32[3,72,128]{2,1,0:T(8,128)S(1)}, f32[3,72,128]{2,1,0:T(8,128)S(1)}, u32[]{:S(2)}, u32[]{:S(2)}) collective-permute-start(f32[3,72,128]{2,1,0:T(8,128)S(1)} %get-tuple-element.32), channel_id=1, source_target_pairs={{0,0},{1,2},{2,1},{3,3},{4,4},{5,6},{6,5},{7,7},{8,8},{9,10},{10,9... | collective-permute-start | bytes 331784 | tf_op jit(solution)/shard_map/ppermute | solution.py:956
  20.7 17.9 %collective-permute-start.4 = (f32[14,72,128]{2,1,0:T(8,128)S(1)}, f32[14,72,128]{2,1,0:T(8,128)S(1)}, u32[]{:S(2)}, u32[]{:S(2)}) collective-permute-start(f32[14,72,128]{2,1,0:T(8,128)S(1)} %get-tuple-element.28), channel_id=1, source_target_pairs={{0,1},{1,0},{2,3},{3,2},{4,5},{5,4},{6,7},{7,6},{8,9},{9,8},{10,11... | collective-permute-start | bytes 1548296 | tf_op jit(solution)/shard_map/ppermute | solution.py:957
  25.1 13.4 %collective-permute-start.5 = (f32[14,72,128]{2,1,0:T(8,128)S(1)}, f32[14,72,128]{2,1,0:T(8,128)S(1)}, u32[]{:S(2)}, u32[]{:S(2)}) collective-permute-start(f32[14,72,128]{2,1,0:T(8,128)S(1)} %get-tuple-element.29), channel_id=1, source_target_pairs={{0,0},{1,2},{2,1},{3,3},{4,4},{5,6},{6,5},{7,7},{8,8},{9,10},{10,9... | collective-permute-start | bytes 1548296 | tf_op jit(solution)/shard_map/ppermute | solution.py:957
  34.1 8.9 %collective-permute-start.10 = (f32[40,128]{1,0:T(8,128)S(1)}, f32[40,128]{1,0:T(8,128)S(1)}, u32[]{:S(2)}, u32[]{:S(2)}) collective-permute-start(f32[40,128]{1,0:T(8,128)S(1)} %pad_maximum_fusion.4.payload), channel_id=1, source_target_pairs={{0,3},{1,2},{2,1},{3,0},{4,7},{5,6},{6,5},{7,4},{8,11},{9,10},{10,... | collective-permute-start | bytes 61448 | tf_op jit(solution)/shard_map/ppermute | solution.py:978
  35.3 7.7 %collective-permute-start.9 = (f32[40,128]{1,0:T(8,128)S(1)}, f32[40,128]{1,0:T(8,128)S(1)}, u32[]{:S(2)}, u32[]{:S(2)}) collective-permute-start(f32[40,128]{1,0:T(8,128)S(1)} %pad_maximum_fusion.4.payload), channel_id=1, source_target_pairs={{0,2},{1,3},{2,0},{3,1},{4,6},{5,7},{6,4},{7,5},{8,10},{9,11},{10,... | collective-permute-start | bytes 61448 | tf_op jit(solution)/shard_map/ppermute | solution.py:978
  37.8 5.2 %collective-permute-start.8 = (f32[40,128]{1,0:T(8,128)S(1)}, f32[40,128]{1,0:T(8,128)S(1)}, u32[]{:S(2)}, u32[]{:S(2)}) collective-permute-start(f32[40,128]{1,0:T(8,128)S(1)} %pad_maximum_fusion.4.payload), channel_id=1, source_target_pairs={{0,1},{1,0},{2,3},{3,2},{4,5},{5,4},{6,7},{7,6},{8,9},{9,8},{10,11... | collective-permute-start | bytes 61448 | tf_op jit(solution)/shard_map/ppermute | solution.py:978
  43.0 10.7 %collective-permute-start.13 = (f32[4,40,128]{2,1,0:T(8,128)S(1)}, f32[4,40,128]{2,1,0:T(8,128)S(1)}, u32[]{:S(2)}, u32[]{:S(2)}) collective-permute-start(f32[4,40,128]{2,1,0:T(8,128)S(1)} %pad_maximum_fusion.2.column), channel_id=1, source_target_pairs={{0,24},{4,28},{8,16},{12,20},{16,8},{20,12},{24,0},{28,4},{1,25},{... | collective-permute-start | bytes 245768 | tf_op jit(solution)/shard_map/ppermute | solution.py:985
  45.9 7.9 %collective-permute-start.12 = (f32[4,40,128]{2,1,0:T(8,128)S(1)}, f32[4,40,128]{2,1,0:T(8,128)S(1)}, u32[]{:S(2)}, u32[]{:S(2)}) collective-permute-start(f32[4,40,128]{2,1,0:T(8,128)S(1)} %pad_maximum_fusion.2.column), channel_id=1, source_target_pairs={{0,8},{4,12},{8,0},{12,4},{16,24},{20,28},{24,16},{28,20},{1,9},{5... | collective-permute-start | bytes 245768 | tf_op jit(solution)/shard_map/ppermute | solution.py:985
  45.9 7.9 %collective-permute-start.11 = (f32[4,40,128]{2,1,0:T(8,128)S(1)}, f32[4,40,128]{2,1,0:T(8,128)S(1)}, u32[]{:S(2)}, u32[]{:S(2)}) collective-permute-start(f32[4,40,128]{2,1,0:T(8,128)S(1)} %pad_maximum_fusion.2.column), channel_id=1, source_target_pairs={{0,16},{4,20},{8,24},{12,28},{16,0},{20,4},{24,8},{28,12},{1,17},{... | collective-permute-start | bytes 245768 | tf_op jit(solution)/shard_map/ppermute | solution.py:985
  53.8 2.6 %collective-permute-start.14 = (f32[4,4,40,128]{3,2,1,0:T(8,128)S(1)}, f32[4,4,40,128]{3,2,1,0:T(8,128)S(1)}, u32[]{:S(2)}, u32[]{:S(2)}) collective-permute-start(f32[4,4,40,128]{3,2,1,0:T(8,128)S(1)} %pad_maximum_fusion.here), channel_id=1, source_target_pairs={{0,4},{4,0},{8,12},{12,8},{1,5},{5,1},{9,13},{13,9},{2,6},{6,2},{1... | collective-permute-start | bytes 983048 | tf_op jit(solution)/shard_map/ppermute | solution.py:988
  94.1 5.6 %collective-permute-start.17 = (f32[32,128]{1,0:T(8,128)S(1)}, f32[32,128]{1,0:T(8,128)S(1)}, u32[]{:S(2)}, u32[]{:S(2)}) collective-permute-start(f32[32,128]{1,0:T(8,128)S(1)} %get-tuple-element.47), channel_id=1, source_target_pairs={{0,3},{1,2},{2,1},{3,0},{4,7},{5,6},{6,5},{7,4},{8,11},{9,10},{10,... | collective-permute-start | bytes 49160 | tf_op jit(solution)/shard_map/ppermute | solution.py:978
  96.3 4.8 %collective-permute-start.16 = (f32[32,128]{1,0:T(8,128)S(1)}, f32[32,128]{1,0:T(8,128)S(1)}, u32[]{:S(2)}, u32[]{:S(2)}) collective-permute-start(f32[32,128]{1,0:T(8,128)S(1)} %get-tuple-element.47), channel_id=1, source_target_pairs={{0,2},{1,3},{2,0},{3,1},{4,6},{5,7},{6,4},{7,5},{8,10},{9,11},{10,... | collective-permute-start | bytes 49160 | tf_op jit(solution)/shard_map/ppermute | solution.py:978
  98.7 3.7 %collective-permute-start.15 = (f32[32,128]{1,0:T(8,128)S(1)}, f32[32,128]{1,0:T(8,128)S(1)}, u32[]{:S(2)}, u32[]{:S(2)}) collective-permute-start(f32[32,128]{1,0:T(8,128)S(1)} %get-tuple-element.47), channel_id=1, source_target_pairs={{0,1},{1,0},{2,3},{3,2},{4,5},{5,4},{6,7},{7,6},{8,9},{9,8},{10,11... | collective-permute-start | bytes 49160 | tf_op jit(solution)/shard_map/ppermute | solution.py:978
  102.4 4.6 %collective-permute-start.19 = (f32[4,32,128]{2,1,0:T(8,128)S(1)}, f32[4,32,128]{2,1,0:T(8,128)S(1)}, u32[]{:S(2)}, u32[]{:S(2)}) collective-permute-start(f32[4,32,128]{2,1,0:T(8,128)S(1)} %get-tuple-element.52), channel_id=1, source_target_pairs={{0,8},{4,12},{8,0},{12,4},{16,24},{20,28},{24,16},{28,20},{1,9},{5... | collective-permute-start | bytes 196616 | tf_op jit(solution)/shard_map/ppermute | solution.py:985
  103.1 4.4 %collective-permute-start.18 = (f32[4,32,128]{2,1,0:T(8,128)S(1)}, f32[4,32,128]{2,1,0:T(8,128)S(1)}, u32[]{:S(2)}, u32[]{:S(2)}) collective-permute-start(f32[4,32,128]{2,1,0:T(8,128)S(1)} %get-tuple-element.52), channel_id=1, source_target_pairs={{0,16},{4,20},{8,24},{12,28},{16,0},{20,4},{24,8},{28,12},{1,17},{... | collective-permute-start | bytes 196616 | tf_op jit(solution)/shard_map/ppermute | solution.py:985
  103.9 5.2 %collective-permute-start.20 = (f32[4,32,128]{2,1,0:T(8,128)S(1)}, f32[4,32,128]{2,1,0:T(8,128)S(1)}, u32[]{:S(2)}, u32[]{:S(2)}) collective-permute-start(f32[4,32,128]{2,1,0:T(8,128)S(1)} %get-tuple-element.52), channel_id=1, source_target_pairs={{0,24},{4,28},{8,16},{12,20},{16,8},{20,12},{24,0},{28,4},{1,25},{... | collective-permute-start | bytes 196616 | tf_op jit(solution)/shard_map/ppermute | solution.py:985
  109.0 1.6 %collective-permute-start.21 = (f32[4,4,32,128]{3,2,1,0:T(8,128)S(1)}, f32[4,4,32,128]{3,2,1,0:T(8,128)S(1)}, u32[]{:S(2)}, u32[]{:S(2)}) collective-permute-start(f32[4,4,32,128]{3,2,1,0:T(8,128)S(1)} %pad_maximum_fusion.1.here), channel_id=1, source_target_pairs={{0,4},{4,0},{8,12},{12,8},{1,5},{5,1},{9,13},{13,9},{2,6},{6,2},{1... | collective-permute-start | bytes 786440 | tf_op jit(solution)/shard_map/ppermute | solution.py:988
